TPU v7x, 128 devices: a whole 4x4x4 slice. The times are simulated.
128 devices in a mesh: wide: 32 (over y, z, core), narrow: 4 (over x).
Axes of the slice: x: 4, y: 4, z: 4, core: 2. Of those that a mesh axis runs over, the one named last changes fastest.
Arguments:
- coefficients: float32 [16, 256, 32, 128], P('narrow', 'wide'), may hold values from -6 to 6
- observed: float32 [16, 256, 32, 128], P('narrow', 'wide'), may hold values from -6 to 6
- blocks: bfloat16 [4, 32, 128, 128, 128], P('narrow', 'wide'), may hold values from -0.3125 to 0.3125
- block_rows: int32 [4, 32, 128], P('narrow', 'wide'), may hold values from 0 to 31
- block_cols: int32 [4, 32, 128], P('narrow', 'wide'), may hold values from 0 to 59, as said below
- live_count: int32 [4, 32], P('narrow', 'wide'), may hold values from 1 to 128, as said below
Outputs:
- updated: float32 [16, 256, 32, 128], P('narrow', 'wide')
- residual: float32 [16, 256, 32, 128], P('narrow', 'wide')
Inputs may be any that keep to these rules, and one draw needn't show every extreme that they name: block_cols of a slot lies in the 3 x 3 neighbourhood of its block_rows position: with r = block_rows, c // 10 - r // 8 and c % 10 - r % 8 are each 0, 1 or 2. `live_count`: at least one tile uses all 128 slots.
All inputs are finite; a program needn't handle non-finite values.
Results may differ from a plain program's by a relative error of at most 0.0065.
Values may be sent and summed in bfloat16 or wider, within the bound.
No kernel may reach another device: no remote copies, remote signals or barrier semaphores. Data moves between devices by JAX's collectives and lax.ppermute only.
A program may use at most 64 MiB of HBM per device.

v0:
```python
import functools

import jax
import jax.numpy as jnp
from jax import lax
from jax.experimental import pallas as pl
from jax.experimental.pallas import tpu as pltpu
from jax.sharding import PartitionSpec as P

ITERS = 5
descent = 0.1
NN = (((1,), (0,)), ((), ()))
NT = (((1,), (1,)), ((), ()))

ROW_FIRST, ROW_LAST, COL_FIRST, COL_LAST, EVEN = range(5)


def cast_low(value):
    return value.astype(jnp.bfloat16)


def wide_value(value):
    return value.astype(jnp.float32)


def kept(value, drop):
    return jnp.where(drop, jnp.zeros_like(value), value)


def half_step(source_ref, blocks_ref, total_ref, source_ids, target_ids, slots, dims):
    for slot in range(slots):
        product = lax.dot_general(
            source_ref[source_ids[slot]],
            blocks_ref[slot],
            dims,
            preferred_element_type=jnp.float32,
        )
        target = target_ids[slot]
        total_ref[target] = total_ref[target] + product


def products(sizes, info_ref, rows_ref, cols_ref, observed_ref, blocks_ref, next_ref, grad_ref, residual_ref, low_ref, rlow_ref):
    tile_x, tile_y, slots = sizes
    own = tile_x * tile_y
    extended = (tile_x + 2) * (tile_y + 2)
    low_ref[extended] = jnp.zeros_like(low_ref[extended])
    for block in range(own):
        residual_ref[block] = -observed_ref[block]
    residual_ref[own] = jnp.zeros_like(residual_ref[own])
    half_step(low_ref, blocks_ref, residual_ref, cols_ref, rows_ref, slots, NN)
    for block in range(own + 1):
        rlow_ref[block] = cast_low(residual_ref[block])
    for block in range(extended + 1):
        grad_ref[block] = jnp.zeros_like(grad_ref[block])
    half_step(rlow_ref, blocks_ref, grad_ref, rows_ref, cols_ref, slots, NT)


def send_columns(sizes, last, info_ref, grad_ref, pair_ref, next_ref):
    tile_x, tile_y, _ = sizes
    span = tile_y + 2
    even = info_ref[EVEN] == 1
    for out_ref, right in ((pair_ref, even), (next_ref, jnp.logical_not(even))):
        if last:
            col = jnp.where(right, span - 1, 0)
            for row in range(tile_x + 2):
                out_ref[row] = cast_low(grad_ref[row * span + col])
        else:
            col = jnp.where(right, span - 2, 0)
            for row in range(tile_x + 2):
                for step in range(2):
                    out_ref[row * 2 + step] = cast_low(grad_ref[row * span + col + step])


def outside(sizes, info_ref, row, col):
    tile_x, tile_y, _ = sizes
    flag = None
    for hit, place in (
        (row == 0, ROW_FIRST),
        (row == tile_x + 1, ROW_LAST),
        (col == 0, COL_FIRST),
        (col == tile_y + 1, COL_LAST),
    ):
        if hit:
            here = info_ref[place] == 1
            flag = here if flag is None else jnp.logical_or(flag, here)
    return flag


def first_kernel(sizes, last, info_ref, rows_ref, cols_ref, coef_ref, above_ref, below_ref, pair_in, next_in, observed_ref, blocks_ref, x_ref, grad_ref, residual_ref, pair_ref, next_ref, low_ref, rlow_ref):
    tile_x, tile_y, _ = sizes
    span = tile_y + 2
    even = info_ref[EVEN] == 1
    for row in range(tile_x + 2):
        for col in range(span):
            if col == 0:
                value = jnp.where(even, wide_value(next_in[row]), wide_value(pair_in[row]))
            elif col == tile_y + 1:
                value = jnp.where(even, wide_value(pair_in[row]), wide_value(next_in[row]))
            elif row == 0:
                value = wide_value(above_ref[col - 1])
            elif row == tile_x + 1:
                value = wide_value(below_ref[col - 1])
            else:
                value = coef_ref[(row - 1) * tile_y + col - 1]
            drop = outside(sizes, info_ref, row, col)
            if drop is not None:
                value = kept(value, drop)
            x_ref[row * span + col] = value
            low_ref[row * span + col] = cast_low(value)
    products(sizes, info_ref, rows_ref, cols_ref, observed_ref, blocks_ref, None, grad_ref, residual_ref, low_ref, rlow_ref)
    send_columns(sizes, last, info_ref, grad_ref, pair_ref, next_ref)


def step_kernel(sizes, last, info_ref, rows_ref, cols_ref, x_in, grad_in, above_ref, below_ref, observed_ref, blocks_ref, x_ref, grad_ref, residual_ref, pair_ref, next_ref, low_ref, rlow_ref):
    tile_x, tile_y, _ = sizes
    span = tile_y + 2
    first = info_ref[ROW_FIRST] == 1
    final = info_ref[ROW_LAST] == 1
    for row in range(tile_x + 2):
        for col in range(span):
            at = row * span + col
            gradient = grad_in[at]
            if row < 2:
                gradient = gradient + kept(wide_value(above_ref[row * span + col]), first)
            elif row >= tile_x:
                gradient = gradient + kept(wide_value(below_ref[(row - tile_x) * span + col]), final)
            value = x_in[at] - descent * gradient
            drop = outside(sizes, info_ref, row, col)
            if drop is not None:
                value = kept(value, drop)
            x_ref[at] = value
            low_ref[at] = cast_low(value)
    products(sizes, info_ref, rows_ref, cols_ref, observed_ref, blocks_ref, None, grad_ref, residual_ref, low_ref, rlow_ref)
    send_columns(sizes, last, info_ref, grad_ref, pair_ref, next_ref)


def fold_kernel(sizes, last, info_ref, grad_in, pair_in, next_in, grad_ref, up_ref, down_ref):
    tile_x, tile_y, _ = sizes
    span = tile_y + 2
    even = info_ref[EVEN] == 1
    width = 1 if last else 2
    lefts = {1: 0} if last else {0: 0, 1: 1}
    rights = {tile_y: 0} if last else {tile_y: 0, tile_y + 1: 1}
    for row in range(tile_x + 2):
        for col in range(span):
            at = row * span + col
            value = grad_in[at]
            for places, from_pair, place in (
                (lefts, jnp.logical_not(even), COL_FIRST),
                (rights, even, COL_LAST),
            ):
                if col in places:
                    where = row * width + places[col]
                    came = jnp.where(from_pair, wide_value(pair_in[where]), wide_value(next_in[where]))
                    value = value + kept(came, info_ref[place] == 1)
            grad_ref[at] = value
            if last:
                if 1 <= col <= tile_y:
                    if row == 0:
                        up_ref[col - 1] = cast_low(value)
                    if row == tile_x + 1:
                        down_ref[col - 1] = cast_low(value)
            else:
                if row < 2:
                    up_ref[row * span + col] = cast_low(value)
                if row >= tile_x:
                    down_ref[(row - tile_x) * span + col] = cast_low(value)


def final_kernel(sizes, info_ref, x_in, grad_in, above_ref, below_ref, out_ref):
    tile_x, tile_y, _ = sizes
    span = tile_y + 2
    first = info_ref[ROW_FIRST] == 1
    final = info_ref[ROW_LAST] == 1
    for row in range(1, tile_x + 1):
        for col in range(1, tile_y + 1):
            at = row * span + col
            gradient = grad_in[at]
            if row == 1:
                gradient = gradient + kept(wide_value(above_ref[col - 1]), first)
            if row == tile_x:
                gradient = gradient + kept(wide_value(below_ref[col - 1]), final)
            out_ref[(row - 1) * tile_y + col - 1] = x_in[at] - descent * gradient


def local(coefficients, observed, blocks, block_rows, block_cols, live_count):
    tile_x, tile_y, frames, width = coefficients.shape
    slots = blocks.shape[2]
    own = tile_x * tile_y
    span = tile_y + 2
    extended = (tile_x + 2) * span
    sizes = (tile_x, tile_y, slots)
    narrow = lax.axis_size("narrow")
    wide = lax.axis_size("wide")
    a = lax.axis_index("narrow")
    b = lax.axis_index("wide")
    info = jnp.stack([a == 0, a == narrow - 1, b == 0, b == wide - 1, b % 2 == 0]).astype(jnp.int32)
    even = b % 2 == 0

    up_ring = [(i, (i - 1) % narrow) for i in range(narrow)]
    down_ring = [(i, (i + 1) % narrow) for i in range(narrow)]
    pairs = [(i, i ^ 1) for i in range(wide)]
    others = [(i, ((i - 1) ^ 1) + 1) for i in range(1, wide - 1)] + [(0, wide - 1), (wide - 1, 0)]

    def along_narrow(up, down):
        return lax.ppermute(down, "narrow", down_ring), lax.ppermute(up, "narrow", up_ring)

    def along_wide(pair, other):
        return lax.ppermute(pair, "wide", pairs), lax.ppermute(other, "wide", others)

    matrices = blocks.reshape(slots, width, width)
    live = jnp.arange(slots, dtype=jnp.int32) < live_count.reshape(())
    row_ids = jnp.where(live, block_rows.reshape(slots), own)
    col_ids = jnp.where(live, block_cols.reshape(slots), extended)
    seen = observed.reshape(own, frames, width)

    smem = pl.BlockSpec(memory_space=pltpu.SMEM)
    vmem = pl.BlockSpec(memory_space=pltpu.VMEM)

    def shape(count, kind):
        return jax.ShapeDtypeStruct((count, frames, width), kind)

    params = pltpu.CompilerParams(vmem_limit_bytes=24 << 20)
    scratch = [
        pltpu.VMEM((extended + 1, frames, width), jnp.bfloat16),
        pltpu.VMEM((own + 1, frames, width), jnp.bfloat16),
    ]

    def step_call(kernel, last, inputs, name):
        sent = tile_x + 2 if last else 2 * (tile_x + 2)
        return pl.pallas_call(
            functools.partial(kernel, sizes, last),
            out_shape=[
                shape(extended, jnp.float32),
                shape(extended + 1, jnp.float32),
                shape(own + 1, jnp.float32),
                shape(sent, jnp.bfloat16),
                shape(sent, jnp.bfloat16),
            ],
            in_specs=[smem] * 3 + [vmem] * (len(inputs) - 3),
            out_specs=[vmem] * 5,
            scratch_shapes=scratch,
            compiler_params=params,
            name=name,
        )(*inputs)

    start = cast_low(coefficients)
    above, below = along_narrow(start[0], start[tile_x - 1])
    sides = []
    for col in (0, tile_y - 1):
        sides.append(
            jnp.concatenate([above[col : col + 1], start[:, col], below[col : col + 1]], axis=0)
        )
    pair_in, next_in = along_wide(
        jnp.where(even, sides[1], sides[0]), jnp.where(even, sides[0], sides[1])
    )
    x, grad, residual, pair_out, next_out = step_call(
        first_kernel,
        False,
        [info, row_ids, col_ids, coefficients.reshape(own, frames, width), above, below, pair_in, next_in, seen, matrices],
        "first_step",
    )
    for iteration in range(ITERS):
        last = iteration == ITERS - 1
        pair_in, next_in = along_wide(pair_out, next_out)
        rows_sent = tile_y if last else 2 * span
        grad, up, down = pl.pallas_call(
            functools.partial(fold_kernel, sizes, last),
            out_shape=[
                shape(extended, jnp.float32),
                shape(rows_sent, jnp.bfloat16),
                shape(rows_sent, jnp.bfloat16),
            ],
            in_specs=[smem] + [vmem] * 3,
            out_specs=[vmem] * 3,
            compiler_params=params,
            name="fold_columns",
        )(info, grad, pair_in, next_in)
        above, below = along_narrow(up, down)
        if last:
            updated = pl.pallas_call(
                functools.partial(final_kernel, sizes),
                out_shape=shape(own, jnp.float32),
                in_specs=[smem] + [vmem] * 4,
                out_specs=vmem,
                compiler_params=params,
                name="final_update",
            )(info, x, grad, above, below)
        else:
            x, grad, residual, pair_out, next_out = step_call(
                step_kernel,
                iteration == ITERS - 2,
                [info, row_ids, col_ids, x, grad, above, below, seen, matrices],
                "one_step",
            )
    return (
        updated.reshape(coefficients.shape),
        residual[:own].reshape(coefficients.shape),
    )


def solution(mesh):
    placed = (
        P("narrow", "wide", None, None),
        P("narrow", "wide", None, None),
        P("narrow", "wide", None, None, None),
        P("narrow", "wide", None),
        P("narrow", "wide", None),
        P("narrow", "wide"),
    )
    return jax.shard_map(
        local,
        mesh=mesh,
        in_specs=placed,
        out_specs=(P("narrow", "wide", None, None), P("narrow", "wide", None, None)),
        check_vma=False,
    )
```

profile of v0, /device:TPU:6, one launch (start us, length us, event | category | flops | bytes accessed | tf_op | source)
XLA Modules:
  0.0 120.5 jit_solution(14628150492159938810)
XLA Ops:
  0.6 1.1 convert_element_type.7
  1.8 0.9 collective-permute-start.1
  2.7 2.4 %collective-permute-start = (bf16[8,32,128]{2,1,0:T(8,128)(2,1)S(1)}, bf16[8,32,128]{2,1,0:T(8,128)(2,1)S(1)}, u32[]{:S(2)}, u32[]{:S(2)}) collective-permute-start(bf16[8,32,128]{2,1,0:T(8,128)(2,1)S(1)} %get-tuple-element.77), channel_id=1, source_target_pairs={{0,1},{1,2},{2,3},{3,0},{4,5},{5,6},{6,7},{7,4},{8,9},{9,10},{10,1... | collective-permute-start | bytes 196616 | tf_op jit(solution)/shard_map/ppermute | solution.py:206
  5.8 1.6 %collective-permute-done.1.below_ref = bf16[8,32,128]{2,1,0:T(8,128)(2,1)S(1)} collective-permute-done((bf16[8,32,128]{2,1,0:T(8,128)(2,1)S(1)}, bf16[8,32,128]{2,1,0:T(8,128)(2,1)S(1)}, u32[]{:S(2)}, u32[]{:S(2)}) %collective-permute-start.1) | collective-permute-done | bytes 65568 | tf_op jit(solution)/shard_map/ppermute | solution.py:206
  7.4 4.9 %collective-permute-start.3 = (bf16[6,32,128]{2,1,0:T(8,128)(2,1)S(1)}, bf16[6,32,128]{2,1,0:T(8,128)(2,1)S(1)}, u32[]{:S(2)}, u32[]{:S(2)}) collective-permute-start(bf16[6,32,128]{2,1,0:T(8,128)(2,1)S(1)} %get-tuple-element.78), channel_id=1, source_target_pairs={{4,8},{8,4},{12,16},{16,12},{20,24},{24,20},{28,32},{32,28},{36,40... | collective-permute-start | bytes 147464 | tf_op jit(solution)/shard_map/ppermute | solution.py:209
  12.2 0.7 compare_select_fusion
  13.0 1.3 %collective-permute-done.3.next_in = bf16[6,32,128]{2,1,0:T(8,128)(2,1)S(1)} collective-permute-done((bf16[6,32,128]{2,1,0:T(8,128)(2,1)S(1)}, bf16[6,32,128]{2,1,0:T(8,128)(2,1)S(1)}, u32[]{:S(2)}, u32[]{:S(2)}) %collective-permute-start.3) | collective-permute-done | bytes 49184 | tf_op jit(solution)/shard_map/ppermute | solution.py:209
  14.3 2.2 %copy-done = bf16[1,1,128,128,128]{4,3,2,1,0:T(8,128)(2,1)S(1)} copy-done((bf16[1,1,128,128,128]{4,3,2,1,0:T(8,128)(2,1)S(1)}, bf16[1,1,128,128,128]{4,3,2,1,0:T(8,128)(2,1)}, u32[]{:S(2)}) %copy-start) | copy-done | bytes 4194328
  16.5 1.0 copy-done.2
  17.5 1.0 copy-done.4
  18.6 5.0 %first_step.1 = (f32[60,32,128]{2,1,0:T(8,128)S(1)}, f32[61,32,128]{2,1,0:T(8,128)S(1)}, f32[33,32,128]{2,1,0:T(8,128)}, bf16[12,32,128]{2,1,0:T(8,128)(2,1)S(1)}, bf16[12,32,128]{2,1,0:T(8,128)(2,1)S(1)}) custom-call(s32[5]{0:T(128)S(1)} %convert_element_type.6.info_ref, s32[128]{0:T(128)S(1)} %get-tuple-element.85.rows_ref, ...), custom_call_target="tpu_custom_call" | custom-call | tf_op jit(solution)/shard_map/first_step/pallas_call | solution.py:231
  23.6 4.7 %collective-permute-start.5 = (bf16[12,32,128]{2,1,0:T(8,128)(2,1)S(1)}, bf16[12,32,128]{2,1,0:T(8,128)(2,1)S(1)}, u32[]{:S(2)}, u32[]{:S(2)}) collective-permute-start(bf16[12,32,128]{2,1,0:T(8,128)(2,1)S(1)} %get-tuple-element.41), channel_id=1, source_target_pairs={{4,8},{8,4},{12,16},{16,12},{20,24},{24,20},{28,32},{32,28},{36,40... | collective-permute-start | bytes 294920 | tf_op jit(solution)/shard_map/ppermute | solution.py:209
  28.3 2.6 %collective-permute-done.5.next_in = bf16[12,32,128]{2,1,0:T(8,128)(2,1)S(1)} collective-permute-done((bf16[12,32,128]{2,1,0:T(8,128)(2,1)S(1)}, bf16[12,32,128]{2,1,0:T(8,128)(2,1)S(1)}, u32[]{:S(2)}, u32[]{:S(2)}) %collective-permute-start.5) | collective-permute-done | bytes 98336 | tf_op jit(solution)/shard_map/ppermute | solution.py:209
  30.9 0.6 fold_columns.5
  31.6 3.3 %collective-permute-start.6 = (bf16[20,32,128]{2,1,0:T(8,128)(2,1)S(1)}, bf16[20,32,128]{2,1,0:T(8,128)(2,1)S(1)}, u32[]{:S(2)}, u32[]{:S(2)}) collective-permute-start(bf16[20,32,128]{2,1,0:T(8,128)(2,1)S(1)} %get-tuple-element.43), channel_id=1, source_target_pairs={{0,1},{1,2},{2,3},{3,0},{4,5},{5,6},{6,7},{7,4},{8,9},{9,10},{10,1... | collective-permute-start | bytes 491528 | tf_op jit(solution)/shard_map/ppermute | solution.py:206
  34.9 2.8 %collective-permute-done.6.above_ref = bf16[20,32,128]{2,1,0:T(8,128)(2,1)S(1)} collective-permute-done((bf16[20,32,128]{2,1,0:T(8,128)(2,1)S(1)}, bf16[20,32,128]{2,1,0:T(8,128)(2,1)S(1)}, u32[]{:S(2)}, u32[]{:S(2)}) %collective-permute-start.6) | collective-permute-done | bytes 163872 | tf_op jit(solution)/shard_map/ppermute | solution.py:206
  37.7 3.7 %collective-permute-done.7.below_ref = bf16[20,32,128]{2,1,0:T(8,128)(2,1)S(1)} collective-permute-done((bf16[20,32,128]{2,1,0:T(8,128)(2,1)S(1)}, bf16[20,32,128]{2,1,0:T(8,128)(2,1)S(1)}, u32[]{:S(2)}, u32[]{:S(2)}) %collective-permute-start.7) | collective-permute-done | bytes 163872 | tf_op jit(solution)/shard_map/ppermute | solution.py:206
  41.4 5.1 %one_step.4 = (f32[60,32,128]{2,1,0:T(8,128)S(1)}, f32[61,32,128]{2,1,0:T(8,128)S(1)}, f32[33,32,128]{2,1,0:T(8,128)}, bf16[12,32,128]{2,1,0:T(8,128)(2,1)S(1)}, bf16[12,32,128]{2,1,0:T(8,128)(2,1)S(1)}) custom-call(s32[5]{0:T(128)S(1)} %convert_element_type.6.info_ref, s32[128]{0:T(128)S(1)} %get-tuple-element.85.rows_ref, ...), custom_call_target="tpu_custom_call" | custom-call | tf_op jit(solution)/shard_map/one_step/pallas_call | solution.py:231
  46.5 2.9 %collective-permute-start.9 = (bf16[12,32,128]{2,1,0:T(8,128)(2,1)S(1)}, bf16[12,32,128]{2,1,0:T(8,128)(2,1)S(1)}, u32[]{:S(2)}, u32[]{:S(2)}) collective-permute-start(bf16[12,32,128]{2,1,0:T(8,128)(2,1)S(1)} %get-tuple-element.48), channel_id=1, source_target_pairs={{4,8},{8,4},{12,16},{16,12},{20,24},{24,20},{28,32},{32,28},{36,40... | collective-permute-start | bytes 294920 | tf_op jit(solution)/shard_map/ppermute | solution.py:209
  49.4 4.5 %collective-permute-done.9.next_in = bf16[12,32,128]{2,1,0:T(8,128)(2,1)S(1)} collective-permute-done((bf16[12,32,128]{2,1,0:T(8,128)(2,1)S(1)}, bf16[12,32,128]{2,1,0:T(8,128)(2,1)S(1)}, u32[]{:S(2)}, u32[]{:S(2)}) %collective-permute-start.9) | collective-permute-done | bytes 98336 | tf_op jit(solution)/shard_map/ppermute | solution.py:209
  53.9 0.6 fold_columns.6
  54.6 2.0 %collective-permute-start.11 = (bf16[20,32,128]{2,1,0:T(8,128)(2,1)S(1)}, bf16[20,32,128]{2,1,0:T(8,128)(2,1)S(1)}, u32[]{:S(2)}, u32[]{:S(2)}) collective-permute-start(bf16[20,32,128]{2,1,0:T(8,128)(2,1)S(1)} %get-tuple-element.51), channel_id=1, source_target_pairs={{0,3},{1,0},{2,1},{3,2},{4,7},{5,4},{6,5},{7,6},{8,11},{9,8},{10,9... | collective-permute-start | bytes 491528 | tf_op jit(solution)/shard_map/ppermute | solution.py:206
  56.6 3.3 %collective-permute-done.10.above_ref = bf16[20,32,128]{2,1,0:T(8,128)(2,1)S(1)} collective-permute-done((bf16[20,32,128]{2,1,0:T(8,128)(2,1)S(1)}, bf16[20,32,128]{2,1,0:T(8,128)(2,1)S(1)}, u32[]{:S(2)}, u32[]{:S(2)}) %collective-permute-start.10) | collective-permute-done | bytes 163872 | tf_op jit(solution)/shard_map/ppermute | solution.py:206
  59.9 1.5 %collective-permute-done.11.below_ref = bf16[20,32,128]{2,1,0:T(8,128)(2,1)S(1)} collective-permute-done((bf16[20,32,128]{2,1,0:T(8,128)(2,1)S(1)}, bf16[20,32,128]{2,1,0:T(8,128)(2,1)S(1)}, u32[]{:S(2)}, u32[]{:S(2)}) %collective-permute-start.11) | collective-permute-done | bytes 163872 | tf_op jit(solution)/shard_map/ppermute | solution.py:206
  61.4 5.1 %one_step.5 = (f32[60,32,128]{2,1,0:T(8,128)S(1)}, f32[61,32,128]{2,1,0:T(8,128)S(1)}, f32[33,32,128]{2,1,0:T(8,128)}, bf16[12,32,128]{2,1,0:T(8,128)(2,1)S(1)}, bf16[12,32,128]{2,1,0:T(8,128)(2,1)S(1)}) custom-call(s32[5]{0:T(128)S(1)} %convert_element_type.6.info_ref, s32[128]{0:T(128)S(1)} %get-tuple-element.85.rows_ref, ...), custom_call_target="tpu_custom_call" | custom-call | tf_op jit(solution)/shard_map/one_step/pallas_call | solution.py:231
  66.5 1.7 %collective-permute-start.13 = (bf16[12,32,128]{2,1,0:T(8,128)(2,1)S(1)}, bf16[12,32,128]{2,1,0:T(8,128)(2,1)S(1)}, u32[]{:S(2)}, u32[]{:S(2)}) collective-permute-start(bf16[12,32,128]{2,1,0:T(8,128)(2,1)S(1)} %get-tuple-element.55), channel_id=1, source_target_pairs={{4,8},{8,4},{12,16},{16,12},{20,24},{24,20},{28,32},{32,28},{36,40... | collective-permute-start | bytes 294920 | tf_op jit(solution)/shard_map/ppermute | solution.py:209
  68.1 5.7 %collective-permute-done.13.next_in = bf16[12,32,128]{2,1,0:T(8,128)(2,1)S(1)} collective-permute-done((bf16[12,32,128]{2,1,0:T(8,128)(2,1)S(1)}, bf16[12,32,128]{2,1,0:T(8,128)(2,1)S(1)}, u32[]{:S(2)}, u32[]{:S(2)}) %collective-permute-start.13) | collective-permute-done | bytes 98336 | tf_op jit(solution)/shard_map/ppermute | solution.py:209
  73.8 0.6 fold_columns.7
  74.5 2.0 %collective-permute-start.15 = (bf16[20,32,128]{2,1,0:T(8,128)(2,1)S(1)}, bf16[20,32,128]{2,1,0:T(8,128)(2,1)S(1)}, u32[]{:S(2)}, u32[]{:S(2)}) collective-permute-start(bf16[20,32,128]{2,1,0:T(8,128)(2,1)S(1)} %get-tuple-element.58), channel_id=1, source_target_pairs={{0,3},{1,0},{2,1},{3,2},{4,7},{5,4},{6,5},{7,6},{8,11},{9,8},{10,9... | collective-permute-start | bytes 491528 | tf_op jit(solution)/shard_map/ppermute | solution.py:206
  76.6 3.3 %collective-permute-done.14.above_ref = bf16[20,32,128]{2,1,0:T(8,128)(2,1)S(1)} collective-permute-done((bf16[20,32,128]{2,1,0:T(8,128)(2,1)S(1)}, bf16[20,32,128]{2,1,0:T(8,128)(2,1)S(1)}, u32[]{:S(2)}, u32[]{:S(2)}) %collective-permute-start.14) | collective-permute-done | bytes 163872 | tf_op jit(solution)/shard_map/ppermute | solution.py:206
  79.8 1.3 %collective-permute-done.15.below_ref = bf16[20,32,128]{2,1,0:T(8,128)(2,1)S(1)} collective-permute-done((bf16[20,32,128]{2,1,0:T(8,128)(2,1)S(1)}, bf16[20,32,128]{2,1,0:T(8,128)(2,1)S(1)}, u32[]{:S(2)}, u32[]{:S(2)}) %collective-permute-start.15) | collective-permute-done | bytes 163872 | tf_op jit(solution)/shard_map/ppermute | solution.py:206
  81.1 5.1 %one_step.6 = (f32[60,32,128]{2,1,0:T(8,128)S(1)}, f32[61,32,128]{2,1,0:T(8,128)S(1)}, f32[33,32,128]{2,1,0:T(8,128)}, bf16[12,32,128]{2,1,0:T(8,128)(2,1)S(1)}, bf16[12,32,128]{2,1,0:T(8,128)(2,1)S(1)}) custom-call(s32[5]{0:T(128)S(1)} %convert_element_type.6.info_ref, s32[128]{0:T(128)S(1)} %get-tuple-element.85.rows_ref, ...), custom_call_target="tpu_custom_call" | custom-call | tf_op jit(solution)/shard_map/one_step/pallas_call | solution.py:231
  86.7 0.8 collective-permute-done.16.pair_in
  87.5 6.1 %collective-permute-done.17.next_in = bf16[12,32,128]{2,1,0:T(8,128)(2,1)S(1)} collective-permute-done((bf16[12,32,128]{2,1,0:T(8,128)(2,1)S(1)}, bf16[12,32,128]{2,1,0:T(8,128)(2,1)S(1)}, u32[]{:S(2)}, u32[]{:S(2)}) %collective-permute-start.17) | collective-permute-done | bytes 98336 | tf_op jit(solution)/shard_map/ppermute | solution.py:209
  93.6 0.6 fold_columns.8
  94.3 2.0 %collective-permute-start.19 = (bf16[20,32,128]{2,1,0:T(8,128)(2,1)S(1)}, bf16[20,32,128]{2,1,0:T(8,128)(2,1)S(1)}, u32[]{:S(2)}, u32[]{:S(2)}) collective-permute-start(bf16[20,32,128]{2,1,0:T(8,128)(2,1)S(1)} %get-tuple-element.65), channel_id=1, source_target_pairs={{0,3},{1,0},{2,1},{3,2},{4,7},{5,4},{6,5},{7,6},{8,11},{9,8},{10,9... | collective-permute-start | bytes 491528 | tf_op jit(solution)/shard_map/ppermute | solution.py:206
  96.3 3.3 %collective-permute-done.18.above_ref = bf16[20,32,128]{2,1,0:T(8,128)(2,1)S(1)} collective-permute-done((bf16[20,32,128]{2,1,0:T(8,128)(2,1)S(1)}, bf16[20,32,128]{2,1,0:T(8,128)(2,1)S(1)}, u32[]{:S(2)}, u32[]{:S(2)}) %collective-permute-start.18) | collective-permute-done | bytes 163872 | tf_op jit(solution)/shard_map/ppermute | solution.py:206
  99.6 1.3 %collective-permute-done.19.below_ref = bf16[20,32,128]{2,1,0:T(8,128)(2,1)S(1)} collective-permute-done((bf16[20,32,128]{2,1,0:T(8,128)(2,1)S(1)}, bf16[20,32,128]{2,1,0:T(8,128)(2,1)S(1)}, u32[]{:S(2)}, u32[]{:S(2)}) %collective-permute-start.19) | collective-permute-done | bytes 163872 | tf_op jit(solution)/shard_map/ppermute | solution.py:206
  100.9 4.5 %one_step.7 = (f32[60,32,128]{2,1,0:T(8,128)S(1)}, f32[61,32,128]{2,1,0:T(8,128)S(1)}, f32[33,32,128]{2,1,0:T(8,128)S(1)}, bf16[6,32,128]{2,1,0:T(8,128)(2,1)S(1)}, bf16[6,32,128]{2,1,0:T(8,128)(2,1)S(1)}) custom-call(s32[5]{0:T(128)S(1)} %convert_element_type.6.info_ref, s32[128]{0:T(128)S(1)} %get-tuple-element.85.rows_ref, ...), custom_call_target="tpu_custom_call" | custom-call | tf_op jit(solution)/shard_map/one_step/pallas_call | solution.py:231
  105.6 1.1 collective-permute-done.20.pair_in
  106.7 5.7 %collective-permute-done.21.next_in = bf16[6,32,128]{2,1,0:T(8,128)(2,1)S(1)} collective-permute-done((bf16[6,32,128]{2,1,0:T(8,128)(2,1)S(1)}, bf16[6,32,128]{2,1,0:T(8,128)(2,1)S(1)}, u32[]{:S(2)}, u32[]{:S(2)}) %collective-permute-start.21) | collective-permute-done | bytes 49184 | tf_op jit(solution)/shard_map/ppermute | solution.py:209
  112.4 0.6 fold_columns.9
  113.0 0.5 collective-permute-start.22
  113.6 1.6 %collective-permute-start.23 = (bf16[8,32,128]{2,1,0:T(8,128)(2,1)S(1)}, bf16[8,32,128]{2,1,0:T(8,128)(2,1)S(1)}, u32[]{:S(2)}, u32[]{:S(2)}) collective-permute-start(bf16[8,32,128]{2,1,0:T(8,128)(2,1)S(1)} %get-tuple-element.72), channel_id=1, source_target_pairs={{0,3},{1,0},{2,1},{3,2},{4,7},{5,4},{6,5},{7,6},{8,11},{9,8},{10,9... | collective-permute-start | bytes 196616 | tf_op jit(solution)/shard_map/ppermute | solution.py:206
  115.1 0.8 slice.35
  116.0 1.4 %collective-permute-done.22.above_ref = bf16[8,32,128]{2,1,0:T(8,128)(2,1)S(1)} collective-permute-done((bf16[8,32,128]{2,1,0:T(8,128)(2,1)S(1)}, bf16[8,32,128]{2,1,0:T(8,128)(2,1)S(1)}, u32[]{:S(2)}, u32[]{:S(2)}) %collective-permute-start.22) | collective-permute-done | bytes 65568 | tf_op jit(solution)/shard_map/ppermute | solution.py:206
  117.4 1.7 %collective-permute-done.23.below_ref = bf16[8,32,128]{2,1,0:T(8,128)(2,1)S(1)} collective-permute-done((bf16[8,32,128]{2,1,0:T(8,128)(2,1)S(1)}, bf16[8,32,128]{2,1,0:T(8,128)(2,1)S(1)}, u32[]{:S(2)}, u32[]{:S(2)}) %collective-permute-start.23) | collective-permute-done | bytes 65568 | tf_op jit(solution)/shard_map/ppermute | solution.py:206
  119.0 1.4 %final_update.1 = f32[32,32,128]{2,1,0:T(8,128)} custom-call(s32[5]{0:T(128)S(1)} %convert_element_type.6.info_ref, f32[60,32,128]{2,1,0:T(8,128)S(1)} %get-tuple-element.66.x_in, f32[60,32,128]{2,1,0:T(8,128)S(1)} %get-tuple-element.70.grad_in, bf16[8,32,128]{2,1,0:T(8,128)(2,1)S(1)} %collective-permute-done.22.above_ref, ...), custom_call_target="tpu_custom_call" | custom-call | tf_op jit(solution)/shard_map/final_update/pallas_call | solution.py:281
  (31 shorter events, 1.0 us)
Async XLA Ops:
  0.6 40.8 %copy-start.3 = (f32[4,8,32,128]{3,2,1,0:T(8,128)S(1)}, f32[4,8,32,128]{3,2,1,0:T(8,128)}, u32[]{:S(2)}) copy-start(f32[4,8,32,128]{3,2,1,0:T(8,128)} %param.7) | copy-start | bytes 1572868
  1.8 5.5 %collective-permute-start.1 = (bf16[8,32,128]{2,1,0:T(8,128)(2,1)S(1)}, bf16[8,32,128]{2,1,0:T(8,128)(2,1)S(1)}, u32[]{:S(2)}, u32[]{:S(2)}) collective-permute-start(bf16[8,32,128]{2,1,0:T(8,128)(2,1)S(1)} %get-tuple-element.76), channel_id=1, source_target_pairs={{0,3},{1,0},{2,1},{3,2},{4,7},{5,4},{6,5},{7,6},{8,11},{9,8},{10,9... | collective-permute-start | bytes 196616 | tf_op jit(solution)/shard_map/ppermute | solution.py:206
  2.7 4.7 %collective-permute-start = (bf16[8,32,128]{2,1,0:T(8,128)(2,1)S(1)}, bf16[8,32,128]{2,1,0:T(8,128)(2,1)S(1)}, u32[]{:S(2)}, u32[]{:S(2)}) collective-permute-start(bf16[8,32,128]{2,1,0:T(8,128)(2,1)S(1)} %get-tuple-element.77), channel_id=1, source_target_pairs={{0,1},{1,2},{2,3},{3,0},{4,5},{5,6},{6,7},{7,4},{8,9},{9,10},{10,1... | collective-permute-start | bytes 196616 | tf_op jit(solution)/shard_map/ppermute | solution.py:206
  7.4 6.9 %collective-permute-start.3 = (bf16[6,32,128]{2,1,0:T(8,128)(2,1)S(1)}, bf16[6,32,128]{2,1,0:T(8,128)(2,1)S(1)}, u32[]{:S(2)}, u32[]{:S(2)}) collective-permute-start(bf16[6,32,128]{2,1,0:T(8,128)(2,1)S(1)} %get-tuple-element.78), channel_id=1, source_target_pairs={{4,8},{8,4},{12,16},{16,12},{20,24},{24,20},{28,32},{32,28},{36,40... | collective-permute-start | bytes 147464 | tf_op jit(solution)/shard_map/ppermute | solution.py:209
  12.2 2.1 %collective-permute-start.2 = (bf16[6,32,128]{2,1,0:T(8,128)(2,1)S(1)}, bf16[6,32,128]{2,1,0:T(8,128)(2,1)S(1)}, u32[]{:S(2)}, u32[]{:S(2)}) collective-permute-start(bf16[6,32,128]{2,1,0:T(8,128)(2,1)S(1)} %get-tuple-element.79), channel_id=1, source_target_pairs={{0,4},{4,0},{8,12},{12,8},{16,20},{20,16},{24,28},{28,24},{32,36},... | collective-permute-start | bytes 147464 | tf_op jit(solution)/shard_map/ppermute | solution.py:209
  14.3 2.2 %copy-start = (bf16[1,1,128,128,128]{4,3,2,1,0:T(8,128)(2,1)S(1)}, bf16[1,1,128,128,128]{4,3,2,1,0:T(8,128)(2,1)}, u32[]{:S(2)}) copy-start(bf16[1,1,128,128,128]{4,3,2,1,0:T(8,128)(2,1)} %param.8) | copy-start | bytes 12582916
  16.5 1.0 copy-start.2
  17.5 1.0 copy-start.4
  18.6 22.8 %copy-start.1 = (bf16[1,1,128,128,128]{4,3,2,1,0:T(8,128)(2,1)S(1)}, bf16[1,1,128,128,128]{4,3,2,1,0:T(8,128)(2,1)}, u32[]{:S(2)}) copy-start(bf16[1,1,128,128,128]{4,3,2,1,0:T(8,128)(2,1)} %param.8) | copy-start | bytes 12582916
  23.6 4.7 %collective-permute-start.4 = (bf16[12,32,128]{2,1,0:T(8,128)(2,1)S(1)}, bf16[12,32,128]{2,1,0:T(8,128)(2,1)S(1)}, u32[]{:S(2)}, u32[]{:S(2)}) collective-permute-start(bf16[12,32,128]{2,1,0:T(8,128)(2,1)S(1)} %get-tuple-element.40), channel_id=1, source_target_pairs={{0,4},{4,0},{8,12},{12,8},{16,20},{20,16},{24,28},{28,24},{32,36},... | collective-permute-start | bytes 294920 | tf_op jit(solution)/shard_map/ppermute | solution.py:209
  23.6 7.4 %collective-permute-start.5 = (bf16[12,32,128]{2,1,0:T(8,128)(2,1)S(1)}, bf16[12,32,128]{2,1,0:T(8,128)(2,1)S(1)}, u32[]{:S(2)}, u32[]{:S(2)}) collective-permute-start(bf16[12,32,128]{2,1,0:T(8,128)(2,1)S(1)} %get-tuple-element.41), channel_id=1, source_target_pairs={{4,8},{8,4},{12,16},{16,12},{20,24},{24,20},{28,32},{32,28},{36,40... | collective-permute-start | bytes 294920 | tf_op jit(solution)/shard_map/ppermute | solution.py:209
  31.6 6.1 %collective-permute-start.6 = (bf16[20,32,128]{2,1,0:T(8,128)(2,1)S(1)}, bf16[20,32,128]{2,1,0:T(8,128)(2,1)S(1)}, u32[]{:S(2)}, u32[]{:S(2)}) collective-permute-start(bf16[20,32,128]{2,1,0:T(8,128)(2,1)S(1)} %get-tuple-element.43), channel_id=1, source_target_pairs={{0,1},{1,2},{2,3},{3,0},{4,5},{5,6},{6,7},{7,4},{8,9},{9,10},{10,1... | collective-permute-start | bytes 491528 | tf_op jit(solution)/shard_map/ppermute | solution.py:206
  34.8 6.5 %collective-permute-start.7 = (bf16[20,32,128]{2,1,0:T(8,128)(2,1)S(1)}, bf16[20,32,128]{2,1,0:T(8,128)(2,1)S(1)}, u32[]{:S(2)}, u32[]{:S(2)}) collective-permute-start(bf16[20,32,128]{2,1,0:T(8,128)(2,1)S(1)} %get-tuple-element.44), channel_id=1, source_target_pairs={{0,3},{1,0},{2,1},{3,2},{4,7},{5,4},{6,5},{7,6},{8,11},{9,8},{10,9... | collective-permute-start | bytes 491528 | tf_op jit(solution)/shard_map/ppermute | solution.py:206
  46.5 2.9 %collective-permute-start.8 = (bf16[12,32,128]{2,1,0:T(8,128)(2,1)S(1)}, bf16[12,32,128]{2,1,0:T(8,128)(2,1)S(1)}, u32[]{:S(2)}, u32[]{:S(2)}) collective-permute-start(bf16[12,32,128]{2,1,0:T(8,128)(2,1)S(1)} %get-tuple-element.47), channel_id=1, source_target_pairs={{0,4},{4,0},{8,12},{12,8},{16,20},{20,16},{24,28},{28,24},{32,36},... | collective-permute-start | bytes 294920 | tf_op jit(solution)/shard_map/ppermute | solution.py:209
  46.5 7.4 %collective-permute-start.9 = (bf16[12,32,128]{2,1,0:T(8,128)(2,1)S(1)}, bf16[12,32,128]{2,1,0:T(8,128)(2,1)S(1)}, u32[]{:S(2)}, u32[]{:S(2)}) collective-permute-start(bf16[12,32,128]{2,1,0:T(8,128)(2,1)S(1)} %get-tuple-element.48), channel_id=1, source_target_pairs={{4,8},{8,4},{12,16},{16,12},{20,24},{24,20},{28,32},{32,28},{36,40... | collective-permute-start | bytes 294920 | tf_op jit(solution)/shard_map/ppermute | solution.py:209
  54.5 5.4 %collective-permute-start.10 = (bf16[20,32,128]{2,1,0:T(8,128)(2,1)S(1)}, bf16[20,32,128]{2,1,0:T(8,128)(2,1)S(1)}, u32[]{:S(2)}, u32[]{:S(2)}) collective-permute-start(bf16[20,32,128]{2,1,0:T(8,128)(2,1)S(1)} %get-tuple-element.50), channel_id=1, source_target_pairs={{0,1},{1,2},{2,3},{3,0},{4,5},{5,6},{6,7},{7,4},{8,9},{9,10},{10,1... | collective-permute-start | bytes 491528 | tf_op jit(solution)/shard_map/ppermute | solution.py:206
  54.6 6.8 %collective-permute-start.11 = (bf16[20,32,128]{2,1,0:T(8,128)(2,1)S(1)}, bf16[20,32,128]{2,1,0:T(8,128)(2,1)S(1)}, u32[]{:S(2)}, u32[]{:S(2)}) collective-permute-start(bf16[20,32,128]{2,1,0:T(8,128)(2,1)S(1)} %get-tuple-element.51), channel_id=1, source_target_pairs={{0,3},{1,0},{2,1},{3,2},{4,7},{5,4},{6,5},{7,6},{8,11},{9,8},{10,9... | collective-permute-start | bytes 491528 | tf_op jit(solution)/shard_map/ppermute | solution.py:206
  66.5 1.7 %collective-permute-start.12 = (bf16[12,32,128]{2,1,0:T(8,128)(2,1)S(1)}, bf16[12,32,128]{2,1,0:T(8,128)(2,1)S(1)}, u32[]{:S(2)}, u32[]{:S(2)}) collective-permute-start(bf16[12,32,128]{2,1,0:T(8,128)(2,1)S(1)} %get-tuple-element.54), channel_id=1, source_target_pairs={{0,4},{4,0},{8,12},{12,8},{16,20},{20,16},{24,28},{28,24},{32,36},... | collective-permute-start | bytes 294920 | tf_op jit(solution)/shard_map/ppermute | solution.py:209
  66.5 7.4 %collective-permute-start.13 = (bf16[12,32,128]{2,1,0:T(8,128)(2,1)S(1)}, bf16[12,32,128]{2,1,0:T(8,128)(2,1)S(1)}, u32[]{:S(2)}, u32[]{:S(2)}) collective-permute-start(bf16[12,32,128]{2,1,0:T(8,128)(2,1)S(1)} %get-tuple-element.55), channel_id=1, source_target_pairs={{4,8},{8,4},{12,16},{16,12},{20,24},{24,20},{28,32},{32,28},{36,40... | collective-permute-start | bytes 294920 | tf_op jit(solution)/shard_map/ppermute | solution.py:209
  74.5 5.4 %collective-permute-start.14 = (bf16[20,32,128]{2,1,0:T(8,128)(2,1)S(1)}, bf16[20,32,128]{2,1,0:T(8,128)(2,1)S(1)}, u32[]{:S(2)}, u32[]{:S(2)}) collective-permute-start(bf16[20,32,128]{2,1,0:T(8,128)(2,1)S(1)} %get-tuple-element.57), channel_id=1, source_target_pairs={{0,1},{1,2},{2,3},{3,0},{4,5},{5,6},{6,7},{7,4},{8,9},{9,10},{10,1... | collective-permute-start | bytes 491528 | tf_op jit(solution)/shard_map/ppermute | solution.py:206
  74.5 6.6 %collective-permute-start.15 = (bf16[20,32,128]{2,1,0:T(8,128)(2,1)S(1)}, bf16[20,32,128]{2,1,0:T(8,128)(2,1)S(1)}, u32[]{:S(2)}, u32[]{:S(2)}) collective-permute-start(bf16[20,32,128]{2,1,0:T(8,128)(2,1)S(1)} %get-tuple-element.58), channel_id=1, source_target_pairs={{0,3},{1,0},{2,1},{3,2},{4,7},{5,4},{6,5},{7,6},{8,11},{9,8},{10,9... | collective-permute-start | bytes 491528 | tf_op jit(solution)/shard_map/ppermute | solution.py:206
  86.2 1.3 %collective-permute-start.16 = (bf16[12,32,128]{2,1,0:T(8,128)(2,1)S(1)}, bf16[12,32,128]{2,1,0:T(8,128)(2,1)S(1)}, u32[]{:S(2)}, u32[]{:S(2)}) collective-permute-start(bf16[12,32,128]{2,1,0:T(8,128)(2,1)S(1)} %get-tuple-element.61), channel_id=1, source_target_pairs={{0,4},{4,0},{8,12},{12,8},{16,20},{20,16},{24,28},{28,24},{32,36},... | collective-permute-start | bytes 294920 | tf_op jit(solution)/shard_map/ppermute | solution.py:209
  86.2 7.4 %collective-permute-start.17 = (bf16[12,32,128]{2,1,0:T(8,128)(2,1)S(1)}, bf16[12,32,128]{2,1,0:T(8,128)(2,1)S(1)}, u32[]{:S(2)}, u32[]{:S(2)}) collective-permute-start(bf16[12,32,128]{2,1,0:T(8,128)(2,1)S(1)} %get-tuple-element.62), channel_id=1, source_target_pairs={{4,8},{8,4},{12,16},{16,12},{20,24},{24,20},{28,32},{32,28},{36,40... | collective-permute-start | bytes 294920 | tf_op jit(solution)/shard_map/ppermute | solution.py:209
  94.2 5.4 %collective-permute-start.18 = (bf16[20,32,128]{2,1,0:T(8,128)(2,1)S(1)}, bf16[20,32,128]{2,1,0:T(8,128)(2,1)S(1)}, u32[]{:S(2)}, u32[]{:S(2)}) collective-permute-start(bf16[20,32,128]{2,1,0:T(8,128)(2,1)S(1)} %get-tuple-element.64), channel_id=1, source_target_pairs={{0,1},{1,2},{2,3},{3,0},{4,5},{5,6},{6,7},{7,4},{8,9},{9,10},{10,1... | collective-permute-start | bytes 491528 | tf_op jit(solution)/shard_map/ppermute | solution.py:206
  94.3 6.6 %collective-permute-start.19 = (bf16[20,32,128]{2,1,0:T(8,128)(2,1)S(1)}, bf16[20,32,128]{2,1,0:T(8,128)(2,1)S(1)}, u32[]{:S(2)}, u32[]{:S(2)}) collective-permute-start(bf16[20,32,128]{2,1,0:T(8,128)(2,1)S(1)} %get-tuple-element.65), channel_id=1, source_target_pairs={{0,3},{1,0},{2,1},{3,2},{4,7},{5,4},{6,5},{7,6},{8,11},{9,8},{10,9... | collective-permute-start | bytes 491528 | tf_op jit(solution)/shard_map/ppermute | solution.py:206
  105.4 1.3 %collective-permute-start.20 = (bf16[6,32,128]{2,1,0:T(8,128)(2,1)S(1)}, bf16[6,32,128]{2,1,0:T(8,128)(2,1)S(1)}, u32[]{:S(2)}, u32[]{:S(2)}) collective-permute-start(bf16[6,32,128]{2,1,0:T(8,128)(2,1)S(1)} %get-tuple-element.68), channel_id=1, source_target_pairs={{0,4},{4,0},{8,12},{12,8},{16,20},{20,16},{24,28},{28,24},{32,36},... | collective-permute-start | bytes 147464 | tf_op jit(solution)/shard_map/ppermute | solution.py:209
  105.5 6.9 %collective-permute-start.21 = (bf16[6,32,128]{2,1,0:T(8,128)(2,1)S(1)}, bf16[6,32,128]{2,1,0:T(8,128)(2,1)S(1)}, u32[]{:S(2)}, u32[]{:S(2)}) collective-permute-start(bf16[6,32,128]{2,1,0:T(8,128)(2,1)S(1)} %get-tuple-element.69), channel_id=1, source_target_pairs={{4,8},{8,4},{12,16},{16,12},{20,24},{24,20},{28,32},{32,28},{36,40... | collective-permute-start | bytes 147464 | tf_op jit(solution)/shard_map/ppermute | solution.py:209
  113.0 4.3 %collective-permute-start.22 = (bf16[8,32,128]{2,1,0:T(8,128)(2,1)S(1)}, bf16[8,32,128]{2,1,0:T(8,128)(2,1)S(1)}, u32[]{:S(2)}, u32[]{:S(2)}) collective-permute-start(bf16[8,32,128]{2,1,0:T(8,128)(2,1)S(1)} %get-tuple-element.71), channel_id=1, source_target_pairs={{0,1},{1,2},{2,3},{3,0},{4,5},{5,6},{6,7},{7,4},{8,9},{9,10},{10,1... | collective-permute-start | bytes 196616 | tf_op jit(solution)/shard_map/ppermute | solution.py:206
  113.6 5.5 %collective-permute-start.23 = (bf16[8,32,128]{2,1,0:T(8,128)(2,1)S(1)}, bf16[8,32,128]{2,1,0:T(8,128)(2,1)S(1)}, u32[]{:S(2)}, u32[]{:S(2)}) collective-permute-start(bf16[8,32,128]{2,1,0:T(8,128)(2,1)S(1)} %get-tuple-element.72), channel_id=1, source_target_pairs={{0,3},{1,0},{2,1},{3,2},{4,7},{5,4},{6,5},{7,6},{8,11},{9,8},{10,9... | collective-permute-start | bytes 196616 | tf_op jit(solution)/shard_map/ppermute | solution.py:206
where the time goes:
time: 121 us; the launch traced here: 120 us
  waiting for transfers between devices  52.9 us (44%)
  starting transfers between devices  29.7 us (25%)
  Pallas kernels  29.3 us (24%)
  local copies, waits for them, and re-layouts  5.23 us (4%)
  other arithmetic  1.84 us (2%)
  between operations  1.42 us (1%)
    ppermute x6, waiting for transfers between devices, along_wide(): lax.ppermute(other, 'wide', others)  25.8 us
    pallas_call x5, Pallas kernels, step_call(): pl.pallas_call(functools.partial(kernel, sizes, last), out_shape=[shape(e...  24.7 us
    ppermute x6, starting transfers between devices, along_wide(): lax.ppermute(other, 'wide', others)  14.7 us
    ppermute x6, waiting for transfers between devices, along_narrow(): lax.ppermute(down, 'narrow', down_ring)  14.1 us
    ppermute x6, waiting for transfers between devices, along_narrow(): lax.ppermute(up, 'narrow', up_ring)  11 us
    ppermute x6, starting transfers between devices, along_narrow(): lax.ppermute(up, 'narrow', up_ring)  8.5 us
    ppermute x6, starting transfers between devices, along_narrow(): lax.ppermute(down, 'narrow', down_ring)  6.45 us
    unnamed x10, local copies, waits for them, and re-layouts  4.28 us
  transfers between devices with their start and end apart: 24, of which 19 were waited for; matrix products, arithmetic and copies ran while one was open for 1% of the time, Pallas kernels for 0%

commit v1 on v0

v1 whole, which is shorter than its diff:
```python
import functools

import jax
import jax.numpy as jnp
from jax import lax
from jax.experimental import pallas as pl
from jax.experimental.pallas import tpu as pltpu
from jax.sharding import PartitionSpec as P

ITERS = 5
descent = 0.1

ROW_FIRST, ROW_LAST, COL_FIRST, COL_LAST, EVEN = range(5)


def cast_low(value):
    return value.astype(jnp.bfloat16)


def wide_value(value):
    return value.astype(jnp.float32)


def kept(value, drop):
    return jnp.where(drop, jnp.zeros_like(value), value)


def half_step(source_ref, blocks_ref, total_ref, source_ids, target_ids, slots):
    for slot in range(slots):
        product = jnp.dot(
            source_ref[source_ids[slot]], blocks_ref[slot], preferred_element_type=jnp.float32
        )
        target = target_ids[slot]
        total_ref[target] = total_ref[target] + product


def products(sizes, rows_ref, cols_ref, observed_ref, blocks_ref, turned_ref, grad_ref, residual_ref, low_ref, rlow_ref):
    tile_x, tile_y, slots = sizes
    own = tile_x * tile_y
    extended = (tile_x + 2) * (tile_y + 2)
    low_ref[extended] = jnp.zeros_like(low_ref[extended])
    for block in range(own):
        residual_ref[block] = -observed_ref[block]
    residual_ref[own] = jnp.zeros_like(residual_ref[own])
    half_step(low_ref, blocks_ref, residual_ref, cols_ref, rows_ref, slots)
    for block in range(own + 1):
        rlow_ref[block] = cast_low(residual_ref[block])
    for block in range(extended + 1):
        grad_ref[block] = jnp.zeros_like(grad_ref[block])
    half_step(rlow_ref, turned_ref, grad_ref, rows_ref, cols_ref, slots)


def send_columns(sizes, last, info_ref, grad_ref, pair_ref, next_ref):
    tile_x, tile_y, _ = sizes
    span = tile_y + 2
    even = info_ref[EVEN] == 1
    for out_ref, right in ((pair_ref, even), (next_ref, jnp.logical_not(even))):
        if last:
            col = jnp.where(right, span - 1, 0)
            for row in range(tile_x + 2):
                out_ref[row] = cast_low(grad_ref[row * span + col])
        else:
            col = jnp.where(right, span - 2, 0)
            for row in range(tile_x + 2):
                for step in range(2):
                    out_ref[row * 2 + step] = cast_low(grad_ref[row * span + col + step])


def outside(sizes, info_ref, row, col):
    tile_x, tile_y, _ = sizes
    flag = None
    for hit, place in (
        (row == 0, ROW_FIRST),
        (row == tile_x + 1, ROW_LAST),
        (col == 0, COL_FIRST),
        (col == tile_y + 1, COL_LAST),
    ):
        if hit:
            here = info_ref[place] == 1
            flag = here if flag is None else jnp.logical_or(flag, here)
    return flag


def came_along_wide(sizes, last, info_ref, pair_in, next_in, row, col):
    tile_x, tile_y, _ = sizes
    even = info_ref[EVEN] == 1
    width = 1 if last else 2
    lefts = {1: 0} if last else {0: 0, 1: 1}
    rights = {tile_y: 0} if last else {tile_y: 0, tile_y + 1: 1}
    for places, from_pair, place in (
        (lefts, jnp.logical_not(even), COL_FIRST),
        (rights, even, COL_LAST),
    ):
        if col in places:
            at = row * width + places[col]
            came = jnp.where(from_pair, pair_in[at], next_in[at])
            return kept(wide_value(came), info_ref[place] == 1)
    return None


def turn_kernel(group, blocks_ref, turned_ref):
    def turn(step, carry):
        for place in range(group):
            slot = step * group + place
            turned_ref[slot] = blocks_ref[slot].T
        return carry

    lax.fori_loop(0, blocks_ref.shape[0] // group, turn, 0)


def first_kernel(sizes, info_ref, rows_ref, cols_ref, coef_ref, above_ref, below_ref, pair_in, next_in, observed_ref, blocks_ref, turned_ref, x_ref, grad_ref, pair_ref, next_ref, low_ref, rlow_ref, residual_ref):
    tile_x, tile_y, _ = sizes
    span = tile_y + 2
    even = info_ref[EVEN] == 1
    for row in range(tile_x + 2):
        for col in range(span):
            if col == 0:
                value = wide_value(jnp.where(even, next_in[row], pair_in[row]))
            elif col == tile_y + 1:
                value = wide_value(jnp.where(even, pair_in[row], next_in[row]))
            elif row == 0:
                value = wide_value(above_ref[col - 1])
            elif row == tile_x + 1:
                value = wide_value(below_ref[col - 1])
            else:
                value = coef_ref[(row - 1) * tile_y + col - 1]
            drop = outside(sizes, info_ref, row, col)
            if drop is not None:
                value = kept(value, drop)
            x_ref[row * span + col] = value
            low_ref[row * span + col] = cast_low(value)
    products(sizes, rows_ref, cols_ref, observed_ref, blocks_ref, turned_ref, grad_ref, residual_ref, low_ref, rlow_ref)
    send_columns(sizes, False, info_ref, grad_ref, pair_ref, next_ref)


def step_kernel(sizes, last, info_ref, rows_ref, cols_ref, x_in, grad_in, pair_in, next_in, above_ref, below_ref, observed_ref, blocks_ref, turned_ref, x_ref, grad_ref, pair_ref, next_ref, *rest):
    tile_x, tile_y, _ = sizes
    span = tile_y + 2
    if last:
        residual_ref, low_ref, rlow_ref = rest
    else:
        low_ref, rlow_ref, residual_ref = rest
    first = info_ref[ROW_FIRST] == 1
    final = info_ref[ROW_LAST] == 1
    for row in range(tile_x + 2):
        for col in range(span):
            at = row * span + col
            gradient = grad_in[at]
            came = came_along_wide(sizes, False, info_ref, pair_in, next_in, row, col)
            if came is not None:
                gradient = gradient + came
            if row < 2:
                gradient = gradient + wide_value(kept(above_ref[row * span + col], first))
            elif row >= tile_x:
                gradient = gradient + wide_value(kept(below_ref[(row - tile_x) * span + col], final))
            value = x_in[at] - descent * gradient
            drop = outside(sizes, info_ref, row, col)
            if drop is not None:
                value = kept(value, drop)
            x_ref[at] = value
            low_ref[at] = cast_low(value)
    products(sizes, rows_ref, cols_ref, observed_ref, blocks_ref, turned_ref, grad_ref, residual_ref, low_ref, rlow_ref)
    send_columns(sizes, last, info_ref, grad_ref, pair_ref, next_ref)


def fold_kernel(sizes, last, info_ref, grad_in, pair_in, next_in, up_ref, down_ref):
    tile_x, tile_y, _ = sizes
    span = tile_y + 2

    def folded(row, col):
        value = grad_in[row * span + col]
        came = came_along_wide(sizes, last, info_ref, pair_in, next_in, row, col)
        return cast_low(value if came is None else value + came)

    if last:
        for col in range(1, tile_y + 1):
            up_ref[col - 1] = folded(0, col)
            down_ref[col - 1] = folded(tile_x + 1, col)
    else:
        for row in range(2):
            for col in range(span):
                up_ref[row * span + col] = folded(row, col)
                down_ref[row * span + col] = folded(tile_x + row, col)


def final_kernel(sizes, info_ref, x_in, grad_in, pair_in, next_in, above_ref, below_ref, out_ref):
    tile_x, tile_y, _ = sizes
    span = tile_y + 2
    first = info_ref[ROW_FIRST] == 1
    final = info_ref[ROW_LAST] == 1
    for row in range(1, tile_x + 1):
        for col in range(1, tile_y + 1):
            at = row * span + col
            gradient = grad_in[at]
            came = came_along_wide(sizes, True, info_ref, pair_in, next_in, row, col)
            if came is not None:
                gradient = gradient + came
            if row == 1:
                gradient = gradient + wide_value(kept(above_ref[col - 1], first))
            if row == tile_x:
                gradient = gradient + wide_value(kept(below_ref[col - 1], final))
            out_ref[(row - 1) * tile_y + col - 1] = x_in[at] - descent * gradient


def local(coefficients, observed, blocks, block_rows, block_cols, live_count):
    tile_x, tile_y, frames, width = coefficients.shape
    slots = blocks.shape[2]
    own = tile_x * tile_y
    span = tile_y + 2
    extended = (tile_x + 2) * span
    sizes = (tile_x, tile_y, slots)
    narrow = lax.axis_size("narrow")
    wide = lax.axis_size("wide")
    a = lax.axis_index("narrow")
    b = lax.axis_index("wide")
    info = jnp.stack([a == 0, a == narrow - 1, b == 0, b == wide - 1, b % 2 == 0]).astype(jnp.int32)
    even = b % 2 == 0

    up_ring = [(i, (i - 1) % narrow) for i in range(narrow)]
    down_ring = [(i, (i + 1) % narrow) for i in range(narrow)]
    pairs = [(i, i ^ 1) for i in range(wide)]
    others = [(i, ((i - 1) ^ 1) + 1) for i in range(1, wide - 1)] + [(0, 0), (wide - 1, wide - 1)]

    def along_narrow(up, down):
        return lax.ppermute(down, "narrow", down_ring), lax.ppermute(up, "narrow", up_ring)

    def along_wide(pair, other):
        return lax.ppermute(pair, "wide", pairs), lax.ppermute(other, "wide", others)

    matrices = blocks.reshape(slots, width, width)
    live = jnp.arange(slots, dtype=jnp.int32) < live_count.reshape(())
    row_ids = jnp.where(live, block_rows.reshape(slots), own)
    col_ids = jnp.where(live, block_cols.reshape(slots), extended)
    seen = observed.reshape(own, frames, width)

    smem = pl.BlockSpec(memory_space=pltpu.SMEM)
    vmem = pl.BlockSpec(memory_space=pltpu.VMEM)

    def shape(count, kind):
        return jax.ShapeDtypeStruct((count, frames, width), kind)

    def call(kernel, name, inputs, scalars, outputs, scratch=(), flops=0):
        return pl.pallas_call(
            kernel,
            out_shape=outputs,
            in_specs=[smem] * scalars + [vmem] * (len(inputs) - scalars),
            out_specs=jax.tree.map(lambda _: vmem, outputs),
            scratch_shapes=list(scratch),
            compiler_params=pltpu.CompilerParams(vmem_limit_bytes=24 << 20),
            cost_estimate=pl.CostEstimate(flops=flops, bytes_accessed=1 << 20, transcendentals=0),
            name=name,
        )(*inputs)

    low_scratch = pltpu.VMEM((extended + 1, frames, width), jnp.bfloat16)
    rlow_scratch = pltpu.VMEM((own + 1, frames, width), jnp.bfloat16)
    residual_scratch = pltpu.VMEM((own + 1, frames, width), jnp.float32)
    work = 4 * slots * frames * width * width

    def step_outputs(last):
        sent = tile_x + 2 if last else 2 * (tile_x + 2)
        outputs = [
            shape(extended, jnp.float32),
            shape(extended + 1, jnp.float32),
            shape(sent, jnp.bfloat16),
            shape(sent, jnp.bfloat16),
        ]
        return outputs + [shape(own + 1, jnp.float32)] if last else outputs

    above, below = along_narrow(cast_low(coefficients[0]), cast_low(coefficients[tile_x - 1]))
    turned = call(
        functools.partial(turn_kernel, 32),
        "turn_blocks",
        [matrices],
        0,
        jax.ShapeDtypeStruct(matrices.shape, matrices.dtype),
        flops=work,
    )
    sides = []
    for col in (0, tile_y - 1):
        sides.append(
            jnp.concatenate(
                [above[col : col + 1], cast_low(coefficients[:, col]), below[col : col + 1]], axis=0
            )
        )
    pair_in, next_in = along_wide(
        jnp.where(even, sides[1], sides[0]), jnp.where(even, sides[0], sides[1])
    )
    x, grad, pair_out, next_out = call(
        functools.partial(first_kernel, sizes),
        "first_step",
        [info, row_ids, col_ids, coefficients.reshape(own, frames, width), above, below, pair_in, next_in, seen, matrices, turned],
        3,
        step_outputs(False),
        [low_scratch, rlow_scratch, residual_scratch],
        work,
    )
    for iteration in range(ITERS):
        last = iteration == ITERS - 1
        pair_in, next_in = along_wide(pair_out, next_out)
        rows_sent = tile_y if last else 2 * span
        up, down = call(
            functools.partial(fold_kernel, sizes, last),
            "fold_columns",
            [info, grad, pair_in, next_in],
            1,
            [shape(rows_sent, jnp.bfloat16), shape(rows_sent, jnp.bfloat16)],
        )
        above, below = along_narrow(up, down)
        if last:
            updated = call(
                functools.partial(final_kernel, sizes),
                "final_update",
                [info, x, grad, pair_in, next_in, above, below],
                1,
                shape(own, jnp.float32),
            )
        else:
            ending = iteration == ITERS - 2
            x, grad, pair_out, next_out, *rest = call(
                functools.partial(step_kernel, sizes, ending),
                "one_step",
                [info, row_ids, col_ids, x, grad, pair_in, next_in, above, below, seen, matrices, turned],
                3,
                step_outputs(ending),
                [low_scratch, rlow_scratch] + ([] if ending else [residual_scratch]),
                work,
            )
    residual = rest[0]
    return (
        updated.reshape(coefficients.shape),
        residual[:own].reshape(coefficients.shape),
    )


def solution(mesh):
    placed = (
        P("narrow", "wide", None, None),
        P("narrow", "wide", None, None),
        P("narrow", "wide", None, None, None),
        P("narrow", "wide", None),
        P("narrow", "wide", None),
        P("narrow", "wide"),
    )
    return jax.shard_map(
        local,
        mesh=mesh,
        in_specs=placed,
        out_specs=(P("narrow", "wide", None, None), P("narrow", "wide", None, None)),
        check_vma=False,
    )
```

time: 121 us -> 115 us (0.950)
  the two profiles are of different devices: /device:TPU:6 before, /device:TPU:26 now
where the time goes in v1:
time: 115 us; the launch traced here: 114 us
  waiting for transfers between devices  51.9 us (45%)
  starting transfers between devices  32.7 us (28%)
  Pallas kernels  23.1 us (20%)
  local copies, waits for them, and re-layouts  3.15 us (3%)
  other arithmetic  1.79 us (2%)
  between operations  1.54 us (1%)
    ppermute x6, waiting for transfers between devices, along_wide(): lax.ppermute(other, 'wide', others)  27.4 us
    pallas_call x12, Pallas kernels, call(): pl.pallas_call(kernel, out_shape=outputs, in_specs=[smem] * scalars + [vm...  23.1 us
    ppermute x6, starting transfers between devices, along_wide(): lax.ppermute(other, 'wide', others)  16.8 us
    ppermute x6, waiting for transfers between devices, along_narrow(): lax.ppermute(down, 'narrow', down_ring)  15.7 us
    ppermute x6, starting transfers between devices, along_narrow(): lax.ppermute(down, 'narrow', down_ring)  9.33 us
    ppermute x6, waiting for transfers between devices, along_narrow(): lax.ppermute(up, 'narrow', up_ring)  8.79 us
    ppermute x6, starting transfers between devices, along_narrow(): lax.ppermute(up, 'narrow', up_ring)  5.38 us
  transfers between devices with their start and end apart: 24, of which 16 were waited for; matrix products, arithmetic and copies ran while one was open for 1% of the time, Pallas kernels for 1%

profile of v1, /device:TPU:26, one launch (start us, length us, event | category | flops | bytes accessed | tf_op | source)
XLA Modules:
  0.0 114.2 jit_solution(1242391150611683721)
XLA Ops:
  0.6 1.1 convert.6
  1.7 0.6 collective-permute-start.1
  2.3 1.5 %collective-permute-start = (bf16[8,32,128]{2,1,0:T(8,128)(2,1)S(1)}, bf16[8,32,128]{2,1,0:T(8,128)(2,1)S(1)}, u32[]{:S(2)}, u32[]{:S(2)}) collective-permute-start(bf16[8,32,128]{2,1,0:T(8,128)(2,1)S(1)} %get-tuple-element.67), channel_id=1, source_target_pairs={{0,1},{1,2},{2,3},{3,0},{4,5},{5,6},{6,7},{7,4},{8,9},{9,10},{10,1... | collective-permute-start | bytes 196616 | tf_op jit(solution)/shard_map/ppermute | solution.py:225
  4.5 1.6 %collective-permute-done.1.below_ref = bf16[8,32,128]{2,1,0:T(8,128)(2,1)S(1)} collective-permute-done((bf16[8,32,128]{2,1,0:T(8,128)(2,1)S(1)}, bf16[8,32,128]{2,1,0:T(8,128)(2,1)S(1)}, u32[]{:S(2)}, u32[]{:S(2)}) %collective-permute-start.1) | collective-permute-done | bytes 65568 | tf_op jit(solution)/shard_map/ppermute | solution.py:225
  6.1 1.3 %collective-permute-done.above_ref = bf16[8,32,128]{2,1,0:T(8,128)(2,1)S(1)} collective-permute-done((bf16[8,32,128]{2,1,0:T(8,128)(2,1)S(1)}, bf16[8,32,128]{2,1,0:T(8,128)(2,1)S(1)}, u32[]{:S(2)}, u32[]{:S(2)}) %collective-permute-start) | collective-permute-done | bytes 65568 | tf_op jit(solution)/shard_map/ppermute | solution.py:225
  7.4 4.6 %collective-permute-start.3 = (bf16[6,32,128]{2,1,0:T(8,128)(2,1)S(1)}, bf16[6,32,128]{2,1,0:T(8,128)(2,1)S(1)}, u32[]{:S(2)}, u32[]{:S(2)}) collective-permute-start(bf16[6,32,128]{2,1,0:T(8,128)(2,1)S(1)} %get-tuple-element.68), channel_id=1, source_target_pairs={{4,8},{8,4},{12,16},{16,12},{20,24},{24,20},{28,32},{32,28},{36,40... | collective-permute-start | bytes 147464 | tf_op jit(solution)/shard_map/ppermute | solution.py:228
  12.0 0.7 compare_select_fusion
  12.8 2.2 %copy-done = bf16[1,1,128,128,128]{4,3,2,1,0:T(8,128)(2,1)S(1)} copy-done((bf16[1,1,128,128,128]{4,3,2,1,0:T(8,128)(2,1)S(1)}, bf16[1,1,128,128,128]{4,3,2,1,0:T(8,128)(2,1)}, u32[]{:S(2)}) %copy-start) | copy-done | bytes 4194328
  15.0 1.3 %turn_blocks.1.turned_ref = bf16[128,128,128]{2,1,0:T(8,128)(2,1)S(1)} custom-call(bf16[128,128,128]{2,1,0:T(8,128)(2,1)S(1)} %bitcast.24), custom_call_target="tpu_custom_call" | custom-call | flops 268435456 | bytes 1048576 | tf_op jit(solution)/shard_map/turn_blocks/pallas_call | solution.py:243
  16.4 3.3 %first_step.1 = (f32[60,32,128]{2,1,0:T(8,128)S(1)}, f32[61,32,128]{2,1,0:T(8,128)S(1)}, bf16[12,32,128]{2,1,0:T(8,128)(2,1)S(1)}, bf16[12,32,128]{2,1,0:T(8,128)(2,1)S(1)}) custom-call(s32[5]{0:T(128)S(1)} %convert_element_type.19.info_ref, s32[128]{0:T(128)S(1)} %get-tuple-element.75.rows_ref, s32[128]{0:T(128)S(1)} %get-tuple-element.74.cols_ref, ...), custom_call_target="tpu_custom_call" | custom-call | flops 268435456 | bytes 1048576 | tf_op jit(solution)/shard_map/first_step/pallas_call | solution.py:243
  19.7 0.6 collective-permute-start.4
  20.3 3.1 %collective-permute-start.5 = (bf16[12,32,128]{2,1,0:T(8,128)(2,1)S(1)}, bf16[12,32,128]{2,1,0:T(8,128)(2,1)S(1)}, u32[]{:S(2)}, u32[]{:S(2)}) collective-permute-start(bf16[12,32,128]{2,1,0:T(8,128)(2,1)S(1)} %get-tuple-element.36), channel_id=1, source_target_pairs={{4,8},{8,4},{12,16},{16,12},{20,24},{24,20},{28,32},{32,28},{36,40... | collective-permute-start | bytes 294920 | tf_op jit(solution)/shard_map/ppermute | solution.py:228
  23.4 4.9 %collective-permute-done.5.next_in = bf16[12,32,128]{2,1,0:T(8,128)(2,1)S(1)} collective-permute-done((bf16[12,32,128]{2,1,0:T(8,128)(2,1)S(1)}, bf16[12,32,128]{2,1,0:T(8,128)(2,1)S(1)}, u32[]{:S(2)}, u32[]{:S(2)}) %collective-permute-start.5) | collective-permute-done | bytes 98336 | tf_op jit(solution)/shard_map/ppermute | solution.py:228
  28.4 0.6 fold_columns.5
  29.3 2.6 %collective-permute-start.7 = (bf16[20,32,128]{2,1,0:T(8,128)(2,1)S(1)}, bf16[20,32,128]{2,1,0:T(8,128)(2,1)S(1)}, u32[]{:S(2)}, u32[]{:S(2)}) collective-permute-start(bf16[20,32,128]{2,1,0:T(8,128)(2,1)S(1)} %get-tuple-element.38), channel_id=1, source_target_pairs={{0,3},{1,0},{2,1},{3,2},{4,7},{5,4},{6,5},{7,6},{8,11},{9,8},{10,9... | collective-permute-start | bytes 491528 | tf_op jit(solution)/shard_map/ppermute | solution.py:225
  31.9 3.2 %collective-permute-done.6.above_ref = bf16[20,32,128]{2,1,0:T(8,128)(2,1)S(1)} collective-permute-done((bf16[20,32,128]{2,1,0:T(8,128)(2,1)S(1)}, bf16[20,32,128]{2,1,0:T(8,128)(2,1)S(1)}, u32[]{:S(2)}, u32[]{:S(2)}) %collective-permute-start.6) | collective-permute-done | bytes 163872 | tf_op jit(solution)/shard_map/ppermute | solution.py:225
  35.1 3.5 %one_step.4 = (f32[60,32,128]{2,1,0:T(8,128)S(1)}, f32[61,32,128]{2,1,0:T(8,128)S(1)}, bf16[12,32,128]{2,1,0:T(8,128)(2,1)S(1)}, bf16[12,32,128]{2,1,0:T(8,128)(2,1)S(1)}) custom-call(s32[5]{0:T(128)S(1)} %convert_element_type.19.info_ref, s32[128]{0:T(128)S(1)} %get-tuple-element.75.rows_ref, s32[128]{0:T(128)S(1)} %get-tuple-element.74.cols_ref, ...), custom_call_target="tpu_custom_call" | custom-call | flops 268435456 | bytes 1048576 | tf_op jit(solution)/shard_map/one_step/pallas_call | solution.py:243
  38.8 2.9 %collective-permute-start.9 = (bf16[12,32,128]{2,1,0:T(8,128)(2,1)S(1)}, bf16[12,32,128]{2,1,0:T(8,128)(2,1)S(1)}, u32[]{:S(2)}, u32[]{:S(2)}) collective-permute-start(bf16[12,32,128]{2,1,0:T(8,128)(2,1)S(1)} %get-tuple-element.42), channel_id=1, source_target_pairs={{4,8},{8,4},{12,16},{16,12},{20,24},{24,20},{28,32},{32,28},{36,40... | collective-permute-start | bytes 294920 | tf_op jit(solution)/shard_map/ppermute | solution.py:228
  41.7 5.1 %collective-permute-done.9.next_in = bf16[12,32,128]{2,1,0:T(8,128)(2,1)S(1)} collective-permute-done((bf16[12,32,128]{2,1,0:T(8,128)(2,1)S(1)}, bf16[12,32,128]{2,1,0:T(8,128)(2,1)S(1)}, u32[]{:S(2)}, u32[]{:S(2)}) %collective-permute-start.9) | collective-permute-done | bytes 98336 | tf_op jit(solution)/shard_map/ppermute | solution.py:228
  46.8 0.6 fold_columns.6
  47.4 2.7 %collective-permute-start.10 = (bf16[20,32,128]{2,1,0:T(8,128)(2,1)S(1)}, bf16[20,32,128]{2,1,0:T(8,128)(2,1)S(1)}, u32[]{:S(2)}, u32[]{:S(2)}) collective-permute-start(bf16[20,32,128]{2,1,0:T(8,128)(2,1)S(1)} %get-tuple-element.43), channel_id=1, source_target_pairs={{0,1},{1,2},{2,3},{3,0},{4,5},{5,6},{6,7},{7,4},{8,9},{9,10},{10,1... | collective-permute-start | bytes 491528 | tf_op jit(solution)/shard_map/ppermute | solution.py:225
  50.1 0.7 collective-permute-start.11
  50.8 3.2 %collective-permute-done.10.above_ref = bf16[20,32,128]{2,1,0:T(8,128)(2,1)S(1)} collective-permute-done((bf16[20,32,128]{2,1,0:T(8,128)(2,1)S(1)}, bf16[20,32,128]{2,1,0:T(8,128)(2,1)S(1)}, u32[]{:S(2)}, u32[]{:S(2)}) %collective-permute-start.10) | collective-permute-done | bytes 163872 | tf_op jit(solution)/shard_map/ppermute | solution.py:225
  54.0 2.6 %collective-permute-done.11.below_ref = bf16[20,32,128]{2,1,0:T(8,128)(2,1)S(1)} collective-permute-done((bf16[20,32,128]{2,1,0:T(8,128)(2,1)S(1)}, bf16[20,32,128]{2,1,0:T(8,128)(2,1)S(1)}, u32[]{:S(2)}, u32[]{:S(2)}) %collective-permute-start.11) | collective-permute-done | bytes 163872 | tf_op jit(solution)/shard_map/ppermute | solution.py:225
  56.6 3.5 %one_step.5 = (f32[60,32,128]{2,1,0:T(8,128)S(1)}, f32[61,32,128]{2,1,0:T(8,128)S(1)}, bf16[12,32,128]{2,1,0:T(8,128)(2,1)S(1)}, bf16[12,32,128]{2,1,0:T(8,128)(2,1)S(1)}) custom-call(s32[5]{0:T(128)S(1)} %convert_element_type.19.info_ref, s32[128]{0:T(128)S(1)} %get-tuple-element.75.rows_ref, s32[128]{0:T(128)S(1)} %get-tuple-element.74.cols_ref, ...), custom_call_target="tpu_custom_call" | custom-call | flops 268435456 | bytes 1048576 | tf_op jit(solution)/shard_map/one_step/pallas_call | solution.py:243
  60.5 2.4 %collective-permute-start.13 = (bf16[12,32,128]{2,1,0:T(8,128)(2,1)S(1)}, bf16[12,32,128]{2,1,0:T(8,128)(2,1)S(1)}, u32[]{:S(2)}, u32[]{:S(2)}) collective-permute-start(bf16[12,32,128]{2,1,0:T(8,128)(2,1)S(1)} %get-tuple-element.48), channel_id=1, source_target_pairs={{4,8},{8,4},{12,16},{16,12},{20,24},{24,20},{28,32},{32,28},{36,40... | collective-permute-start | bytes 294920 | tf_op jit(solution)/shard_map/ppermute | solution.py:228
  62.9 5.7 %collective-permute-done.13.next_in = bf16[12,32,128]{2,1,0:T(8,128)(2,1)S(1)} collective-permute-done((bf16[12,32,128]{2,1,0:T(8,128)(2,1)S(1)}, bf16[12,32,128]{2,1,0:T(8,128)(2,1)S(1)}, u32[]{:S(2)}, u32[]{:S(2)}) %collective-permute-start.13) | collective-permute-done | bytes 98336 | tf_op jit(solution)/shard_map/ppermute | solution.py:228
  68.5 0.6 fold_columns.7
  69.1 2.1 %collective-permute-start.14 = (bf16[20,32,128]{2,1,0:T(8,128)(2,1)S(1)}, bf16[20,32,128]{2,1,0:T(8,128)(2,1)S(1)}, u32[]{:S(2)}, u32[]{:S(2)}) collective-permute-start(bf16[20,32,128]{2,1,0:T(8,128)(2,1)S(1)} %get-tuple-element.49), channel_id=1, source_target_pairs={{0,1},{1,2},{2,3},{3,0},{4,5},{5,6},{6,7},{7,4},{8,9},{9,10},{10,1... | collective-permute-start | bytes 491528 | tf_op jit(solution)/shard_map/ppermute | solution.py:225
  71.2 3.3 %collective-permute-done.14.above_ref = bf16[20,32,128]{2,1,0:T(8,128)(2,1)S(1)} collective-permute-done((bf16[20,32,128]{2,1,0:T(8,128)(2,1)S(1)}, bf16[20,32,128]{2,1,0:T(8,128)(2,1)S(1)}, u32[]{:S(2)}, u32[]{:S(2)}) %collective-permute-start.14) | collective-permute-done | bytes 163872 | tf_op jit(solution)/shard_map/ppermute | solution.py:225
  74.5 2.0 %collective-permute-done.15.below_ref = bf16[20,32,128]{2,1,0:T(8,128)(2,1)S(1)} collective-permute-done((bf16[20,32,128]{2,1,0:T(8,128)(2,1)S(1)}, bf16[20,32,128]{2,1,0:T(8,128)(2,1)S(1)}, u32[]{:S(2)}, u32[]{:S(2)}) %collective-permute-start.15) | collective-permute-done | bytes 163872 | tf_op jit(solution)/shard_map/ppermute | solution.py:225
  76.5 3.5 %one_step.6 = (f32[60,32,128]{2,1,0:T(8,128)S(1)}, f32[61,32,128]{2,1,0:T(8,128)S(1)}, bf16[12,32,128]{2,1,0:T(8,128)(2,1)S(1)}, bf16[12,32,128]{2,1,0:T(8,128)(2,1)S(1)}) custom-call(s32[5]{0:T(128)S(1)} %convert_element_type.19.info_ref, s32[128]{0:T(128)S(1)} %get-tuple-element.75.rows_ref, s32[128]{0:T(128)S(1)} %get-tuple-element.74.cols_ref, ...), custom_call_target="tpu_custom_call" | custom-call | flops 268435456 | bytes 1048576 | tf_op jit(solution)/shard_map/one_step/pallas_call | solution.py:243
  80.1 1.9 %collective-permute-start.17 = (bf16[12,32,128]{2,1,0:T(8,128)(2,1)S(1)}, bf16[12,32,128]{2,1,0:T(8,128)(2,1)S(1)}, u32[]{:S(2)}, u32[]{:S(2)}) collective-permute-start(bf16[12,32,128]{2,1,0:T(8,128)(2,1)S(1)} %get-tuple-element.54), channel_id=1, source_target_pairs={{4,8},{8,4},{12,16},{16,12},{20,24},{24,20},{28,32},{32,28},{36,40... | collective-permute-start | bytes 294920 | tf_op jit(solution)/shard_map/ppermute | solution.py:228
  82.1 6.1 %collective-permute-done.17.next_in = bf16[12,32,128]{2,1,0:T(8,128)(2,1)S(1)} collective-permute-done((bf16[12,32,128]{2,1,0:T(8,128)(2,1)S(1)}, bf16[12,32,128]{2,1,0:T(8,128)(2,1)S(1)}, u32[]{:S(2)}, u32[]{:S(2)}) %collective-permute-start.17) | collective-permute-done | bytes 98336 | tf_op jit(solution)/shard_map/ppermute | solution.py:228
  88.2 0.6 fold_columns.8
  88.8 1.4 %collective-permute-start.18 = (bf16[20,32,128]{2,1,0:T(8,128)(2,1)S(1)}, bf16[20,32,128]{2,1,0:T(8,128)(2,1)S(1)}, u32[]{:S(2)}, u32[]{:S(2)}) collective-permute-start(bf16[20,32,128]{2,1,0:T(8,128)(2,1)S(1)} %get-tuple-element.55), channel_id=1, source_target_pairs={{0,1},{1,2},{2,3},{3,0},{4,5},{5,6},{6,7},{7,4},{8,9},{9,10},{10,1... | collective-permute-start | bytes 491528 | tf_op jit(solution)/shard_map/ppermute | solution.py:225
  90.1 0.7 collective-permute-start.19
  90.9 3.3 %collective-permute-done.18.above_ref = bf16[20,32,128]{2,1,0:T(8,128)(2,1)S(1)} collective-permute-done((bf16[20,32,128]{2,1,0:T(8,128)(2,1)S(1)}, bf16[20,32,128]{2,1,0:T(8,128)(2,1)S(1)}, u32[]{:S(2)}, u32[]{:S(2)}) %collective-permute-start.18) | collective-permute-done | bytes 163872 | tf_op jit(solution)/shard_map/ppermute | solution.py:225
  94.2 1.3 %collective-permute-done.19.below_ref = bf16[20,32,128]{2,1,0:T(8,128)(2,1)S(1)} collective-permute-done((bf16[20,32,128]{2,1,0:T(8,128)(2,1)S(1)}, bf16[20,32,128]{2,1,0:T(8,128)(2,1)S(1)}, u32[]{:S(2)}, u32[]{:S(2)}) %collective-permute-start.19) | collective-permute-done | bytes 163872 | tf_op jit(solution)/shard_map/ppermute | solution.py:225
  95.4 3.5 %one_step.7 = (f32[60,32,128]{2,1,0:T(8,128)S(1)}, f32[61,32,128]{2,1,0:T(8,128)S(1)}, bf16[6,32,128]{2,1,0:T(8,128)(2,1)S(1)}, bf16[6,32,128]{2,1,0:T(8,128)(2,1)S(1)}, f32[33,32,128]{2,1,0:T(8,128)S(1)}) custom-call(s32[5]{0:T(128)S(1)} %convert_element_type.19.info_ref, s32[128]{0:T(128)S(1)} %get-tuple-element.75.rows_ref, ...), custom_call_target="tpu_custom_call" | custom-call | flops 268435456 | bytes 1048576 | tf_op jit(solution)/shard_map/one_step/pallas_call | solution.py:243
  99.0 1.9 %collective-permute-start.21 = (bf16[6,32,128]{2,1,0:T(8,128)(2,1)S(1)}, bf16[6,32,128]{2,1,0:T(8,128)(2,1)S(1)}, u32[]{:S(2)}, u32[]{:S(2)}) collective-permute-start(bf16[6,32,128]{2,1,0:T(8,128)(2,1)S(1)} %get-tuple-element.60), channel_id=1, source_target_pairs={{4,8},{8,4},{12,16},{16,12},{20,24},{24,20},{28,32},{32,28},{36,40... | collective-permute-start | bytes 147464 | tf_op jit(solution)/shard_map/ppermute | solution.py:228
  101.0 5.6 %collective-permute-done.21.next_in = bf16[6,32,128]{2,1,0:T(8,128)(2,1)S(1)} collective-permute-done((bf16[6,32,128]{2,1,0:T(8,128)(2,1)S(1)}, bf16[6,32,128]{2,1,0:T(8,128)(2,1)S(1)}, u32[]{:S(2)}, u32[]{:S(2)}) %collective-permute-start.21) | collective-permute-done | bytes 49184 | tf_op jit(solution)/shard_map/ppermute | solution.py:228
  107.1 1.3 %collective-permute-start.22 = (bf16[8,32,128]{2,1,0:T(8,128)(2,1)S(1)}, bf16[8,32,128]{2,1,0:T(8,128)(2,1)S(1)}, u32[]{:S(2)}, u32[]{:S(2)}) collective-permute-start(bf16[8,32,128]{2,1,0:T(8,128)(2,1)S(1)} %get-tuple-element.61), channel_id=1, source_target_pairs={{0,1},{1,2},{2,3},{3,0},{4,5},{5,6},{6,7},{7,4},{8,9},{9,10},{10,1... | collective-permute-start | bytes 196616 | tf_op jit(solution)/shard_map/ppermute | solution.py:225
  108.5 0.7 collective-permute-start.23
  109.2 0.8 slice.39
  110.0 1.4 %collective-permute-done.22.above_ref = bf16[8,32,128]{2,1,0:T(8,128)(2,1)S(1)} collective-permute-done((bf16[8,32,128]{2,1,0:T(8,128)(2,1)S(1)}, bf16[8,32,128]{2,1,0:T(8,128)(2,1)S(1)}, u32[]{:S(2)}, u32[]{:S(2)}) %collective-permute-start.22) | collective-permute-done | bytes 65568 | tf_op jit(solution)/shard_map/ppermute | solution.py:225
  111.4 1.3 %collective-permute-done.23.below_ref = bf16[8,32,128]{2,1,0:T(8,128)(2,1)S(1)} collective-permute-done((bf16[8,32,128]{2,1,0:T(8,128)(2,1)S(1)}, bf16[8,32,128]{2,1,0:T(8,128)(2,1)S(1)}, u32[]{:S(2)}, u32[]{:S(2)}) %collective-permute-start.23) | collective-permute-done | bytes 65568 | tf_op jit(solution)/shard_map/ppermute | solution.py:225
  112.7 1.4 %final_update.1 = f32[32,32,128]{2,1,0:T(8,128)} custom-call(s32[5]{0:T(128)S(1)} %convert_element_type.19.info_ref, f32[60,32,128]{2,1,0:T(8,128)S(1)} %get-tuple-element.57.x_in, f32[61,32,128]{2,1,0:T(8,128)S(1)} %get-tuple-element.58.grad_in, bf16[6,32,128]{2,1,0:T(8,128)(2,1)S(1)} %collective-permute-done.20.pair_in, ...), custom_call_target="tpu_custom_call" | custom-call | bytes 1048576 | tf_op jit(solution)/shard_map/final_update/pallas_call | solution.py:243
  (30 shorter events, 1.7 us)
Async XLA Ops:
  1.7 4.3 %collective-permute-start.1 = (bf16[8,32,128]{2,1,0:T(8,128)(2,1)S(1)}, bf16[8,32,128]{2,1,0:T(8,128)(2,1)S(1)}, u32[]{:S(2)}, u32[]{:S(2)}) collective-permute-start(bf16[8,32,128]{2,1,0:T(8,128)(2,1)S(1)} %get-tuple-element.66), channel_id=1, source_target_pairs={{0,3},{1,0},{2,1},{3,2},{4,7},{5,4},{6,5},{7,6},{8,11},{9,8},{10,9... | collective-permute-start | bytes 196616 | tf_op jit(solution)/shard_map/ppermute | solution.py:225
  2.3 5.0 %collective-permute-start = (bf16[8,32,128]{2,1,0:T(8,128)(2,1)S(1)}, bf16[8,32,128]{2,1,0:T(8,128)(2,1)S(1)}, u32[]{:S(2)}, u32[]{:S(2)}) collective-permute-start(bf16[8,32,128]{2,1,0:T(8,128)(2,1)S(1)} %get-tuple-element.67), channel_id=1, source_target_pairs={{0,1},{1,2},{2,3},{3,0},{4,5},{5,6},{6,7},{7,4},{8,9},{9,10},{10,1... | collective-permute-start | bytes 196616 | tf_op jit(solution)/shard_map/ppermute | solution.py:225
  7.4 9.0 %collective-permute-start.3 = (bf16[6,32,128]{2,1,0:T(8,128)(2,1)S(1)}, bf16[6,32,128]{2,1,0:T(8,128)(2,1)S(1)}, u32[]{:S(2)}, u32[]{:S(2)}) collective-permute-start(bf16[6,32,128]{2,1,0:T(8,128)(2,1)S(1)} %get-tuple-element.68), channel_id=1, source_target_pairs={{4,8},{8,4},{12,16},{16,12},{20,24},{24,20},{28,32},{32,28},{36,40... | collective-permute-start | bytes 147464 | tf_op jit(solution)/shard_map/ppermute | solution.py:228
  11.9 4.4 %collective-permute-start.2 = (bf16[6,32,128]{2,1,0:T(8,128)(2,1)S(1)}, bf16[6,32,128]{2,1,0:T(8,128)(2,1)S(1)}, u32[]{:S(2)}, u32[]{:S(2)}) collective-permute-start(bf16[6,32,128]{2,1,0:T(8,128)(2,1)S(1)} %get-tuple-element.69), channel_id=1, source_target_pairs={{0,4},{4,0},{8,12},{12,8},{16,20},{20,16},{24,28},{28,24},{32,36},... | collective-permute-start | bytes 147464 | tf_op jit(solution)/shard_map/ppermute | solution.py:228
  12.8 2.2 %copy-start = (bf16[1,1,128,128,128]{4,3,2,1,0:T(8,128)(2,1)S(1)}, bf16[1,1,128,128,128]{4,3,2,1,0:T(8,128)(2,1)}, u32[]{:S(2)}) copy-start(bf16[1,1,128,128,128]{4,3,2,1,0:T(8,128)(2,1)} %param.8) | copy-start | bytes 12582916
  15.0 1.3 %copy-start.2 = (f32[4,8,32,128]{3,2,1,0:T(8,128)S(1)}, f32[4,8,32,128]{3,2,1,0:T(8,128)}, u32[]{:S(2)}) copy-start(f32[4,8,32,128]{3,2,1,0:T(8,128)} %param.7) | copy-start | bytes 1572868
  15.0 1.3 %copy-start.3 = (f32[4,8,32,128]{3,2,1,0:T(8,128)S(1)}, f32[4,8,32,128]{3,2,1,0:T(8,128)}, u32[]{:S(2)}) copy-start(f32[4,8,32,128]{3,2,1,0:T(8,128)} %param.6) | copy-start | bytes 1572868
  16.4 18.8 %copy-start.1 = (bf16[1,1,128,128,128]{4,3,2,1,0:T(8,128)(2,1)S(1)}, bf16[1,1,128,128,128]{4,3,2,1,0:T(8,128)(2,1)}, u32[]{:S(2)}) copy-start(bf16[1,1,128,128,128]{4,3,2,1,0:T(8,128)(2,1)} %param.8) | copy-start | bytes 12582916
  19.7 3.7 %collective-permute-start.4 = (bf16[12,32,128]{2,1,0:T(8,128)(2,1)S(1)}, bf16[12,32,128]{2,1,0:T(8,128)(2,1)S(1)}, u32[]{:S(2)}, u32[]{:S(2)}) collective-permute-start(bf16[12,32,128]{2,1,0:T(8,128)(2,1)S(1)} %get-tuple-element.35), channel_id=1, source_target_pairs={{0,4},{4,0},{8,12},{12,8},{16,20},{20,16},{24,28},{28,24},{32,36},... | collective-permute-start | bytes 294920 | tf_op jit(solution)/shard_map/ppermute | solution.py:228
  20.3 8.0 %collective-permute-start.5 = (bf16[12,32,128]{2,1,0:T(8,128)(2,1)S(1)}, bf16[12,32,128]{2,1,0:T(8,128)(2,1)S(1)}, u32[]{:S(2)}, u32[]{:S(2)}) collective-permute-start(bf16[12,32,128]{2,1,0:T(8,128)(2,1)S(1)} %get-tuple-element.36), channel_id=1, source_target_pairs={{4,8},{8,4},{12,16},{16,12},{20,24},{24,20},{28,32},{32,28},{36,40... | collective-permute-start | bytes 294920 | tf_op jit(solution)/shard_map/ppermute | solution.py:228
  29.0 6.2 %collective-permute-start.6 = (bf16[20,32,128]{2,1,0:T(8,128)(2,1)S(1)}, bf16[20,32,128]{2,1,0:T(8,128)(2,1)S(1)}, u32[]{:S(2)}, u32[]{:S(2)}) collective-permute-start(bf16[20,32,128]{2,1,0:T(8,128)(2,1)S(1)} %get-tuple-element.37), channel_id=1, source_target_pairs={{0,1},{1,2},{2,3},{3,0},{4,5},{5,6},{6,7},{7,4},{8,9},{9,10},{10,1... | collective-permute-start | bytes 491528 | tf_op jit(solution)/shard_map/ppermute | solution.py:225
  29.3 5.8 %collective-permute-start.7 = (bf16[20,32,128]{2,1,0:T(8,128)(2,1)S(1)}, bf16[20,32,128]{2,1,0:T(8,128)(2,1)S(1)}, u32[]{:S(2)}, u32[]{:S(2)}) collective-permute-start(bf16[20,32,128]{2,1,0:T(8,128)(2,1)S(1)} %get-tuple-element.38), channel_id=1, source_target_pairs={{0,3},{1,0},{2,1},{3,2},{4,7},{5,4},{6,5},{7,6},{8,11},{9,8},{10,9... | collective-permute-start | bytes 491528 | tf_op jit(solution)/shard_map/ppermute | solution.py:225
  38.7 3.0 %collective-permute-start.8 = (bf16[12,32,128]{2,1,0:T(8,128)(2,1)S(1)}, bf16[12,32,128]{2,1,0:T(8,128)(2,1)S(1)}, u32[]{:S(2)}, u32[]{:S(2)}) collective-permute-start(bf16[12,32,128]{2,1,0:T(8,128)(2,1)S(1)} %get-tuple-element.41), channel_id=1, source_target_pairs={{0,4},{4,0},{8,12},{12,8},{16,20},{20,16},{24,28},{28,24},{32,36},... | collective-permute-start | bytes 294920 | tf_op jit(solution)/shard_map/ppermute | solution.py:228
  38.8 8.0 %collective-permute-start.9 = (bf16[12,32,128]{2,1,0:T(8,128)(2,1)S(1)}, bf16[12,32,128]{2,1,0:T(8,128)(2,1)S(1)}, u32[]{:S(2)}, u32[]{:S(2)}) collective-permute-start(bf16[12,32,128]{2,1,0:T(8,128)(2,1)S(1)} %get-tuple-element.42), channel_id=1, source_target_pairs={{4,8},{8,4},{12,16},{16,12},{20,24},{24,20},{28,32},{32,28},{36,40... | collective-permute-start | bytes 294920 | tf_op jit(solution)/shard_map/ppermute | solution.py:228
  47.4 6.6 %collective-permute-start.10 = (bf16[20,32,128]{2,1,0:T(8,128)(2,1)S(1)}, bf16[20,32,128]{2,1,0:T(8,128)(2,1)S(1)}, u32[]{:S(2)}, u32[]{:S(2)}) collective-permute-start(bf16[20,32,128]{2,1,0:T(8,128)(2,1)S(1)} %get-tuple-element.43), channel_id=1, source_target_pairs={{0,1},{1,2},{2,3},{3,0},{4,5},{5,6},{6,7},{7,4},{8,9},{9,10},{10,1... | collective-permute-start | bytes 491528 | tf_op jit(solution)/shard_map/ppermute | solution.py:225
  50.1 6.5 %collective-permute-start.11 = (bf16[20,32,128]{2,1,0:T(8,128)(2,1)S(1)}, bf16[20,32,128]{2,1,0:T(8,128)(2,1)S(1)}, u32[]{:S(2)}, u32[]{:S(2)}) collective-permute-start(bf16[20,32,128]{2,1,0:T(8,128)(2,1)S(1)} %get-tuple-element.44), channel_id=1, source_target_pairs={{0,3},{1,0},{2,1},{3,2},{4,7},{5,4},{6,5},{7,6},{8,11},{9,8},{10,9... | collective-permute-start | bytes 491528 | tf_op jit(solution)/shard_map/ppermute | solution.py:225
  60.2 2.7 %collective-permute-start.12 = (bf16[12,32,128]{2,1,0:T(8,128)(2,1)S(1)}, bf16[12,32,128]{2,1,0:T(8,128)(2,1)S(1)}, u32[]{:S(2)}, u32[]{:S(2)}) collective-permute-start(bf16[12,32,128]{2,1,0:T(8,128)(2,1)S(1)} %get-tuple-element.47), channel_id=1, source_target_pairs={{0,4},{4,0},{8,12},{12,8},{16,20},{20,16},{24,28},{28,24},{32,36},... | collective-permute-start | bytes 294920 | tf_op jit(solution)/shard_map/ppermute | solution.py:228
  60.5 8.0 %collective-permute-start.13 = (bf16[12,32,128]{2,1,0:T(8,128)(2,1)S(1)}, bf16[12,32,128]{2,1,0:T(8,128)(2,1)S(1)}, u32[]{:S(2)}, u32[]{:S(2)}) collective-permute-start(bf16[12,32,128]{2,1,0:T(8,128)(2,1)S(1)} %get-tuple-element.48), channel_id=1, source_target_pairs={{4,8},{8,4},{12,16},{16,12},{20,24},{24,20},{28,32},{32,28},{36,40... | collective-permute-start | bytes 294920 | tf_op jit(solution)/shard_map/ppermute | solution.py:228
  69.1 5.4 %collective-permute-start.14 = (bf16[20,32,128]{2,1,0:T(8,128)(2,1)S(1)}, bf16[20,32,128]{2,1,0:T(8,128)(2,1)S(1)}, u32[]{:S(2)}, u32[]{:S(2)}) collective-permute-start(bf16[20,32,128]{2,1,0:T(8,128)(2,1)S(1)} %get-tuple-element.49), channel_id=1, source_target_pairs={{0,1},{1,2},{2,3},{3,0},{4,5},{5,6},{6,7},{7,4},{8,9},{9,10},{10,1... | collective-permute-start | bytes 491528 | tf_op jit(solution)/shard_map/ppermute | solution.py:225
  71.2 5.3 %collective-permute-start.15 = (bf16[20,32,128]{2,1,0:T(8,128)(2,1)S(1)}, bf16[20,32,128]{2,1,0:T(8,128)(2,1)S(1)}, u32[]{:S(2)}, u32[]{:S(2)}) collective-permute-start(bf16[20,32,128]{2,1,0:T(8,128)(2,1)S(1)} %get-tuple-element.50), channel_id=1, source_target_pairs={{0,3},{1,0},{2,1},{3,2},{4,7},{5,4},{6,5},{7,6},{8,11},{9,8},{10,9... | collective-permute-start | bytes 491528 | tf_op jit(solution)/shard_map/ppermute | solution.py:225
  80.0 2.0 %collective-permute-start.16 = (bf16[12,32,128]{2,1,0:T(8,128)(2,1)S(1)}, bf16[12,32,128]{2,1,0:T(8,128)(2,1)S(1)}, u32[]{:S(2)}, u32[]{:S(2)}) collective-permute-start(bf16[12,32,128]{2,1,0:T(8,128)(2,1)S(1)} %get-tuple-element.53), channel_id=1, source_target_pairs={{0,4},{4,0},{8,12},{12,8},{16,20},{20,16},{24,28},{28,24},{32,36},... | collective-permute-start | bytes 294920 | tf_op jit(solution)/shard_map/ppermute | solution.py:228
  80.1 8.0 %collective-permute-start.17 = (bf16[12,32,128]{2,1,0:T(8,128)(2,1)S(1)}, bf16[12,32,128]{2,1,0:T(8,128)(2,1)S(1)}, u32[]{:S(2)}, u32[]{:S(2)}) collective-permute-start(bf16[12,32,128]{2,1,0:T(8,128)(2,1)S(1)} %get-tuple-element.54), channel_id=1, source_target_pairs={{4,8},{8,4},{12,16},{16,12},{20,24},{24,20},{28,32},{32,28},{36,40... | collective-permute-start | bytes 294920 | tf_op jit(solution)/shard_map/ppermute | solution.py:228
  88.8 5.4 %collective-permute-start.18 = (bf16[20,32,128]{2,1,0:T(8,128)(2,1)S(1)}, bf16[20,32,128]{2,1,0:T(8,128)(2,1)S(1)}, u32[]{:S(2)}, u32[]{:S(2)}) collective-permute-start(bf16[20,32,128]{2,1,0:T(8,128)(2,1)S(1)} %get-tuple-element.55), channel_id=1, source_target_pairs={{0,1},{1,2},{2,3},{3,0},{4,5},{5,6},{6,7},{7,4},{8,9},{9,10},{10,1... | collective-permute-start | bytes 491528 | tf_op jit(solution)/shard_map/ppermute | solution.py:225
  90.1 5.3 %collective-permute-start.19 = (bf16[20,32,128]{2,1,0:T(8,128)(2,1)S(1)}, bf16[20,32,128]{2,1,0:T(8,128)(2,1)S(1)}, u32[]{:S(2)}, u32[]{:S(2)}) collective-permute-start(bf16[20,32,128]{2,1,0:T(8,128)(2,1)S(1)} %get-tuple-element.56), channel_id=1, source_target_pairs={{0,3},{1,0},{2,1},{3,2},{4,7},{5,4},{6,5},{7,6},{8,11},{9,8},{10,9... | collective-permute-start | bytes 491528 | tf_op jit(solution)/shard_map/ppermute | solution.py:225
  98.9 2.0 %collective-permute-start.20 = (bf16[6,32,128]{2,1,0:T(8,128)(2,1)S(1)}, bf16[6,32,128]{2,1,0:T(8,128)(2,1)S(1)}, u32[]{:S(2)}, u32[]{:S(2)}) collective-permute-start(bf16[6,32,128]{2,1,0:T(8,128)(2,1)S(1)} %get-tuple-element.59), channel_id=1, source_target_pairs={{0,4},{4,0},{8,12},{12,8},{16,20},{20,16},{24,28},{28,24},{32,36},... | collective-permute-start | bytes 147464 | tf_op jit(solution)/shard_map/ppermute | solution.py:228
  99.0 7.5 %collective-permute-start.21 = (bf16[6,32,128]{2,1,0:T(8,128)(2,1)S(1)}, bf16[6,32,128]{2,1,0:T(8,128)(2,1)S(1)}, u32[]{:S(2)}, u32[]{:S(2)}) collective-permute-start(bf16[6,32,128]{2,1,0:T(8,128)(2,1)S(1)} %get-tuple-element.60), channel_id=1, source_target_pairs={{4,8},{8,4},{12,16},{16,12},{20,24},{24,20},{28,32},{32,28},{36,40... | collective-permute-start | bytes 147464 | tf_op jit(solution)/shard_map/ppermute | solution.py:228
  107.1 4.3 %collective-permute-start.22 = (bf16[8,32,128]{2,1,0:T(8,128)(2,1)S(1)}, bf16[8,32,128]{2,1,0:T(8,128)(2,1)S(1)}, u32[]{:S(2)}, u32[]{:S(2)}) collective-permute-start(bf16[8,32,128]{2,1,0:T(8,128)(2,1)S(1)} %get-tuple-element.61), channel_id=1, source_target_pairs={{0,1},{1,2},{2,3},{3,0},{4,5},{5,6},{6,7},{7,4},{8,9},{9,10},{10,1... | collective-permute-start | bytes 196616 | tf_op jit(solution)/shard_map/ppermute | solution.py:225
  108.5 4.3 %collective-permute-start.23 = (bf16[8,32,128]{2,1,0:T(8,128)(2,1)S(1)}, bf16[8,32,128]{2,1,0:T(8,128)(2,1)S(1)}, u32[]{:S(2)}, u32[]{:S(2)}) collective-permute-start(bf16[8,32,128]{2,1,0:T(8,128)(2,1)S(1)} %get-tuple-element.62), channel_id=1, source_target_pairs={{0,3},{1,0},{2,1},{3,2},{4,7},{5,4},{6,5},{7,6},{8,11},{9,8},{10,9... | collective-permute-start | bytes 196616 | tf_op jit(solution)/shard_map/ppermute | solution.py:225

commit v2 on v1

--- a/solution.py
+++ b/solution.py
@@ -98,14 +98,32 @@
     return None
 
 
-def turn_kernel(group, blocks_ref, turned_ref):
-    def turn(step, carry):
-        for place in range(group):
-            slot = step * group + place
+def prepare_kernel(sizes, chunks, flags_ref, live_ref, rows_in, cols_in, blocks_in, info_ref, rows_ref, cols_ref, blocks_ref, turned_ref, arrived):
+    tile_x, tile_y, slots = sizes
+    size = slots // chunks
+
+    def bring(chunk):
+        part = pl.ds(chunk * size, size)
+        return pltpu.make_async_copy(blocks_in.at[part], blocks_ref.at[part], arrived.at[chunk])
+
+    for chunk in range(chunks):
+        bring(chunk).start()
+    for place in range(5):
+        info_ref[place] = flags_ref[place]
+    live = live_ref[0]
+
+    def copy(slot, carry):
+        used = slot < live
+        rows_ref[slot] = jnp.where(used, rows_in[slot], tile_x * tile_y)
+        cols_ref[slot] = jnp.where(used, cols_in[slot], (tile_x + 2) * (tile_y + 2))
+        return carry
+
+    lax.fori_loop(0, slots, copy, 0)
+    for chunk in range(chunks):
+        bring(chunk).wait()
+        for place in range(size):
+            slot = chunk * size + place
             turned_ref[slot] = blocks_ref[slot].T
-        return carry
-
-    lax.fori_loop(0, blocks_ref.shape[0] // group, turn, 0)
 
 
 def first_kernel(sizes, info_ref, rows_ref, cols_ref, coef_ref, above_ref, below_ref, pair_in, next_in, observed_ref, blocks_ref, turned_ref, x_ref, grad_ref, pair_ref, next_ref, low_ref, rlow_ref, residual_ref):
@@ -213,24 +231,34 @@
     wide = lax.axis_size("wide")
     a = lax.axis_index("narrow")
     b = lax.axis_index("wide")
-    info = jnp.stack([a == 0, a == narrow - 1, b == 0, b == wide - 1, b % 2 == 0]).astype(jnp.int32)
+    flags = jnp.stack([a == 0, a == narrow - 1, b == 0, b == wide - 1, b % 2 == 0]).astype(jnp.int32)
     even = b % 2 == 0
 
-    up_ring = [(i, (i - 1) % narrow) for i in range(narrow)]
-    down_ring = [(i, (i + 1) % narrow) for i in range(narrow)]
-    pairs = [(i, i ^ 1) for i in range(wide)]
-    others = [(i, ((i - 1) ^ 1) + 1) for i in range(1, wide - 1)] + [(0, 0), (wide - 1, wide - 1)]
+    def everywhere(move):
+        return [
+            (i * narrow + j, to_i * narrow + to_j)
+            for i in range(wide)
+            for j in range(narrow)
+            for to_i, to_j in [move(i, j)]
+        ]
+
+    def other(i, j):
+        return (i, j ^ 1) if i in (0, wide - 1) else (((i - 1) ^ 1) + 1, j)
+
+    up_ring = everywhere(lambda i, j: (i, (j - 1) % narrow))
+    down_ring = everywhere(lambda i, j: (i, (j + 1) % narrow))
+    pairs = everywhere(lambda i, j: (i ^ 1, j))
+    others = everywhere(other)
+
+    def send(value, ring):
+        return lax.ppermute(value, ("wide", "narrow"), ring)
 
     def along_narrow(up, down):
-        return lax.ppermute(down, "narrow", down_ring), lax.ppermute(up, "narrow", up_ring)
+        return send(down, down_ring), send(up, up_ring)
 
     def along_wide(pair, other):
-        return lax.ppermute(pair, "wide", pairs), lax.ppermute(other, "wide", others)
-
-    matrices = blocks.reshape(slots, width, width)
-    live = jnp.arange(slots, dtype=jnp.int32) < live_count.reshape(())
-    row_ids = jnp.where(live, block_rows.reshape(slots), own)
-    col_ids = jnp.where(live, block_cols.reshape(slots), extended)
+        return send(pair, pairs), send(other, others)
+
     seen = observed.reshape(own, frames, width)
 
     smem = pl.BlockSpec(memory_space=pltpu.SMEM)
@@ -238,13 +266,16 @@
 
     def shape(count, kind):
         return jax.ShapeDtypeStruct((count, frames, width), kind)
+
+    def place(output):
+        return vmem if len(output.shape) > 1 else smem
 
     def call(kernel, name, inputs, scalars, outputs, scratch=(), flops=0):
         return pl.pallas_call(
             kernel,
             out_shape=outputs,
             in_specs=[smem] * scalars + [vmem] * (len(inputs) - scalars),
-            out_specs=jax.tree.map(lambda _: vmem, outputs),
+            out_specs=jax.tree.map(place, outputs),
             scratch_shapes=list(scratch),
             compiler_params=pltpu.CompilerParams(vmem_limit_bytes=24 << 20),
             cost_estimate=pl.CostEstimate(flops=flops, bytes_accessed=1 << 20, transcendentals=0),
@@ -266,22 +297,32 @@
         ]
         return outputs + [shape(own + 1, jnp.float32)] if last else outputs
 
-    above, below = along_narrow(cast_low(coefficients[0]), cast_low(coefficients[tile_x - 1]))
-    turned = call(
-        functools.partial(turn_kernel, 32),
-        "turn_blocks",
-        [matrices],
-        0,
-        jax.ShapeDtypeStruct(matrices.shape, matrices.dtype),
-        flops=work,
-    )
+    edges = lax.optimization_barrier(
+        (coefficients[0], coefficients[tile_x - 1], coefficients[:, 0], coefficients[:, tile_y - 1])
+    )
+    top, bottom, left, right = [cast_low(edge) for edge in edges]
+    above, below = along_narrow(top, bottom)
+    chunks = 8
+    info, row_ids, col_ids, matrices, turned = pl.pallas_call(
+        functools.partial(prepare_kernel, sizes, chunks),
+        out_shape=[
+            pltpu.SMEM((5,), jnp.int32),
+            pltpu.SMEM((slots,), jnp.int32),
+            pltpu.SMEM((slots,), jnp.int32),
+            pltpu.VMEM((slots, width, width), jnp.bfloat16),
+            pltpu.VMEM((slots, width, width), jnp.bfloat16),
+        ],
+        in_specs=[smem] * 4 + [pl.BlockSpec(memory_space=pltpu.HBM)],
+        out_specs=[smem] * 3 + [vmem] * 2,
+        scratch_shapes=[pltpu.SemaphoreType.DMA((chunks,))],
+        compiler_params=pltpu.CompilerParams(vmem_limit_bytes=24 << 20),
+        cost_estimate=pl.CostEstimate(flops=work, bytes_accessed=12 << 20, transcendentals=0),
+        name="prepare_slots",
+    )(flags, live_count.reshape(1), block_rows.reshape(slots), block_cols.reshape(slots), pltpu.with_memory_space_constraint(blocks.reshape(slots, width, width), pltpu.HBM))
+    above, below, turned = lax.optimization_barrier((above, below, turned))
     sides = []
-    for col in (0, tile_y - 1):
-        sides.append(
-            jnp.concatenate(
-                [above[col : col + 1], cast_low(coefficients[:, col]), below[col : col + 1]], axis=0
-            )
-        )
+    for col, edge in ((0, left), (tile_y - 1, right)):
+        sides.append(jnp.concatenate([above[col : col + 1], edge, below[col : col + 1]], axis=0))
     pair_in, next_in = along_wide(
         jnp.where(even, sides[1], sides[0]), jnp.where(even, sides[0], sides[1])
     )

time: 115 us -> 97.6 us (0.85)
  starting transfers between devices: 32.7 us -> 25 us
  waiting for transfers between devices: 51.9 us -> 47 us
  Pallas kernels: 23.1 us -> 19.2 us
  other arithmetic: 1.79 us -> 0.03 us
    ppermute x24, starting transfers between devices: 32.7 us -> 25 us  [send(): return lax.ppermute(value, ('wide', 'narrow'), ring)]
    pallas_call x12 -> x11, Pallas kernels: 23.1 us -> 16 us  [call(): pl.pallas_call(kernel, out_shape=outputs, in_specs=[smem] * scalars + [vm...]
    ppermute x24, waiting for transfers between devices: 51.9 us -> 47 us  [send(): return lax.ppermute(value, ('wide', 'narrow'), ring)]
    pallas_call x0 -> x1, Pallas kernels: none -> 3.19 us  [local(): pl.pallas_call(functools.partial(prepare_kernel, sizes, chunks), out_shap...]
    squeeze x0 -> x2, local copies, waits for them, and re-layouts: none -> 1.97 us  [the longest x1 0.99 us: local(): coefficients[tile_x - 1]]
  transfers between devices with their start and end apart: 24 -> 24, of which waited for: 16 -> 18; matrix products, arithmetic and copies ran while one was open for 1% -> 1% of each run, Pallas kernels for 1% -> 3%
where the time goes in v2:
time: 97.6 us; the launch traced here: 96.9 us
  waiting for transfers between devices  47 us (48%)
  starting transfers between devices  25 us (26%)
  Pallas kernels  19.2 us (20%)
  local copies, waits for them, and re-layouts  4.23 us (4%)
  between operations  1.46 us (1%)
    ppermute x24, waiting for transfers between devices, send(): return lax.ppermute(value, ('wide', 'narrow'), ring)  47 us
    ppermute x24, starting transfers between devices, send(): return lax.ppermute(value, ('wide', 'narrow'), ring)  25 us
    pallas_call x11, Pallas kernels, call(): pl.pallas_call(kernel, out_shape=outputs, in_specs=[smem] * scalars + [vm...  16 us
    pallas_call x1, Pallas kernels, local(): pl.pallas_call(functools.partial(prepare_kernel, sizes, chunks), out_shap...  3.19 us
  transfers between devices with their start and end apart: 24, of which 18 were waited for; matrix products, arithmetic and copies ran while one was open for 1% of the time, Pallas kernels for 3%

profile of v2, /device:TPU:26, one launch (start us, length us, event | category | flops | bytes accessed | tf_op | source)
XLA Modules:
  0.0 96.9 jit_solution(5620262221366322705)
XLA Ops:
  0.7 1.0 %slice_bitcast_fusion.2 = (bf16[4,32,128]{2,1,0:T(8,128)(2,1)S(1)}, bf16[4,32,128]{2,1,0:T(8,128)(2,1)S(1)}) fusion(f32[4,8,32,128]{3,2,1,0:T(8,128)} %param.6), kind=kLoop, calls=%fused_computation.2 | loop fusion | bytes 131072 | tf_op jit(solution)/shard_map/squeeze | solution.py:301
  1.6 1.0 %slice_bitcast_fusion = (bf16[8,32,128]{2,1,0:T(8,128)(2,1)S(1)}, bf16[8,32,128]{2,1,0:T(8,128)(2,1)S(1)}) fusion(f32[4,8,32,128]{3,2,1,0:T(8,128)} %param.6), kind=kLoop, calls=%fused_computation | loop fusion | bytes 262144 | tf_op jit(solution)/shard_map/squeeze | solution.py:301
  2.6 1.6 %collective-permute-start = (bf16[8,32,128]{2,1,0:T(8,128)(2,1)S(1)}, bf16[8,32,128]{2,1,0:T(8,128)(2,1)S(1)}, u32[]{:S(2)}, u32[]{:S(2)}) collective-permute-start(bf16[8,32,128]{2,1,0:T(8,128)(2,1)S(1)} %get-tuple-element.48), channel_id=1, source_target_pairs={{0,1},{1,2},{2,3},{3,0},{4,5},{5,6},{6,7},{7,4},{8,9},{9,10},{10,1... | collective-permute-start | bytes 196616 | tf_op jit(solution)/shard_map/ppermute | solution.py:254
  4.2 0.5 collective-permute-start.1
  5.4 0.1 stack.23
  5.5 0.7 copy-done.2
  6.1 0.7 copy-done.3
  6.8 3.2 %prepare_slots.1 = (s32[5]{0:T(128)S(4)}, s32[128]{0:T(128)S(4)}, s32[128]{0:T(128)S(4)}, bf16[128,128,128]{2,1,0:T(8,128)(2,1)S(1)}, bf16[128,128,128]{2,1,0:T(8,128)(2,1)S(1)}) custom-call(s32[5]{0:T(128)S(1)} %convert_element_type.15.flags_ref, s32[1]{0:T(128)} %bitcast.25.live_ref, s32[128]{0:T(128)S(1)} %bitcast.32, s32[128]{0:T(128)S(1)} %bitcast.33, ...), custom_call_target="tpu_custom_call" | custom-call | flops 268435456 | bytes 12582912 | tf_op jit(solution)/shard_map/prepare_slots/pallas_call | solution.py:306
  10.1 3.2 %collective-permute-start.3 = (bf16[6,32,128]{2,1,0:T(8,128)(2,1)S(1)}, bf16[6,32,128]{2,1,0:T(8,128)(2,1)S(1)}, u32[]{:S(2)}, u32[]{:S(2)}) collective-permute-start(bf16[6,32,128]{2,1,0:T(8,128)(2,1)S(1)} %get-tuple-element.92), channel_id=1, source_target_pairs={{0,1},{1,0},{2,3},{3,2},{4,8},{5,9},{6,10},{7,11},{8,4},{9,5},{10,... | collective-permute-start | bytes 147464 | tf_op jit(solution)/shard_map/ppermute | solution.py:254
  13.2 2.5 %collective-permute-done.3.next_in = bf16[6,32,128]{2,1,0:T(8,128)(2,1)S(1)} collective-permute-done((bf16[6,32,128]{2,1,0:T(8,128)(2,1)S(1)}, bf16[6,32,128]{2,1,0:T(8,128)(2,1)S(1)}, u32[]{:S(2)}, u32[]{:S(2)}) %collective-permute-start.3) | collective-permute-done | bytes 49184 | tf_op jit(solution)/shard_map/ppermute | solution.py:254
  15.8 2.8 %first_step.1 = (f32[60,32,128]{2,1,0:T(8,128)S(1)}, f32[61,32,128]{2,1,0:T(8,128)S(1)}, bf16[12,32,128]{2,1,0:T(8,128)(2,1)S(1)}, bf16[12,32,128]{2,1,0:T(8,128)(2,1)S(1)}) custom-call(s32[5]{0:T(128)S(4)} %get-tuple-element.45.info_ref, s32[128]{0:T(128)S(4)} %get-tuple-element.46.rows_ref, s32[128]{0:T(128)S(4)} %get-tuple-element.47.cols_ref, ...), custom_call_target="tpu_custom_call" | custom-call | flops 268435456 | bytes 1048576 | tf_op jit(solution)/shard_map/first_step/pallas_call | solution.py:274
  18.7 3.1 %collective-permute-start.5 = (bf16[12,32,128]{2,1,0:T(8,128)(2,1)S(1)}, bf16[12,32,128]{2,1,0:T(8,128)(2,1)S(1)}, u32[]{:S(2)}, u32[]{:S(2)}) collective-permute-start(bf16[12,32,128]{2,1,0:T(8,128)(2,1)S(1)} %get-tuple-element.60), channel_id=1, source_target_pairs={{0,1},{1,0},{2,3},{3,2},{4,8},{5,9},{6,10},{7,11},{8,4},{9,5},{10,... | collective-permute-start | bytes 294920 | tf_op jit(solution)/shard_map/ppermute | solution.py:254
  21.8 3.1 %collective-permute-done.5.next_in = bf16[12,32,128]{2,1,0:T(8,128)(2,1)S(1)} collective-permute-done((bf16[12,32,128]{2,1,0:T(8,128)(2,1)S(1)}, bf16[12,32,128]{2,1,0:T(8,128)(2,1)S(1)}, u32[]{:S(2)}, u32[]{:S(2)}) %collective-permute-start.5) | collective-permute-done | bytes 98336 | tf_op jit(solution)/shard_map/ppermute | solution.py:254
  25.0 1.6 %collective-permute-start.6 = (bf16[20,32,128]{2,1,0:T(8,128)(2,1)S(1)}, bf16[20,32,128]{2,1,0:T(8,128)(2,1)S(1)}, u32[]{:S(2)}, u32[]{:S(2)}) collective-permute-start(bf16[20,32,128]{2,1,0:T(8,128)(2,1)S(1)} %get-tuple-element.61), channel_id=1, source_target_pairs={{0,1},{1,2},{2,3},{3,0},{4,5},{5,6},{6,7},{7,4},{8,9},{9,10},{10,1... | collective-permute-start | bytes 491528 | tf_op jit(solution)/shard_map/ppermute | solution.py:254
  26.6 0.5 collective-permute-start.7
  27.1 3.3 %collective-permute-done.6.above_ref = bf16[20,32,128]{2,1,0:T(8,128)(2,1)S(1)} collective-permute-done((bf16[20,32,128]{2,1,0:T(8,128)(2,1)S(1)}, bf16[20,32,128]{2,1,0:T(8,128)(2,1)S(1)}, u32[]{:S(2)}, u32[]{:S(2)}) %collective-permute-start.6) | collective-permute-done | bytes 163872 | tf_op jit(solution)/shard_map/ppermute | solution.py:254
  30.4 1.5 %collective-permute-done.7.below_ref = bf16[20,32,128]{2,1,0:T(8,128)(2,1)S(1)} collective-permute-done((bf16[20,32,128]{2,1,0:T(8,128)(2,1)S(1)}, bf16[20,32,128]{2,1,0:T(8,128)(2,1)S(1)}, u32[]{:S(2)}, u32[]{:S(2)}) %collective-permute-start.7) | collective-permute-done | bytes 163872 | tf_op jit(solution)/shard_map/ppermute | solution.py:254
  31.9 3.0 %one_step.4 = (f32[60,32,128]{2,1,0:T(8,128)S(1)}, f32[61,32,128]{2,1,0:T(8,128)S(1)}, bf16[12,32,128]{2,1,0:T(8,128)(2,1)S(1)}, bf16[12,32,128]{2,1,0:T(8,128)(2,1)S(1)}) custom-call(s32[5]{0:T(128)S(4)} %get-tuple-element.45.info_ref, s32[128]{0:T(128)S(4)} %get-tuple-element.46.rows_ref, s32[128]{0:T(128)S(4)} %get-tuple-element.47.cols_ref, ...), custom_call_target="tpu_custom_call" | custom-call | flops 268435456 | bytes 1048576 | tf_op jit(solution)/shard_map/one_step/pallas_call | solution.py:274
  35.0 2.4 %collective-permute-start.9 = (bf16[12,32,128]{2,1,0:T(8,128)(2,1)S(1)}, bf16[12,32,128]{2,1,0:T(8,128)(2,1)S(1)}, u32[]{:S(2)}, u32[]{:S(2)}) collective-permute-start(bf16[12,32,128]{2,1,0:T(8,128)(2,1)S(1)} %get-tuple-element.66), channel_id=1, source_target_pairs={{0,1},{1,0},{2,3},{3,2},{4,8},{5,9},{6,10},{7,11},{8,4},{9,5},{10,... | collective-permute-start | bytes 294920 | tf_op jit(solution)/shard_map/ppermute | solution.py:254
  37.4 3.8 %collective-permute-done.9.next_in = bf16[12,32,128]{2,1,0:T(8,128)(2,1)S(1)} collective-permute-done((bf16[12,32,128]{2,1,0:T(8,128)(2,1)S(1)}, bf16[12,32,128]{2,1,0:T(8,128)(2,1)S(1)}, u32[]{:S(2)}, u32[]{:S(2)}) %collective-permute-start.9) | collective-permute-done | bytes 98336 | tf_op jit(solution)/shard_map/ppermute | solution.py:254
  41.3 1.2 %collective-permute-start.10 = (bf16[20,32,128]{2,1,0:T(8,128)(2,1)S(1)}, bf16[20,32,128]{2,1,0:T(8,128)(2,1)S(1)}, u32[]{:S(2)}, u32[]{:S(2)}) collective-permute-start(bf16[20,32,128]{2,1,0:T(8,128)(2,1)S(1)} %get-tuple-element.67), channel_id=1, source_target_pairs={{0,1},{1,2},{2,3},{3,0},{4,5},{5,6},{6,7},{7,4},{8,9},{9,10},{10,1... | collective-permute-start | bytes 491528 | tf_op jit(solution)/shard_map/ppermute | solution.py:254
  42.5 0.9 collective-permute-start.11
  43.4 3.3 %collective-permute-done.10.above_ref = bf16[20,32,128]{2,1,0:T(8,128)(2,1)S(1)} collective-permute-done((bf16[20,32,128]{2,1,0:T(8,128)(2,1)S(1)}, bf16[20,32,128]{2,1,0:T(8,128)(2,1)S(1)}, u32[]{:S(2)}, u32[]{:S(2)}) %collective-permute-start.10) | collective-permute-done | bytes 163872 | tf_op jit(solution)/shard_map/ppermute | solution.py:254
  46.7 1.9 %collective-permute-done.11.below_ref = bf16[20,32,128]{2,1,0:T(8,128)(2,1)S(1)} collective-permute-done((bf16[20,32,128]{2,1,0:T(8,128)(2,1)S(1)}, bf16[20,32,128]{2,1,0:T(8,128)(2,1)S(1)}, u32[]{:S(2)}, u32[]{:S(2)}) %collective-permute-start.11) | collective-permute-done | bytes 163872 | tf_op jit(solution)/shard_map/ppermute | solution.py:254
  48.6 3.0 %one_step.5 = (f32[60,32,128]{2,1,0:T(8,128)S(1)}, f32[61,32,128]{2,1,0:T(8,128)S(1)}, bf16[12,32,128]{2,1,0:T(8,128)(2,1)S(1)}, bf16[12,32,128]{2,1,0:T(8,128)(2,1)S(1)}) custom-call(s32[5]{0:T(128)S(4)} %get-tuple-element.45.info_ref, s32[128]{0:T(128)S(4)} %get-tuple-element.46.rows_ref, s32[128]{0:T(128)S(4)} %get-tuple-element.47.cols_ref, ...), custom_call_target="tpu_custom_call" | custom-call | flops 268435456 | bytes 1048576 | tf_op jit(solution)/shard_map/one_step/pallas_call | solution.py:274
  51.7 1.8 %collective-permute-start.13 = (bf16[12,32,128]{2,1,0:T(8,128)(2,1)S(1)}, bf16[12,32,128]{2,1,0:T(8,128)(2,1)S(1)}, u32[]{:S(2)}, u32[]{:S(2)}) collective-permute-start(bf16[12,32,128]{2,1,0:T(8,128)(2,1)S(1)} %get-tuple-element.72), channel_id=1, source_target_pairs={{0,1},{1,0},{2,3},{3,2},{4,8},{5,9},{6,10},{7,11},{8,4},{9,5},{10,... | collective-permute-start | bytes 294920 | tf_op jit(solution)/shard_map/ppermute | solution.py:254
  53.6 4.4 %collective-permute-done.13.next_in = bf16[12,32,128]{2,1,0:T(8,128)(2,1)S(1)} collective-permute-done((bf16[12,32,128]{2,1,0:T(8,128)(2,1)S(1)}, bf16[12,32,128]{2,1,0:T(8,128)(2,1)S(1)}, u32[]{:S(2)}, u32[]{:S(2)}) %collective-permute-start.13) | collective-permute-done | bytes 98336 | tf_op jit(solution)/shard_map/ppermute | solution.py:254
  58.0 2.1 %collective-permute-start.14 = (bf16[20,32,128]{2,1,0:T(8,128)(2,1)S(1)}, bf16[20,32,128]{2,1,0:T(8,128)(2,1)S(1)}, u32[]{:S(2)}, u32[]{:S(2)}) collective-permute-start(bf16[20,32,128]{2,1,0:T(8,128)(2,1)S(1)} %get-tuple-element.73), channel_id=1, source_target_pairs={{0,1},{1,2},{2,3},{3,0},{4,5},{5,6},{6,7},{7,4},{8,9},{9,10},{10,1... | collective-permute-start | bytes 491528 | tf_op jit(solution)/shard_map/ppermute | solution.py:254
  60.1 3.3 %collective-permute-done.14.above_ref = bf16[20,32,128]{2,1,0:T(8,128)(2,1)S(1)} collective-permute-done((bf16[20,32,128]{2,1,0:T(8,128)(2,1)S(1)}, bf16[20,32,128]{2,1,0:T(8,128)(2,1)S(1)}, u32[]{:S(2)}, u32[]{:S(2)}) %collective-permute-start.14) | collective-permute-done | bytes 163872 | tf_op jit(solution)/shard_map/ppermute | solution.py:254
  63.4 2.0 %collective-permute-done.15.below_ref = bf16[20,32,128]{2,1,0:T(8,128)(2,1)S(1)} collective-permute-done((bf16[20,32,128]{2,1,0:T(8,128)(2,1)S(1)}, bf16[20,32,128]{2,1,0:T(8,128)(2,1)S(1)}, u32[]{:S(2)}, u32[]{:S(2)}) %collective-permute-start.15) | collective-permute-done | bytes 163872 | tf_op jit(solution)/shard_map/ppermute | solution.py:254
  65.5 3.0 %one_step.6 = (f32[60,32,128]{2,1,0:T(8,128)S(1)}, f32[61,32,128]{2,1,0:T(8,128)S(1)}, bf16[12,32,128]{2,1,0:T(8,128)(2,1)S(1)}, bf16[12,32,128]{2,1,0:T(8,128)(2,1)S(1)}) custom-call(s32[5]{0:T(128)S(4)} %get-tuple-element.45.info_ref, s32[128]{0:T(128)S(4)} %get-tuple-element.46.rows_ref, s32[128]{0:T(128)S(4)} %get-tuple-element.47.cols_ref, ...), custom_call_target="tpu_custom_call" | custom-call | flops 268435456 | bytes 1048576 | tf_op jit(solution)/shard_map/one_step/pallas_call | solution.py:274
  68.6 1.1 %collective-permute-start.17 = (bf16[12,32,128]{2,1,0:T(8,128)(2,1)S(1)}, bf16[12,32,128]{2,1,0:T(8,128)(2,1)S(1)}, u32[]{:S(2)}, u32[]{:S(2)}) collective-permute-start(bf16[12,32,128]{2,1,0:T(8,128)(2,1)S(1)} %get-tuple-element.78), channel_id=1, source_target_pairs={{0,1},{1,0},{2,3},{3,2},{4,8},{5,9},{6,10},{7,11},{8,4},{9,5},{10,... | collective-permute-start | bytes 294920 | tf_op jit(solution)/shard_map/ppermute | solution.py:254
  69.6 0.2 collective-permute-done.16.pair_in
  69.8 4.9 %collective-permute-done.17.next_in = bf16[12,32,128]{2,1,0:T(8,128)(2,1)S(1)} collective-permute-done((bf16[12,32,128]{2,1,0:T(8,128)(2,1)S(1)}, bf16[12,32,128]{2,1,0:T(8,128)(2,1)S(1)}, u32[]{:S(2)}, u32[]{:S(2)}) %collective-permute-start.17) | collective-permute-done | bytes 98336 | tf_op jit(solution)/shard_map/ppermute | solution.py:254
  74.9 1.5 %collective-permute-start.18 = (bf16[20,32,128]{2,1,0:T(8,128)(2,1)S(1)}, bf16[20,32,128]{2,1,0:T(8,128)(2,1)S(1)}, u32[]{:S(2)}, u32[]{:S(2)}) collective-permute-start(bf16[20,32,128]{2,1,0:T(8,128)(2,1)S(1)} %get-tuple-element.79), channel_id=1, source_target_pairs={{0,1},{1,2},{2,3},{3,0},{4,5},{5,6},{6,7},{7,4},{8,9},{9,10},{10,1... | collective-permute-start | bytes 491528 | tf_op jit(solution)/shard_map/ppermute | solution.py:254
  76.3 0.6 collective-permute-start.19
  77.0 3.3 %collective-permute-done.18.above_ref = bf16[20,32,128]{2,1,0:T(8,128)(2,1)S(1)} collective-permute-done((bf16[20,32,128]{2,1,0:T(8,128)(2,1)S(1)}, bf16[20,32,128]{2,1,0:T(8,128)(2,1)S(1)}, u32[]{:S(2)}, u32[]{:S(2)}) %collective-permute-start.18) | collective-permute-done | bytes 163872 | tf_op jit(solution)/shard_map/ppermute | solution.py:254
  80.2 1.4 %collective-permute-done.19.below_ref = bf16[20,32,128]{2,1,0:T(8,128)(2,1)S(1)} collective-permute-done((bf16[20,32,128]{2,1,0:T(8,128)(2,1)S(1)}, bf16[20,32,128]{2,1,0:T(8,128)(2,1)S(1)}, u32[]{:S(2)}, u32[]{:S(2)}) %collective-permute-start.19) | collective-permute-done | bytes 163872 | tf_op jit(solution)/shard_map/ppermute | solution.py:254
  81.6 3.0 %one_step.7 = (f32[60,32,128]{2,1,0:T(8,128)S(1)}, f32[61,32,128]{2,1,0:T(8,128)S(1)}, bf16[6,32,128]{2,1,0:T(8,128)(2,1)S(1)}, bf16[6,32,128]{2,1,0:T(8,128)(2,1)S(1)}, f32[33,32,128]{2,1,0:T(8,128)S(1)}) custom-call(s32[5]{0:T(128)S(4)} %get-tuple-element.45.info_ref, s32[128]{0:T(128)S(4)} %get-tuple-element.46.rows_ref, ...), custom_call_target="tpu_custom_call" | custom-call | flops 268435456 | bytes 1048576 | tf_op jit(solution)/shard_map/one_step/pallas_call | solution.py:274
  84.7 0.4 collective-permute-start.21
  85.2 0.8 collective-permute-done.20.pair_in
  85.9 4.5 %collective-permute-done.21.next_in = bf16[6,32,128]{2,1,0:T(8,128)(2,1)S(1)} collective-permute-done((bf16[6,32,128]{2,1,0:T(8,128)(2,1)S(1)}, bf16[6,32,128]{2,1,0:T(8,128)(2,1)S(1)}, u32[]{:S(2)}, u32[]{:S(2)}) %collective-permute-start.21) | collective-permute-done | bytes 49184 | tf_op jit(solution)/shard_map/ppermute | solution.py:254
  90.5 1.3 %collective-permute-start.22 = (bf16[8,32,128]{2,1,0:T(8,128)(2,1)S(1)}, bf16[8,32,128]{2,1,0:T(8,128)(2,1)S(1)}, u32[]{:S(2)}, u32[]{:S(2)}) collective-permute-start(bf16[8,32,128]{2,1,0:T(8,128)(2,1)S(1)} %get-tuple-element.85), channel_id=1, source_target_pairs={{0,1},{1,2},{2,3},{3,0},{4,5},{5,6},{6,7},{7,4},{8,9},{9,10},{10,1... | collective-permute-start | bytes 196616 | tf_op jit(solution)/shard_map/ppermute | solution.py:254
  91.8 0.8 collective-permute-start.23
  92.6 0.8 slice.35
  93.4 1.4 %collective-permute-done.22.above_ref = bf16[8,32,128]{2,1,0:T(8,128)(2,1)S(1)} collective-permute-done((bf16[8,32,128]{2,1,0:T(8,128)(2,1)S(1)}, bf16[8,32,128]{2,1,0:T(8,128)(2,1)S(1)}, u32[]{:S(2)}, u32[]{:S(2)}) %collective-permute-start.22) | collective-permute-done | bytes 65568 | tf_op jit(solution)/shard_map/ppermute | solution.py:254
  94.8 1.2 %collective-permute-done.23.below_ref = bf16[8,32,128]{2,1,0:T(8,128)(2,1)S(1)} collective-permute-done((bf16[8,32,128]{2,1,0:T(8,128)(2,1)S(1)}, bf16[8,32,128]{2,1,0:T(8,128)(2,1)S(1)}, u32[]{:S(2)}, u32[]{:S(2)}) %collective-permute-start.23) | collective-permute-done | bytes 65568 | tf_op jit(solution)/shard_map/ppermute | solution.py:254
  96.0 0.9 final_update.1
  (27 shorter events, 0.8 us)
Async XLA Ops:
  0.6 15.1 %copy-start.1 = (f32[4,8,32,128]{3,2,1,0:T(8,128)S(1)}, f32[4,8,32,128]{3,2,1,0:T(8,128)}, u32[]{:S(2)}) copy-start(f32[4,8,32,128]{3,2,1,0:T(8,128)} %param.6) | copy-start | bytes 1572868
  0.6 15.1 %copy-start = (f32[4,8,32,128]{3,2,1,0:T(8,128)S(1)}, f32[4,8,32,128]{3,2,1,0:T(8,128)}, u32[]{:S(2)}) copy-start(f32[4,8,32,128]{3,2,1,0:T(8,128)} %param.7) | copy-start | bytes 1572868
  2.6 7.4 %collective-permute-start = (bf16[8,32,128]{2,1,0:T(8,128)(2,1)S(1)}, bf16[8,32,128]{2,1,0:T(8,128)(2,1)S(1)}, u32[]{:S(2)}, u32[]{:S(2)}) collective-permute-start(bf16[8,32,128]{2,1,0:T(8,128)(2,1)S(1)} %get-tuple-element.48), channel_id=1, source_target_pairs={{0,1},{1,2},{2,3},{3,0},{4,5},{5,6},{6,7},{7,4},{8,9},{9,10},{10,1... | collective-permute-start | bytes 196616 | tf_op jit(solution)/shard_map/ppermute | solution.py:254
  4.2 5.8 %collective-permute-start.1 = (bf16[8,32,128]{2,1,0:T(8,128)(2,1)S(1)}, bf16[8,32,128]{2,1,0:T(8,128)(2,1)S(1)}, u32[]{:S(2)}, u32[]{:S(2)}) collective-permute-start(bf16[8,32,128]{2,1,0:T(8,128)(2,1)S(1)} %get-tuple-element.49), channel_id=1, source_target_pairs={{0,3},{1,0},{2,1},{3,2},{4,7},{5,4},{6,5},{7,6},{8,11},{9,8},{10,9... | collective-permute-start | bytes 196616 | tf_op jit(solution)/shard_map/ppermute | solution.py:254
  5.5 0.7 copy-start.2
  6.1 0.7 copy-start.3
  10.1 5.7 %collective-permute-start.3 = (bf16[6,32,128]{2,1,0:T(8,128)(2,1)S(1)}, bf16[6,32,128]{2,1,0:T(8,128)(2,1)S(1)}, u32[]{:S(2)}, u32[]{:S(2)}) collective-permute-start(bf16[6,32,128]{2,1,0:T(8,128)(2,1)S(1)} %get-tuple-element.92), channel_id=1, source_target_pairs={{0,1},{1,0},{2,3},{3,2},{4,8},{5,9},{6,10},{7,11},{8,4},{9,5},{10,... | collective-permute-start | bytes 147464 | tf_op jit(solution)/shard_map/ppermute | solution.py:254
  13.2 2.5 %collective-permute-start.2 = (bf16[6,32,128]{2,1,0:T(8,128)(2,1)S(1)}, bf16[6,32,128]{2,1,0:T(8,128)(2,1)S(1)}, u32[]{:S(2)}, u32[]{:S(2)}) collective-permute-start(bf16[6,32,128]{2,1,0:T(8,128)(2,1)S(1)} %get-tuple-element.93), channel_id=1, source_target_pairs={{0,4},{1,5},{2,6},{3,7},{4,0},{5,1},{6,2},{7,3},{8,12},{9,13},{10,... | collective-permute-start | bytes 147464 | tf_op jit(solution)/shard_map/ppermute | solution.py:254
  18.6 3.2 %collective-permute-start.4 = (bf16[12,32,128]{2,1,0:T(8,128)(2,1)S(1)}, bf16[12,32,128]{2,1,0:T(8,128)(2,1)S(1)}, u32[]{:S(2)}, u32[]{:S(2)}) collective-permute-start(bf16[12,32,128]{2,1,0:T(8,128)(2,1)S(1)} %get-tuple-element.59), channel_id=1, source_target_pairs={{0,4},{1,5},{2,6},{3,7},{4,0},{5,1},{6,2},{7,3},{8,12},{9,13},{10,... | collective-permute-start | bytes 294920 | tf_op jit(solution)/shard_map/ppermute | solution.py:254
  18.7 6.2 %collective-permute-start.5 = (bf16[12,32,128]{2,1,0:T(8,128)(2,1)S(1)}, bf16[12,32,128]{2,1,0:T(8,128)(2,1)S(1)}, u32[]{:S(2)}, u32[]{:S(2)}) collective-permute-start(bf16[12,32,128]{2,1,0:T(8,128)(2,1)S(1)} %get-tuple-element.60), channel_id=1, source_target_pairs={{0,1},{1,0},{2,3},{3,2},{4,8},{5,9},{6,10},{7,11},{8,4},{9,5},{10,... | collective-permute-start | bytes 294920 | tf_op jit(solution)/shard_map/ppermute | solution.py:254
  25.0 5.4 %collective-permute-start.6 = (bf16[20,32,128]{2,1,0:T(8,128)(2,1)S(1)}, bf16[20,32,128]{2,1,0:T(8,128)(2,1)S(1)}, u32[]{:S(2)}, u32[]{:S(2)}) collective-permute-start(bf16[20,32,128]{2,1,0:T(8,128)(2,1)S(1)} %get-tuple-element.61), channel_id=1, source_target_pairs={{0,1},{1,2},{2,3},{3,0},{4,5},{5,6},{6,7},{7,4},{8,9},{9,10},{10,1... | collective-permute-start | bytes 491528 | tf_op jit(solution)/shard_map/ppermute | solution.py:254
  26.6 5.3 %collective-permute-start.7 = (bf16[20,32,128]{2,1,0:T(8,128)(2,1)S(1)}, bf16[20,32,128]{2,1,0:T(8,128)(2,1)S(1)}, u32[]{:S(2)}, u32[]{:S(2)}) collective-permute-start(bf16[20,32,128]{2,1,0:T(8,128)(2,1)S(1)} %get-tuple-element.62), channel_id=1, source_target_pairs={{0,3},{1,0},{2,1},{3,2},{4,7},{5,4},{6,5},{7,6},{8,11},{9,8},{10,9... | collective-permute-start | bytes 491528 | tf_op jit(solution)/shard_map/ppermute | solution.py:254
  34.9 2.5 %collective-permute-start.8 = (bf16[12,32,128]{2,1,0:T(8,128)(2,1)S(1)}, bf16[12,32,128]{2,1,0:T(8,128)(2,1)S(1)}, u32[]{:S(2)}, u32[]{:S(2)}) collective-permute-start(bf16[12,32,128]{2,1,0:T(8,128)(2,1)S(1)} %get-tuple-element.65), channel_id=1, source_target_pairs={{0,4},{1,5},{2,6},{3,7},{4,0},{5,1},{6,2},{7,3},{8,12},{9,13},{10,... | collective-permute-start | bytes 294920 | tf_op jit(solution)/shard_map/ppermute | solution.py:254
  35.0 6.2 %collective-permute-start.9 = (bf16[12,32,128]{2,1,0:T(8,128)(2,1)S(1)}, bf16[12,32,128]{2,1,0:T(8,128)(2,1)S(1)}, u32[]{:S(2)}, u32[]{:S(2)}) collective-permute-start(bf16[12,32,128]{2,1,0:T(8,128)(2,1)S(1)} %get-tuple-element.66), channel_id=1, source_target_pairs={{0,1},{1,0},{2,3},{3,2},{4,8},{5,9},{6,10},{7,11},{8,4},{9,5},{10,... | collective-permute-start | bytes 294920 | tf_op jit(solution)/shard_map/ppermute | solution.py:254
  41.3 5.4 %collective-permute-start.10 = (bf16[20,32,128]{2,1,0:T(8,128)(2,1)S(1)}, bf16[20,32,128]{2,1,0:T(8,128)(2,1)S(1)}, u32[]{:S(2)}, u32[]{:S(2)}) collective-permute-start(bf16[20,32,128]{2,1,0:T(8,128)(2,1)S(1)} %get-tuple-element.67), channel_id=1, source_target_pairs={{0,1},{1,2},{2,3},{3,0},{4,5},{5,6},{6,7},{7,4},{8,9},{9,10},{10,1... | collective-permute-start | bytes 491528 | tf_op jit(solution)/shard_map/ppermute | solution.py:254
  42.5 6.1 %collective-permute-start.11 = (bf16[20,32,128]{2,1,0:T(8,128)(2,1)S(1)}, bf16[20,32,128]{2,1,0:T(8,128)(2,1)S(1)}, u32[]{:S(2)}, u32[]{:S(2)}) collective-permute-start(bf16[20,32,128]{2,1,0:T(8,128)(2,1)S(1)} %get-tuple-element.68), channel_id=1, source_target_pairs={{0,3},{1,0},{2,1},{3,2},{4,7},{5,4},{6,5},{7,6},{8,11},{9,8},{10,9... | collective-permute-start | bytes 491528 | tf_op jit(solution)/shard_map/ppermute | solution.py:254
  51.6 1.9 %collective-permute-start.12 = (bf16[12,32,128]{2,1,0:T(8,128)(2,1)S(1)}, bf16[12,32,128]{2,1,0:T(8,128)(2,1)S(1)}, u32[]{:S(2)}, u32[]{:S(2)}) collective-permute-start(bf16[12,32,128]{2,1,0:T(8,128)(2,1)S(1)} %get-tuple-element.71), channel_id=1, source_target_pairs={{0,4},{1,5},{2,6},{3,7},{4,0},{5,1},{6,2},{7,3},{8,12},{9,13},{10,... | collective-permute-start | bytes 294920 | tf_op jit(solution)/shard_map/ppermute | solution.py:254
  51.7 6.2 %collective-permute-start.13 = (bf16[12,32,128]{2,1,0:T(8,128)(2,1)S(1)}, bf16[12,32,128]{2,1,0:T(8,128)(2,1)S(1)}, u32[]{:S(2)}, u32[]{:S(2)}) collective-permute-start(bf16[12,32,128]{2,1,0:T(8,128)(2,1)S(1)} %get-tuple-element.72), channel_id=1, source_target_pairs={{0,1},{1,0},{2,3},{3,2},{4,8},{5,9},{6,10},{7,11},{8,4},{9,5},{10,... | collective-permute-start | bytes 294920 | tf_op jit(solution)/shard_map/ppermute | solution.py:254
  58.0 5.4 %collective-permute-start.14 = (bf16[20,32,128]{2,1,0:T(8,128)(2,1)S(1)}, bf16[20,32,128]{2,1,0:T(8,128)(2,1)S(1)}, u32[]{:S(2)}, u32[]{:S(2)}) collective-permute-start(bf16[20,32,128]{2,1,0:T(8,128)(2,1)S(1)} %get-tuple-element.73), channel_id=1, source_target_pairs={{0,1},{1,2},{2,3},{3,0},{4,5},{5,6},{6,7},{7,4},{8,9},{9,10},{10,1... | collective-permute-start | bytes 491528 | tf_op jit(solution)/shard_map/ppermute | solution.py:254
  60.1 5.3 %collective-permute-start.15 = (bf16[20,32,128]{2,1,0:T(8,128)(2,1)S(1)}, bf16[20,32,128]{2,1,0:T(8,128)(2,1)S(1)}, u32[]{:S(2)}, u32[]{:S(2)}) collective-permute-start(bf16[20,32,128]{2,1,0:T(8,128)(2,1)S(1)} %get-tuple-element.74), channel_id=1, source_target_pairs={{0,3},{1,0},{2,1},{3,2},{4,7},{5,4},{6,5},{7,6},{8,11},{9,8},{10,9... | collective-permute-start | bytes 491528 | tf_op jit(solution)/shard_map/ppermute | solution.py:254
  68.5 1.4 %collective-permute-start.16 = (bf16[12,32,128]{2,1,0:T(8,128)(2,1)S(1)}, bf16[12,32,128]{2,1,0:T(8,128)(2,1)S(1)}, u32[]{:S(2)}, u32[]{:S(2)}) collective-permute-start(bf16[12,32,128]{2,1,0:T(8,128)(2,1)S(1)} %get-tuple-element.77), channel_id=1, source_target_pairs={{0,4},{1,5},{2,6},{3,7},{4,0},{5,1},{6,2},{7,3},{8,12},{9,13},{10,... | collective-permute-start | bytes 294920 | tf_op jit(solution)/shard_map/ppermute | solution.py:254
  68.6 6.2 %collective-permute-start.17 = (bf16[12,32,128]{2,1,0:T(8,128)(2,1)S(1)}, bf16[12,32,128]{2,1,0:T(8,128)(2,1)S(1)}, u32[]{:S(2)}, u32[]{:S(2)}) collective-permute-start(bf16[12,32,128]{2,1,0:T(8,128)(2,1)S(1)} %get-tuple-element.78), channel_id=1, source_target_pairs={{0,1},{1,0},{2,3},{3,2},{4,8},{5,9},{6,10},{7,11},{8,4},{9,5},{10,... | collective-permute-start | bytes 294920 | tf_op jit(solution)/shard_map/ppermute | solution.py:254
  74.9 5.4 %collective-permute-start.18 = (bf16[20,32,128]{2,1,0:T(8,128)(2,1)S(1)}, bf16[20,32,128]{2,1,0:T(8,128)(2,1)S(1)}, u32[]{:S(2)}, u32[]{:S(2)}) collective-permute-start(bf16[20,32,128]{2,1,0:T(8,128)(2,1)S(1)} %get-tuple-element.79), channel_id=1, source_target_pairs={{0,1},{1,2},{2,3},{3,0},{4,5},{5,6},{6,7},{7,4},{8,9},{9,10},{10,1... | collective-permute-start | bytes 491528 | tf_op jit(solution)/shard_map/ppermute | solution.py:254
  76.3 5.3 %collective-permute-start.19 = (bf16[20,32,128]{2,1,0:T(8,128)(2,1)S(1)}, bf16[20,32,128]{2,1,0:T(8,128)(2,1)S(1)}, u32[]{:S(2)}, u32[]{:S(2)}) collective-permute-start(bf16[20,32,128]{2,1,0:T(8,128)(2,1)S(1)} %get-tuple-element.80), channel_id=1, source_target_pairs={{0,3},{1,0},{2,1},{3,2},{4,7},{5,4},{6,5},{7,6},{8,11},{9,8},{10,9... | collective-permute-start | bytes 491528 | tf_op jit(solution)/shard_map/ppermute | solution.py:254
  84.6 1.3 %collective-permute-start.20 = (bf16[6,32,128]{2,1,0:T(8,128)(2,1)S(1)}, bf16[6,32,128]{2,1,0:T(8,128)(2,1)S(1)}, u32[]{:S(2)}, u32[]{:S(2)}) collective-permute-start(bf16[6,32,128]{2,1,0:T(8,128)(2,1)S(1)} %get-tuple-element.83), channel_id=1, source_target_pairs={{0,4},{1,5},{2,6},{3,7},{4,0},{5,1},{6,2},{7,3},{8,12},{9,13},{10,... | collective-permute-start | bytes 147464 | tf_op jit(solution)/shard_map/ppermute | solution.py:254
  84.7 5.7 %collective-permute-start.21 = (bf16[6,32,128]{2,1,0:T(8,128)(2,1)S(1)}, bf16[6,32,128]{2,1,0:T(8,128)(2,1)S(1)}, u32[]{:S(2)}, u32[]{:S(2)}) collective-permute-start(bf16[6,32,128]{2,1,0:T(8,128)(2,1)S(1)} %get-tuple-element.84), channel_id=1, source_target_pairs={{0,1},{1,0},{2,3},{3,2},{4,8},{5,9},{6,10},{7,11},{8,4},{9,5},{10,... | collective-permute-start | bytes 147464 | tf_op jit(solution)/shard_map/ppermute | solution.py:254
  90.5 4.3 %collective-permute-start.22 = (bf16[8,32,128]{2,1,0:T(8,128)(2,1)S(1)}, bf16[8,32,128]{2,1,0:T(8,128)(2,1)S(1)}, u32[]{:S(2)}, u32[]{:S(2)}) collective-permute-start(bf16[8,32,128]{2,1,0:T(8,128)(2,1)S(1)} %get-tuple-element.85), channel_id=1, source_target_pairs={{0,1},{1,2},{2,3},{3,0},{4,5},{5,6},{6,7},{7,4},{8,9},{9,10},{10,1... | collective-permute-start | bytes 196616 | tf_op jit(solution)/shard_map/ppermute | solution.py:254
  91.8 4.3 %collective-permute-start.23 = (bf16[8,32,128]{2,1,0:T(8,128)(2,1)S(1)}, bf16[8,32,128]{2,1,0:T(8,128)(2,1)S(1)}, u32[]{:S(2)}, u32[]{:S(2)}) collective-permute-start(bf16[8,32,128]{2,1,0:T(8,128)(2,1)S(1)} %get-tuple-element.86), channel_id=1, source_target_pairs={{0,3},{1,0},{2,1},{3,2},{4,7},{5,4},{6,5},{7,6},{8,11},{9,8},{10,9... | collective-permute-start | bytes 196616 | tf_op jit(solution)/shard_map/ppermute | solution.py:254

commit v3 on v2

--- a/solution.py
+++ b/solution.py
@@ -10,7 +10,7 @@
 ITERS = 5
 descent = 0.1
 
-ROW_FIRST, ROW_LAST, COL_FIRST, COL_LAST, EVEN = range(5)
+ROW_FIRST, ROW_LAST, COL_FIRST, COL_LAST, EVEN, LIVE = range(6)
 
 
 def cast_low(value):
@@ -25,16 +25,25 @@
     return jnp.where(drop, jnp.zeros_like(value), value)
 
 
-def half_step(source_ref, blocks_ref, total_ref, source_ids, target_ids, slots):
-    for slot in range(slots):
-        product = jnp.dot(
-            source_ref[source_ids[slot]], blocks_ref[slot], preferred_element_type=jnp.float32
-        )
-        target = target_ids[slot]
-        total_ref[target] = total_ref[target] + product
-
-
-def products(sizes, rows_ref, cols_ref, observed_ref, blocks_ref, turned_ref, grad_ref, residual_ref, low_ref, rlow_ref):
+def half_step(source_ref, blocks_ref, total_ref, source_ids, target_ids, live, slots):
+    part = slots // 2
+
+    def add(first):
+        for slot in range(first, first + part):
+            product = jnp.dot(
+                source_ref[source_ids[slot]], blocks_ref[slot], preferred_element_type=jnp.float32
+            )
+            target = target_ids[slot]
+            total_ref[target] = total_ref[target] + product
+
+    add(0)
+
+    @pl.when(live > part)
+    def _():
+        add(part)
+
+
+def products(sizes, info_ref, rows_ref, cols_ref, observed_ref, blocks_ref, turned_ref, grad_ref, residual_ref, low_ref, rlow_ref):
     tile_x, tile_y, slots = sizes
     own = tile_x * tile_y
     extended = (tile_x + 2) * (tile_y + 2)
@@ -42,12 +51,12 @@
     for block in range(own):
         residual_ref[block] = -observed_ref[block]
     residual_ref[own] = jnp.zeros_like(residual_ref[own])
-    half_step(low_ref, blocks_ref, residual_ref, cols_ref, rows_ref, slots)
+    half_step(low_ref, blocks_ref, residual_ref, cols_ref, rows_ref, info_ref[LIVE], slots)
     for block in range(own + 1):
         rlow_ref[block] = cast_low(residual_ref[block])
     for block in range(extended + 1):
         grad_ref[block] = jnp.zeros_like(grad_ref[block])
-    half_step(rlow_ref, turned_ref, grad_ref, rows_ref, cols_ref, slots)
+    half_step(rlow_ref, turned_ref, grad_ref, rows_ref, cols_ref, info_ref[LIVE], slots)
 
 
 def send_columns(sizes, last, info_ref, grad_ref, pair_ref, next_ref):
@@ -98,9 +107,27 @@
     return None
 
 
-def prepare_kernel(sizes, chunks, flags_ref, live_ref, rows_in, cols_in, blocks_in, info_ref, rows_ref, cols_ref, blocks_ref, turned_ref, arrived):
+def plan_kernel(sizes, flags_ref, live_ref, rows_in, cols_in, info_ref, rows_ref, cols_ref):
     tile_x, tile_y, slots = sizes
-    size = slots // chunks
+    live = live_ref[0]
+    for place in range(LIVE):
+        info_ref[place] = flags_ref[place]
+    info_ref[LIVE] = live
+    group = 8
+
+    def copy(step, carry):
+        for place in range(group):
+            slot = step * group + place
+            used = slot < live
+            rows_ref[slot] = jnp.where(used, rows_in[slot], tile_x * tile_y)
+            cols_ref[slot] = jnp.where(used, cols_in[slot], (tile_x + 2) * (tile_y + 2))
+        return carry
+
+    lax.fori_loop(0, slots // group, copy, 0)
+
+
+def turn_kernel(chunks, blocks_in, blocks_ref, turned_ref, arrived):
+    size = blocks_in.shape[0] // chunks
 
     def bring(chunk):
         part = pl.ds(chunk * size, size)
@@ -108,17 +135,6 @@
 
     for chunk in range(chunks):
         bring(chunk).start()
-    for place in range(5):
-        info_ref[place] = flags_ref[place]
-    live = live_ref[0]
-
-    def copy(slot, carry):
-        used = slot < live
-        rows_ref[slot] = jnp.where(used, rows_in[slot], tile_x * tile_y)
-        cols_ref[slot] = jnp.where(used, cols_in[slot], (tile_x + 2) * (tile_y + 2))
-        return carry
-
-    lax.fori_loop(0, slots, copy, 0)
     for chunk in range(chunks):
         bring(chunk).wait()
         for place in range(size):
@@ -147,7 +163,7 @@
                 value = kept(value, drop)
             x_ref[row * span + col] = value
             low_ref[row * span + col] = cast_low(value)
-    products(sizes, rows_ref, cols_ref, observed_ref, blocks_ref, turned_ref, grad_ref, residual_ref, low_ref, rlow_ref)
+    products(sizes, info_ref, rows_ref, cols_ref, observed_ref, blocks_ref, turned_ref, grad_ref, residual_ref, low_ref, rlow_ref)
     send_columns(sizes, False, info_ref, grad_ref, pair_ref, next_ref)
 
 
@@ -177,7 +193,7 @@
                 value = kept(value, drop)
             x_ref[at] = value
             low_ref[at] = cast_low(value)
-    products(sizes, rows_ref, cols_ref, observed_ref, blocks_ref, turned_ref, grad_ref, residual_ref, low_ref, rlow_ref)
+    products(sizes, info_ref, rows_ref, cols_ref, observed_ref, blocks_ref, turned_ref, grad_ref, residual_ref, low_ref, rlow_ref)
     send_columns(sizes, last, info_ref, grad_ref, pair_ref, next_ref)
 
 
@@ -297,29 +313,40 @@
         ]
         return outputs + [shape(own + 1, jnp.float32)] if last else outputs
 
-    edges = lax.optimization_barrier(
-        (coefficients[0], coefficients[tile_x - 1], coefficients[:, 0], coefficients[:, tile_y - 1])
-    )
-    top, bottom, left, right = [cast_low(edge) for edge in edges]
-    above, below = along_narrow(top, bottom)
-    chunks = 8
-    info, row_ids, col_ids, matrices, turned = pl.pallas_call(
-        functools.partial(prepare_kernel, sizes, chunks),
-        out_shape=[
-            pltpu.SMEM((5,), jnp.int32),
+    top, bottom = lax.optimization_barrier((coefficients[0], coefficients[tile_x - 1]))
+    above, below = along_narrow(cast_low(top), cast_low(bottom))
+    in_hbm = pltpu.with_memory_space_constraint
+    info, row_ids, col_ids = call(
+        functools.partial(plan_kernel, sizes),
+        "plan_slots",
+        [
+            flags,
+            live_count.reshape(1),
+            in_hbm(block_rows.reshape(slots), pltpu.HBM),
+            in_hbm(block_cols.reshape(slots), pltpu.HBM),
+        ],
+        4,
+        [
+            pltpu.SMEM((LIVE + 1,), jnp.int32),
             pltpu.SMEM((slots,), jnp.int32),
             pltpu.SMEM((slots,), jnp.int32),
-            pltpu.VMEM((slots, width, width), jnp.bfloat16),
-            pltpu.VMEM((slots, width, width), jnp.bfloat16),
         ],
-        in_specs=[smem] * 4 + [pl.BlockSpec(memory_space=pltpu.HBM)],
-        out_specs=[smem] * 3 + [vmem] * 2,
+        flops=work,
+    )
+    chunks = 8
+    matrices, turned = pl.pallas_call(
+        functools.partial(turn_kernel, chunks),
+        out_shape=[pltpu.VMEM((slots, width, width), jnp.bfloat16)] * 2,
+        in_specs=[pl.BlockSpec(memory_space=pltpu.HBM)],
+        out_specs=[vmem] * 2,
         scratch_shapes=[pltpu.SemaphoreType.DMA((chunks,))],
         compiler_params=pltpu.CompilerParams(vmem_limit_bytes=24 << 20),
         cost_estimate=pl.CostEstimate(flops=work, bytes_accessed=12 << 20, transcendentals=0),
-        name="prepare_slots",
-    )(flags, live_count.reshape(1), block_rows.reshape(slots), block_cols.reshape(slots), pltpu.with_memory_space_constraint(blocks.reshape(slots, width, width), pltpu.HBM))
-    above, below, turned = lax.optimization_barrier((above, below, turned))
+        name="turn_blocks",
+    )(in_hbm(blocks.reshape(slots, width, width), pltpu.HBM))
+    above, below, info = lax.optimization_barrier((above, below, info))
+    left, right = lax.optimization_barrier((coefficients[:, 0], coefficients[:, tile_y - 1]))
+    left, right = cast_low(left), cast_low(right)
     sides = []
     for col, edge in ((0, left), (tile_y - 1, right)):
         sides.append(jnp.concatenate([above[col : col + 1], edge, below[col : col + 1]], axis=0))

time: 97.6 us -> 88.4 us (0.906)
  Pallas kernels: 19.2 us -> 13.2 us
  starting transfers between devices: 25 us -> 22.4 us
  local copies, waits for them, and re-layouts: 4.23 us -> 2.9 us
    pallas_call x11 -> x12, Pallas kernels: 16 us -> 10.6 us  [call(): pl.pallas_call(kernel, out_shape=outputs, in_specs=[smem] * scalars + [vm...]
    ppermute x24, starting transfers between devices: 25 us -> 22.4 us  [send(): return lax.ppermute(value, ('wide', 'narrow'), ring)]
    unnamed x8 -> x4, local copies, waits for them, and re-layouts: 1.32 us -> 0.01 us
  transfers between devices with their start and end apart: 24 -> 24, of which waited for: 18 -> 19; matrix products, arithmetic and copies ran while one was open for 1% -> 2% of each run, Pallas kernels for 3% -> 4%
where the time goes in v3:
time: 88.4 us; the launch traced here: 87.7 us
  waiting for transfers between devices  47.7 us (54%)
  starting transfers between devices  22.4 us (25%)
  Pallas kernels  13.2 us (15%)
  local copies, waits for them, and re-layouts  2.9 us (3%)
  between operations  1.46 us (2%)
    ppermute x24, waiting for transfers between devices, send(): return lax.ppermute(value, ('wide', 'narrow'), ring)  47.7 us
    ppermute x24, starting transfers between devices, send(): return lax.ppermute(value, ('wide', 'narrow'), ring)  22.4 us
    pallas_call x12, Pallas kernels, call(): pl.pallas_call(kernel, out_shape=outputs, in_specs=[smem] * scalars + [vm...  10.6 us
    pallas_call x1, Pallas kernels, local(): pl.pallas_call(functools.partial(turn_kernel, chunks), out_shape=[pltpu.V...  2.63 us
  transfers between devices with their start and end apart: 24, of which 19 were waited for; matrix products, arithmetic and copies ran while one was open for 2% of the time, Pallas kernels for 4%

profile of v3, /device:TPU:26, one launch (start us, length us, event | category | flops | bytes accessed | tf_op | source)
XLA Modules:
  0.0 87.7 jit_solution(14941590065555805190)
XLA Ops:
  0.7 1.1 %slice_bitcast_fusion = (bf16[8,32,128]{2,1,0:T(8,128)(2,1)S(1)}, bf16[8,32,128]{2,1,0:T(8,128)(2,1)S(1)}) fusion(f32[4,8,32,128]{3,2,1,0:T(8,128)} %param.6), kind=kLoop, calls=%fused_computation | loop fusion | bytes 262144 | tf_op jit(solution)/shard_map/squeeze | solution.py:316
  1.7 1.6 %collective-permute-start = (bf16[8,32,128]{2,1,0:T(8,128)(2,1)S(1)}, bf16[8,32,128]{2,1,0:T(8,128)(2,1)S(1)}, u32[]{:S(2)}, u32[]{:S(2)}) collective-permute-start(bf16[8,32,128]{2,1,0:T(8,128)(2,1)S(1)} %get-tuple-element.45), channel_id=1, source_target_pairs={{0,1},{1,2},{2,3},{3,0},{4,5},{5,6},{6,7},{7,4},{8,9},{9,10},{10,1... | collective-permute-start | bytes 196616 | tf_op jit(solution)/shard_map/ppermute | solution.py:270
  3.3 0.5 collective-permute-start.1
  3.8 0.9 %slice_bitcast_fusion.2 = (bf16[4,32,128]{2,1,0:T(8,128)(2,1)S(1)}, bf16[4,32,128]{2,1,0:T(8,128)(2,1)S(1)}) fusion(f32[4,8,32,128]{3,2,1,0:T(8,128)} %param.6), kind=kLoop, calls=%fused_computation.2 | loop fusion | bytes 131072 | tf_op jit(solution)/shard_map/squeeze | solution.py:348
  5.5 1.1 %plan_slots.1 = (s32[6]{0:T(128)S(4)}, s32[128]{0:T(128)S(4)}, s32[128]{0:T(128)S(4)}) custom-call(s32[5]{0:T(128)S(1)} %convert_element_type.17.flags_ref, s32[1]{0:T(128)} %bitcast.25.live_ref, s32[128]{0:T(128)} %bitcast.35, s32[128]{0:T(128)} %bitcast.36), custom_call_target="tpu_custom_call" | custom-call | flops 268435456 | bytes 1048576 | tf_op jit(solution)/shard_map/plan_slots/pallas_call | solution.py:290
  6.6 1.0 %collective-permute-done.1.below_ref = bf16[8,32,128]{2,1,0:T(8,128)(2,1)S(1)} collective-permute-done((bf16[8,32,128]{2,1,0:T(8,128)(2,1)S(1)}, bf16[8,32,128]{2,1,0:T(8,128)(2,1)S(1)}, u32[]{:S(2)}, u32[]{:S(2)}) %collective-permute-start.1) | collective-permute-done | bytes 65568 | tf_op jit(solution)/shard_map/ppermute | solution.py:270
  7.6 2.5 %collective-permute-start.3 = (bf16[6,32,128]{2,1,0:T(8,128)(2,1)S(1)}, bf16[6,32,128]{2,1,0:T(8,128)(2,1)S(1)}, u32[]{:S(2)}, u32[]{:S(2)}) collective-permute-start(bf16[6,32,128]{2,1,0:T(8,128)(2,1)S(1)} %get-tuple-element.92), channel_id=1, source_target_pairs={{0,1},{1,0},{2,3},{3,2},{4,8},{5,9},{6,10},{7,11},{8,4},{9,5},{10,... | collective-permute-start | bytes 147464 | tf_op jit(solution)/shard_map/ppermute | solution.py:270
  10.1 2.6 %turn_blocks.1 = (bf16[128,128,128]{2,1,0:T(8,128)(2,1)S(1)}, bf16[128,128,128]{2,1,0:T(8,128)(2,1)S(1)}) custom-call(bf16[128,128,128]{2,1,0:T(8,128)(2,1)} %bitcast.32), custom_call_target="tpu_custom_call" | custom-call | flops 268435456 | bytes 12582912 | tf_op jit(solution)/shard_map/turn_blocks/pallas_call | solution.py:337
  12.8 0.5 collective-permute-done.3.next_in
  13.3 1.6 %first_step.1 = (f32[60,32,128]{2,1,0:T(8,128)S(1)}, f32[61,32,128]{2,1,0:T(8,128)S(1)}, bf16[12,32,128]{2,1,0:T(8,128)(2,1)S(1)}, bf16[12,32,128]{2,1,0:T(8,128)(2,1)S(1)}) custom-call(s32[6]{0:T(128)S(4)} %get-tuple-element.48.info_ref, s32[128]{0:T(128)S(4)} %get-tuple-element.49.rows_ref, s32[128]{0:T(128)S(4)} %get-tuple-element.50.cols_ref, ...), custom_call_target="tpu_custom_call" | custom-call | flops 268435456 | bytes 1048576 | tf_op jit(solution)/shard_map/first_step/pallas_call | solution.py:290
  14.9 0.1 collective-permute-start.4
  15.0 2.5 %collective-permute-start.5 = (bf16[12,32,128]{2,1,0:T(8,128)(2,1)S(1)}, bf16[12,32,128]{2,1,0:T(8,128)(2,1)S(1)}, u32[]{:S(2)}, u32[]{:S(2)}) collective-permute-start(bf16[12,32,128]{2,1,0:T(8,128)(2,1)S(1)} %get-tuple-element.60), channel_id=1, source_target_pairs={{0,1},{1,0},{2,3},{3,2},{4,8},{5,9},{6,10},{7,11},{8,4},{9,5},{10,... | collective-permute-start | bytes 294920 | tf_op jit(solution)/shard_map/ppermute | solution.py:270
  17.5 3.7 %collective-permute-done.5.next_in = bf16[12,32,128]{2,1,0:T(8,128)(2,1)S(1)} collective-permute-done((bf16[12,32,128]{2,1,0:T(8,128)(2,1)S(1)}, bf16[12,32,128]{2,1,0:T(8,128)(2,1)S(1)}, u32[]{:S(2)}, u32[]{:S(2)}) %collective-permute-start.5) | collective-permute-done | bytes 98336 | tf_op jit(solution)/shard_map/ppermute | solution.py:270
  21.3 1.3 %collective-permute-start.6 = (bf16[20,32,128]{2,1,0:T(8,128)(2,1)S(1)}, bf16[20,32,128]{2,1,0:T(8,128)(2,1)S(1)}, u32[]{:S(2)}, u32[]{:S(2)}) collective-permute-start(bf16[20,32,128]{2,1,0:T(8,128)(2,1)S(1)} %get-tuple-element.61), channel_id=1, source_target_pairs={{0,1},{1,2},{2,3},{3,0},{4,5},{5,6},{6,7},{7,4},{8,9},{9,10},{10,1... | collective-permute-start | bytes 491528 | tf_op jit(solution)/shard_map/ppermute | solution.py:270
  22.6 0.8 collective-permute-start.7
  23.4 3.3 %collective-permute-done.6.above_ref = bf16[20,32,128]{2,1,0:T(8,128)(2,1)S(1)} collective-permute-done((bf16[20,32,128]{2,1,0:T(8,128)(2,1)S(1)}, bf16[20,32,128]{2,1,0:T(8,128)(2,1)S(1)}, u32[]{:S(2)}, u32[]{:S(2)}) %collective-permute-start.6) | collective-permute-done | bytes 163872 | tf_op jit(solution)/shard_map/ppermute | solution.py:270
  26.6 1.2 %collective-permute-done.7.below_ref = bf16[20,32,128]{2,1,0:T(8,128)(2,1)S(1)} collective-permute-done((bf16[20,32,128]{2,1,0:T(8,128)(2,1)S(1)}, bf16[20,32,128]{2,1,0:T(8,128)(2,1)S(1)}, u32[]{:S(2)}, u32[]{:S(2)}) %collective-permute-start.7) | collective-permute-done | bytes 163872 | tf_op jit(solution)/shard_map/ppermute | solution.py:270
  27.9 1.7 %one_step.4 = (f32[60,32,128]{2,1,0:T(8,128)S(1)}, f32[61,32,128]{2,1,0:T(8,128)S(1)}, bf16[12,32,128]{2,1,0:T(8,128)(2,1)S(1)}, bf16[12,32,128]{2,1,0:T(8,128)(2,1)S(1)}) custom-call(s32[6]{0:T(128)S(4)} %get-tuple-element.48.info_ref, s32[128]{0:T(128)S(4)} %get-tuple-element.49.rows_ref, s32[128]{0:T(128)S(4)} %get-tuple-element.50.cols_ref, ...), custom_call_target="tpu_custom_call" | custom-call | flops 268435456 | bytes 1048576 | tf_op jit(solution)/shard_map/one_step/pallas_call | solution.py:290
  29.7 1.9 %collective-permute-start.9 = (bf16[12,32,128]{2,1,0:T(8,128)(2,1)S(1)}, bf16[12,32,128]{2,1,0:T(8,128)(2,1)S(1)}, u32[]{:S(2)}, u32[]{:S(2)}) collective-permute-start(bf16[12,32,128]{2,1,0:T(8,128)(2,1)S(1)} %get-tuple-element.66), channel_id=1, source_target_pairs={{0,1},{1,0},{2,3},{3,2},{4,8},{5,9},{6,10},{7,11},{8,4},{9,5},{10,... | collective-permute-start | bytes 294920 | tf_op jit(solution)/shard_map/ppermute | solution.py:270
  31.6 4.3 %collective-permute-done.9.next_in = bf16[12,32,128]{2,1,0:T(8,128)(2,1)S(1)} collective-permute-done((bf16[12,32,128]{2,1,0:T(8,128)(2,1)S(1)}, bf16[12,32,128]{2,1,0:T(8,128)(2,1)S(1)}, u32[]{:S(2)}, u32[]{:S(2)}) %collective-permute-start.9) | collective-permute-done | bytes 98336 | tf_op jit(solution)/shard_map/ppermute | solution.py:270
  36.0 1.7 %collective-permute-start.10 = (bf16[20,32,128]{2,1,0:T(8,128)(2,1)S(1)}, bf16[20,32,128]{2,1,0:T(8,128)(2,1)S(1)}, u32[]{:S(2)}, u32[]{:S(2)}) collective-permute-start(bf16[20,32,128]{2,1,0:T(8,128)(2,1)S(1)} %get-tuple-element.67), channel_id=1, source_target_pairs={{0,1},{1,2},{2,3},{3,0},{4,5},{5,6},{6,7},{7,4},{8,9},{9,10},{10,1... | collective-permute-start | bytes 491528 | tf_op jit(solution)/shard_map/ppermute | solution.py:270
  37.6 0.4 collective-permute-start.11
  38.1 3.3 %collective-permute-done.10.above_ref = bf16[20,32,128]{2,1,0:T(8,128)(2,1)S(1)} collective-permute-done((bf16[20,32,128]{2,1,0:T(8,128)(2,1)S(1)}, bf16[20,32,128]{2,1,0:T(8,128)(2,1)S(1)}, u32[]{:S(2)}, u32[]{:S(2)}) %collective-permute-start.10) | collective-permute-done | bytes 163872 | tf_op jit(solution)/shard_map/ppermute | solution.py:270
  41.4 1.9 %collective-permute-done.11.below_ref = bf16[20,32,128]{2,1,0:T(8,128)(2,1)S(1)} collective-permute-done((bf16[20,32,128]{2,1,0:T(8,128)(2,1)S(1)}, bf16[20,32,128]{2,1,0:T(8,128)(2,1)S(1)}, u32[]{:S(2)}, u32[]{:S(2)}) %collective-permute-start.11) | collective-permute-done | bytes 163872 | tf_op jit(solution)/shard_map/ppermute | solution.py:270
  43.3 1.7 %one_step.5 = (f32[60,32,128]{2,1,0:T(8,128)S(1)}, f32[61,32,128]{2,1,0:T(8,128)S(1)}, bf16[12,32,128]{2,1,0:T(8,128)(2,1)S(1)}, bf16[12,32,128]{2,1,0:T(8,128)(2,1)S(1)}) custom-call(s32[6]{0:T(128)S(4)} %get-tuple-element.48.info_ref, s32[128]{0:T(128)S(4)} %get-tuple-element.49.rows_ref, s32[128]{0:T(128)S(4)} %get-tuple-element.50.cols_ref, ...), custom_call_target="tpu_custom_call" | custom-call | flops 268435456 | bytes 1048576 | tf_op jit(solution)/shard_map/one_step/pallas_call | solution.py:290
  45.1 1.4 %collective-permute-start.13 = (bf16[12,32,128]{2,1,0:T(8,128)(2,1)S(1)}, bf16[12,32,128]{2,1,0:T(8,128)(2,1)S(1)}, u32[]{:S(2)}, u32[]{:S(2)}) collective-permute-start(bf16[12,32,128]{2,1,0:T(8,128)(2,1)S(1)} %get-tuple-element.72), channel_id=1, source_target_pairs={{0,1},{1,0},{2,3},{3,2},{4,8},{5,9},{6,10},{7,11},{8,4},{9,5},{10,... | collective-permute-start | bytes 294920 | tf_op jit(solution)/shard_map/ppermute | solution.py:270
  46.5 4.8 %collective-permute-done.13.next_in = bf16[12,32,128]{2,1,0:T(8,128)(2,1)S(1)} collective-permute-done((bf16[12,32,128]{2,1,0:T(8,128)(2,1)S(1)}, bf16[12,32,128]{2,1,0:T(8,128)(2,1)S(1)}, u32[]{:S(2)}, u32[]{:S(2)}) %collective-permute-start.13) | collective-permute-done | bytes 98336 | tf_op jit(solution)/shard_map/ppermute | solution.py:270
  51.4 2.1 %collective-permute-start.14 = (bf16[20,32,128]{2,1,0:T(8,128)(2,1)S(1)}, bf16[20,32,128]{2,1,0:T(8,128)(2,1)S(1)}, u32[]{:S(2)}, u32[]{:S(2)}) collective-permute-start(bf16[20,32,128]{2,1,0:T(8,128)(2,1)S(1)} %get-tuple-element.73), channel_id=1, source_target_pairs={{0,1},{1,2},{2,3},{3,0},{4,5},{5,6},{6,7},{7,4},{8,9},{9,10},{10,1... | collective-permute-start | bytes 491528 | tf_op jit(solution)/shard_map/ppermute | solution.py:270
  53.4 3.3 %collective-permute-done.14.above_ref = bf16[20,32,128]{2,1,0:T(8,128)(2,1)S(1)} collective-permute-done((bf16[20,32,128]{2,1,0:T(8,128)(2,1)S(1)}, bf16[20,32,128]{2,1,0:T(8,128)(2,1)S(1)}, u32[]{:S(2)}, u32[]{:S(2)}) %collective-permute-start.14) | collective-permute-done | bytes 163872 | tf_op jit(solution)/shard_map/ppermute | solution.py:270
  56.7 2.0 %collective-permute-done.15.below_ref = bf16[20,32,128]{2,1,0:T(8,128)(2,1)S(1)} collective-permute-done((bf16[20,32,128]{2,1,0:T(8,128)(2,1)S(1)}, bf16[20,32,128]{2,1,0:T(8,128)(2,1)S(1)}, u32[]{:S(2)}, u32[]{:S(2)}) %collective-permute-start.15) | collective-permute-done | bytes 163872 | tf_op jit(solution)/shard_map/ppermute | solution.py:270
  58.7 1.7 %one_step.6 = (f32[60,32,128]{2,1,0:T(8,128)S(1)}, f32[61,32,128]{2,1,0:T(8,128)S(1)}, bf16[12,32,128]{2,1,0:T(8,128)(2,1)S(1)}, bf16[12,32,128]{2,1,0:T(8,128)(2,1)S(1)}) custom-call(s32[6]{0:T(128)S(4)} %get-tuple-element.48.info_ref, s32[128]{0:T(128)S(4)} %get-tuple-element.49.rows_ref, s32[128]{0:T(128)S(4)} %get-tuple-element.50.cols_ref, ...), custom_call_target="tpu_custom_call" | custom-call | flops 268435456 | bytes 1048576 | tf_op jit(solution)/shard_map/one_step/pallas_call | solution.py:290
  60.5 0.8 collective-permute-start.17
  61.3 0.5 collective-permute-done.16.pair_in
  61.8 4.9 %collective-permute-done.17.next_in = bf16[12,32,128]{2,1,0:T(8,128)(2,1)S(1)} collective-permute-done((bf16[12,32,128]{2,1,0:T(8,128)(2,1)S(1)}, bf16[12,32,128]{2,1,0:T(8,128)(2,1)S(1)}, u32[]{:S(2)}, u32[]{:S(2)}) %collective-permute-start.17) | collective-permute-done | bytes 98336 | tf_op jit(solution)/shard_map/ppermute | solution.py:270
  66.8 1.5 %collective-permute-start.18 = (bf16[20,32,128]{2,1,0:T(8,128)(2,1)S(1)}, bf16[20,32,128]{2,1,0:T(8,128)(2,1)S(1)}, u32[]{:S(2)}, u32[]{:S(2)}) collective-permute-start(bf16[20,32,128]{2,1,0:T(8,128)(2,1)S(1)} %get-tuple-element.79), channel_id=1, source_target_pairs={{0,1},{1,2},{2,3},{3,0},{4,5},{5,6},{6,7},{7,4},{8,9},{9,10},{10,1... | collective-permute-start | bytes 491528 | tf_op jit(solution)/shard_map/ppermute | solution.py:270
  68.3 0.6 collective-permute-start.19
  68.9 3.3 %collective-permute-done.18.above_ref = bf16[20,32,128]{2,1,0:T(8,128)(2,1)S(1)} collective-permute-done((bf16[20,32,128]{2,1,0:T(8,128)(2,1)S(1)}, bf16[20,32,128]{2,1,0:T(8,128)(2,1)S(1)}, u32[]{:S(2)}, u32[]{:S(2)}) %collective-permute-start.18) | collective-permute-done | bytes 163872 | tf_op jit(solution)/shard_map/ppermute | solution.py:270
  72.2 1.4 %collective-permute-done.19.below_ref = bf16[20,32,128]{2,1,0:T(8,128)(2,1)S(1)} collective-permute-done((bf16[20,32,128]{2,1,0:T(8,128)(2,1)S(1)}, bf16[20,32,128]{2,1,0:T(8,128)(2,1)S(1)}, u32[]{:S(2)}, u32[]{:S(2)}) %collective-permute-start.19) | collective-permute-done | bytes 163872 | tf_op jit(solution)/shard_map/ppermute | solution.py:270
  73.7 1.7 %one_step.7 = (f32[60,32,128]{2,1,0:T(8,128)S(1)}, f32[61,32,128]{2,1,0:T(8,128)S(1)}, bf16[6,32,128]{2,1,0:T(8,128)(2,1)S(1)}, bf16[6,32,128]{2,1,0:T(8,128)(2,1)S(1)}, f32[33,32,128]{2,1,0:T(8,128)S(1)}) custom-call(s32[6]{0:T(128)S(4)} %get-tuple-element.48.info_ref, s32[128]{0:T(128)S(4)} %get-tuple-element.49.rows_ref, ...), custom_call_target="tpu_custom_call" | custom-call | flops 268435456 | bytes 1048576 | tf_op jit(solution)/shard_map/one_step/pallas_call | solution.py:290
  75.4 0.2 collective-permute-start.21
  75.6 1.1 %collective-permute-done.20.pair_in = bf16[6,32,128]{2,1,0:T(8,128)(2,1)S(1)} collective-permute-done((bf16[6,32,128]{2,1,0:T(8,128)(2,1)S(1)}, bf16[6,32,128]{2,1,0:T(8,128)(2,1)S(1)}, u32[]{:S(2)}, u32[]{:S(2)}) %collective-permute-start.20) | collective-permute-done | bytes 49184 | tf_op jit(solution)/shard_map/ppermute | solution.py:270
  76.7 4.5 %collective-permute-done.21.next_in = bf16[6,32,128]{2,1,0:T(8,128)(2,1)S(1)} collective-permute-done((bf16[6,32,128]{2,1,0:T(8,128)(2,1)S(1)}, bf16[6,32,128]{2,1,0:T(8,128)(2,1)S(1)}, u32[]{:S(2)}, u32[]{:S(2)}) %collective-permute-start.21) | collective-permute-done | bytes 49184 | tf_op jit(solution)/shard_map/ppermute | solution.py:270
  81.2 1.3 %collective-permute-start.22 = (bf16[8,32,128]{2,1,0:T(8,128)(2,1)S(1)}, bf16[8,32,128]{2,1,0:T(8,128)(2,1)S(1)}, u32[]{:S(2)}, u32[]{:S(2)}) collective-permute-start(bf16[8,32,128]{2,1,0:T(8,128)(2,1)S(1)} %get-tuple-element.85), channel_id=1, source_target_pairs={{0,1},{1,2},{2,3},{3,0},{4,5},{5,6},{6,7},{7,4},{8,9},{9,10},{10,1... | collective-permute-start | bytes 196616 | tf_op jit(solution)/shard_map/ppermute | solution.py:270
  82.5 0.8 collective-permute-start.23
  83.3 0.8 slice.35
  84.1 1.4 %collective-permute-done.22.above_ref = bf16[8,32,128]{2,1,0:T(8,128)(2,1)S(1)} collective-permute-done((bf16[8,32,128]{2,1,0:T(8,128)(2,1)S(1)}, bf16[8,32,128]{2,1,0:T(8,128)(2,1)S(1)}, u32[]{:S(2)}, u32[]{:S(2)}) %collective-permute-start.22) | collective-permute-done | bytes 65568 | tf_op jit(solution)/shard_map/ppermute | solution.py:270
  85.5 1.3 %collective-permute-done.23.below_ref = bf16[8,32,128]{2,1,0:T(8,128)(2,1)S(1)} collective-permute-done((bf16[8,32,128]{2,1,0:T(8,128)(2,1)S(1)}, bf16[8,32,128]{2,1,0:T(8,128)(2,1)S(1)}, u32[]{:S(2)}, u32[]{:S(2)}) %collective-permute-start.23) | collective-permute-done | bytes 65568 | tf_op jit(solution)/shard_map/ppermute | solution.py:270
  86.8 0.9 %final_update.1 = f32[32,32,128]{2,1,0:T(8,128)} custom-call(s32[6]{0:T(128)S(4)} %get-tuple-element.48.info_ref, f32[60,32,128]{2,1,0:T(8,128)S(1)} %get-tuple-element.81.x_in, f32[61,32,128]{2,1,0:T(8,128)S(1)} %get-tuple-element.82.grad_in, bf16[6,32,128]{2,1,0:T(8,128)(2,1)S(1)} %collective-permute-done.20.pair_in, ...), custom_call_target="tpu_custom_call" | custom-call | bytes 1048576 | tf_op jit(solution)/shard_map/final_update/pallas_call | solution.py:290
  (24 shorter events, 0.8 us)
Async XLA Ops:
  0.6 12.7 %copy-start.1 = (f32[4,8,32,128]{3,2,1,0:T(8,128)S(1)}, f32[4,8,32,128]{3,2,1,0:T(8,128)}, u32[]{:S(2)}) copy-start(f32[4,8,32,128]{3,2,1,0:T(8,128)} %param.6) | copy-start | bytes 1572868
  0.6 12.7 %copy-start = (f32[4,8,32,128]{3,2,1,0:T(8,128)S(1)}, f32[4,8,32,128]{3,2,1,0:T(8,128)}, u32[]{:S(2)}) copy-start(f32[4,8,32,128]{3,2,1,0:T(8,128)} %param.7) | copy-start | bytes 1572868
  1.7 4.9 %collective-permute-start = (bf16[8,32,128]{2,1,0:T(8,128)(2,1)S(1)}, bf16[8,32,128]{2,1,0:T(8,128)(2,1)S(1)}, u32[]{:S(2)}, u32[]{:S(2)}) collective-permute-start(bf16[8,32,128]{2,1,0:T(8,128)(2,1)S(1)} %get-tuple-element.45), channel_id=1, source_target_pairs={{0,1},{1,2},{2,3},{3,0},{4,5},{5,6},{6,7},{7,4},{8,9},{9,10},{10,1... | collective-permute-start | bytes 196616 | tf_op jit(solution)/shard_map/ppermute | solution.py:270
  3.3 4.3 %collective-permute-start.1 = (bf16[8,32,128]{2,1,0:T(8,128)(2,1)S(1)}, bf16[8,32,128]{2,1,0:T(8,128)(2,1)S(1)}, u32[]{:S(2)}, u32[]{:S(2)}) collective-permute-start(bf16[8,32,128]{2,1,0:T(8,128)(2,1)S(1)} %get-tuple-element.46), channel_id=1, source_target_pairs={{0,3},{1,0},{2,1},{3,2},{4,7},{5,4},{6,5},{7,6},{8,11},{9,8},{10,9... | collective-permute-start | bytes 196616 | tf_op jit(solution)/shard_map/ppermute | solution.py:270
  7.6 5.7 %collective-permute-start.3 = (bf16[6,32,128]{2,1,0:T(8,128)(2,1)S(1)}, bf16[6,32,128]{2,1,0:T(8,128)(2,1)S(1)}, u32[]{:S(2)}, u32[]{:S(2)}) collective-permute-start(bf16[6,32,128]{2,1,0:T(8,128)(2,1)S(1)} %get-tuple-element.92), channel_id=1, source_target_pairs={{0,1},{1,0},{2,3},{3,2},{4,8},{5,9},{6,10},{7,11},{8,4},{9,5},{10,... | collective-permute-start | bytes 147464 | tf_op jit(solution)/shard_map/ppermute | solution.py:270
  10.1 3.2 %collective-permute-start.2 = (bf16[6,32,128]{2,1,0:T(8,128)(2,1)S(1)}, bf16[6,32,128]{2,1,0:T(8,128)(2,1)S(1)}, u32[]{:S(2)}, u32[]{:S(2)}) collective-permute-start(bf16[6,32,128]{2,1,0:T(8,128)(2,1)S(1)} %get-tuple-element.93), channel_id=1, source_target_pairs={{0,4},{1,5},{2,6},{3,7},{4,0},{5,1},{6,2},{7,3},{8,12},{9,13},{10,... | collective-permute-start | bytes 147464 | tf_op jit(solution)/shard_map/ppermute | solution.py:270
  14.9 2.6 %collective-permute-start.4 = (bf16[12,32,128]{2,1,0:T(8,128)(2,1)S(1)}, bf16[12,32,128]{2,1,0:T(8,128)(2,1)S(1)}, u32[]{:S(2)}, u32[]{:S(2)}) collective-permute-start(bf16[12,32,128]{2,1,0:T(8,128)(2,1)S(1)} %get-tuple-element.59), channel_id=1, source_target_pairs={{0,4},{1,5},{2,6},{3,7},{4,0},{5,1},{6,2},{7,3},{8,12},{9,13},{10,... | collective-permute-start | bytes 294920 | tf_op jit(solution)/shard_map/ppermute | solution.py:270
  15.0 6.2 %collective-permute-start.5 = (bf16[12,32,128]{2,1,0:T(8,128)(2,1)S(1)}, bf16[12,32,128]{2,1,0:T(8,128)(2,1)S(1)}, u32[]{:S(2)}, u32[]{:S(2)}) collective-permute-start(bf16[12,32,128]{2,1,0:T(8,128)(2,1)S(1)} %get-tuple-element.60), channel_id=1, source_target_pairs={{0,1},{1,0},{2,3},{3,2},{4,8},{5,9},{6,10},{7,11},{8,4},{9,5},{10,... | collective-permute-start | bytes 294920 | tf_op jit(solution)/shard_map/ppermute | solution.py:270
  21.3 5.4 %collective-permute-start.6 = (bf16[20,32,128]{2,1,0:T(8,128)(2,1)S(1)}, bf16[20,32,128]{2,1,0:T(8,128)(2,1)S(1)}, u32[]{:S(2)}, u32[]{:S(2)}) collective-permute-start(bf16[20,32,128]{2,1,0:T(8,128)(2,1)S(1)} %get-tuple-element.61), channel_id=1, source_target_pairs={{0,1},{1,2},{2,3},{3,0},{4,5},{5,6},{6,7},{7,4},{8,9},{9,10},{10,1... | collective-permute-start | bytes 491528 | tf_op jit(solution)/shard_map/ppermute | solution.py:270
  22.6 5.3 %collective-permute-start.7 = (bf16[20,32,128]{2,1,0:T(8,128)(2,1)S(1)}, bf16[20,32,128]{2,1,0:T(8,128)(2,1)S(1)}, u32[]{:S(2)}, u32[]{:S(2)}) collective-permute-start(bf16[20,32,128]{2,1,0:T(8,128)(2,1)S(1)} %get-tuple-element.62), channel_id=1, source_target_pairs={{0,3},{1,0},{2,1},{3,2},{4,7},{5,4},{6,5},{7,6},{8,11},{9,8},{10,9... | collective-permute-start | bytes 491528 | tf_op jit(solution)/shard_map/ppermute | solution.py:270
  29.6 2.0 %collective-permute-start.8 = (bf16[12,32,128]{2,1,0:T(8,128)(2,1)S(1)}, bf16[12,32,128]{2,1,0:T(8,128)(2,1)S(1)}, u32[]{:S(2)}, u32[]{:S(2)}) collective-permute-start(bf16[12,32,128]{2,1,0:T(8,128)(2,1)S(1)} %get-tuple-element.65), channel_id=1, source_target_pairs={{0,4},{1,5},{2,6},{3,7},{4,0},{5,1},{6,2},{7,3},{8,12},{9,13},{10,... | collective-permute-start | bytes 294920 | tf_op jit(solution)/shard_map/ppermute | solution.py:270
  29.7 6.2 %collective-permute-start.9 = (bf16[12,32,128]{2,1,0:T(8,128)(2,1)S(1)}, bf16[12,32,128]{2,1,0:T(8,128)(2,1)S(1)}, u32[]{:S(2)}, u32[]{:S(2)}) collective-permute-start(bf16[12,32,128]{2,1,0:T(8,128)(2,1)S(1)} %get-tuple-element.66), channel_id=1, source_target_pairs={{0,1},{1,0},{2,3},{3,2},{4,8},{5,9},{6,10},{7,11},{8,4},{9,5},{10,... | collective-permute-start | bytes 294920 | tf_op jit(solution)/shard_map/ppermute | solution.py:270
  36.0 5.4 %collective-permute-start.10 = (bf16[20,32,128]{2,1,0:T(8,128)(2,1)S(1)}, bf16[20,32,128]{2,1,0:T(8,128)(2,1)S(1)}, u32[]{:S(2)}, u32[]{:S(2)}) collective-permute-start(bf16[20,32,128]{2,1,0:T(8,128)(2,1)S(1)} %get-tuple-element.67), channel_id=1, source_target_pairs={{0,1},{1,2},{2,3},{3,0},{4,5},{5,6},{6,7},{7,4},{8,9},{9,10},{10,1... | collective-permute-start | bytes 491528 | tf_op jit(solution)/shard_map/ppermute | solution.py:270
  37.6 5.6 %collective-permute-start.11 = (bf16[20,32,128]{2,1,0:T(8,128)(2,1)S(1)}, bf16[20,32,128]{2,1,0:T(8,128)(2,1)S(1)}, u32[]{:S(2)}, u32[]{:S(2)}) collective-permute-start(bf16[20,32,128]{2,1,0:T(8,128)(2,1)S(1)} %get-tuple-element.68), channel_id=1, source_target_pairs={{0,3},{1,0},{2,1},{3,2},{4,7},{5,4},{6,5},{7,6},{8,11},{9,8},{10,9... | collective-permute-start | bytes 491528 | tf_op jit(solution)/shard_map/ppermute | solution.py:270
  45.0 1.5 %collective-permute-start.12 = (bf16[12,32,128]{2,1,0:T(8,128)(2,1)S(1)}, bf16[12,32,128]{2,1,0:T(8,128)(2,1)S(1)}, u32[]{:S(2)}, u32[]{:S(2)}) collective-permute-start(bf16[12,32,128]{2,1,0:T(8,128)(2,1)S(1)} %get-tuple-element.71), channel_id=1, source_target_pairs={{0,4},{1,5},{2,6},{3,7},{4,0},{5,1},{6,2},{7,3},{8,12},{9,13},{10,... | collective-permute-start | bytes 294920 | tf_op jit(solution)/shard_map/ppermute | solution.py:270
  45.1 6.2 %collective-permute-start.13 = (bf16[12,32,128]{2,1,0:T(8,128)(2,1)S(1)}, bf16[12,32,128]{2,1,0:T(8,128)(2,1)S(1)}, u32[]{:S(2)}, u32[]{:S(2)}) collective-permute-start(bf16[12,32,128]{2,1,0:T(8,128)(2,1)S(1)} %get-tuple-element.72), channel_id=1, source_target_pairs={{0,1},{1,0},{2,3},{3,2},{4,8},{5,9},{6,10},{7,11},{8,4},{9,5},{10,... | collective-permute-start | bytes 294920 | tf_op jit(solution)/shard_map/ppermute | solution.py:270
  51.4 5.4 %collective-permute-start.14 = (bf16[20,32,128]{2,1,0:T(8,128)(2,1)S(1)}, bf16[20,32,128]{2,1,0:T(8,128)(2,1)S(1)}, u32[]{:S(2)}, u32[]{:S(2)}) collective-permute-start(bf16[20,32,128]{2,1,0:T(8,128)(2,1)S(1)} %get-tuple-element.73), channel_id=1, source_target_pairs={{0,1},{1,2},{2,3},{3,0},{4,5},{5,6},{6,7},{7,4},{8,9},{9,10},{10,1... | collective-permute-start | bytes 491528 | tf_op jit(solution)/shard_map/ppermute | solution.py:270
  53.4 5.3 %collective-permute-start.15 = (bf16[20,32,128]{2,1,0:T(8,128)(2,1)S(1)}, bf16[20,32,128]{2,1,0:T(8,128)(2,1)S(1)}, u32[]{:S(2)}, u32[]{:S(2)}) collective-permute-start(bf16[20,32,128]{2,1,0:T(8,128)(2,1)S(1)} %get-tuple-element.74), channel_id=1, source_target_pairs={{0,3},{1,0},{2,1},{3,2},{4,7},{5,4},{6,5},{7,6},{8,11},{9,8},{10,9... | collective-permute-start | bytes 491528 | tf_op jit(solution)/shard_map/ppermute | solution.py:270
  60.4 1.4 %collective-permute-start.16 = (bf16[12,32,128]{2,1,0:T(8,128)(2,1)S(1)}, bf16[12,32,128]{2,1,0:T(8,128)(2,1)S(1)}, u32[]{:S(2)}, u32[]{:S(2)}) collective-permute-start(bf16[12,32,128]{2,1,0:T(8,128)(2,1)S(1)} %get-tuple-element.77), channel_id=1, source_target_pairs={{0,4},{1,5},{2,6},{3,7},{4,0},{5,1},{6,2},{7,3},{8,12},{9,13},{10,... | collective-permute-start | bytes 294920 | tf_op jit(solution)/shard_map/ppermute | solution.py:270
  60.5 6.2 %collective-permute-start.17 = (bf16[12,32,128]{2,1,0:T(8,128)(2,1)S(1)}, bf16[12,32,128]{2,1,0:T(8,128)(2,1)S(1)}, u32[]{:S(2)}, u32[]{:S(2)}) collective-permute-start(bf16[12,32,128]{2,1,0:T(8,128)(2,1)S(1)} %get-tuple-element.78), channel_id=1, source_target_pairs={{0,1},{1,0},{2,3},{3,2},{4,8},{5,9},{6,10},{7,11},{8,4},{9,5},{10,... | collective-permute-start | bytes 294920 | tf_op jit(solution)/shard_map/ppermute | solution.py:270
  66.8 5.4 %collective-permute-start.18 = (bf16[20,32,128]{2,1,0:T(8,128)(2,1)S(1)}, bf16[20,32,128]{2,1,0:T(8,128)(2,1)S(1)}, u32[]{:S(2)}, u32[]{:S(2)}) collective-permute-start(bf16[20,32,128]{2,1,0:T(8,128)(2,1)S(1)} %get-tuple-element.79), channel_id=1, source_target_pairs={{0,1},{1,2},{2,3},{3,0},{4,5},{5,6},{6,7},{7,4},{8,9},{9,10},{10,1... | collective-permute-start | bytes 491528 | tf_op jit(solution)/shard_map/ppermute | solution.py:270
  68.3 5.3 %collective-permute-start.19 = (bf16[20,32,128]{2,1,0:T(8,128)(2,1)S(1)}, bf16[20,32,128]{2,1,0:T(8,128)(2,1)S(1)}, u32[]{:S(2)}, u32[]{:S(2)}) collective-permute-start(bf16[20,32,128]{2,1,0:T(8,128)(2,1)S(1)} %get-tuple-element.80), channel_id=1, source_target_pairs={{0,3},{1,0},{2,1},{3,2},{4,7},{5,4},{6,5},{7,6},{8,11},{9,8},{10,9... | collective-permute-start | bytes 491528 | tf_op jit(solution)/shard_map/ppermute | solution.py:270
  75.3 1.3 %collective-permute-start.20 = (bf16[6,32,128]{2,1,0:T(8,128)(2,1)S(1)}, bf16[6,32,128]{2,1,0:T(8,128)(2,1)S(1)}, u32[]{:S(2)}, u32[]{:S(2)}) collective-permute-start(bf16[6,32,128]{2,1,0:T(8,128)(2,1)S(1)} %get-tuple-element.83), channel_id=1, source_target_pairs={{0,4},{1,5},{2,6},{3,7},{4,0},{5,1},{6,2},{7,3},{8,12},{9,13},{10,... | collective-permute-start | bytes 147464 | tf_op jit(solution)/shard_map/ppermute | solution.py:270
  75.4 5.7 %collective-permute-start.21 = (bf16[6,32,128]{2,1,0:T(8,128)(2,1)S(1)}, bf16[6,32,128]{2,1,0:T(8,128)(2,1)S(1)}, u32[]{:S(2)}, u32[]{:S(2)}) collective-permute-start(bf16[6,32,128]{2,1,0:T(8,128)(2,1)S(1)} %get-tuple-element.84), channel_id=1, source_target_pairs={{0,1},{1,0},{2,3},{3,2},{4,8},{5,9},{6,10},{7,11},{8,4},{9,5},{10,... | collective-permute-start | bytes 147464 | tf_op jit(solution)/shard_map/ppermute | solution.py:270
  81.2 4.3 %collective-permute-start.22 = (bf16[8,32,128]{2,1,0:T(8,128)(2,1)S(1)}, bf16[8,32,128]{2,1,0:T(8,128)(2,1)S(1)}, u32[]{:S(2)}, u32[]{:S(2)}) collective-permute-start(bf16[8,32,128]{2,1,0:T(8,128)(2,1)S(1)} %get-tuple-element.85), channel_id=1, source_target_pairs={{0,1},{1,2},{2,3},{3,0},{4,5},{5,6},{6,7},{7,4},{8,9},{9,10},{10,1... | collective-permute-start | bytes 196616 | tf_op jit(solution)/shard_map/ppermute | solution.py:270
  82.5 4.3 %collective-permute-start.23 = (bf16[8,32,128]{2,1,0:T(8,128)(2,1)S(1)}, bf16[8,32,128]{2,1,0:T(8,128)(2,1)S(1)}, u32[]{:S(2)}, u32[]{:S(2)}) collective-permute-start(bf16[8,32,128]{2,1,0:T(8,128)(2,1)S(1)} %get-tuple-element.86), channel_id=1, source_target_pairs={{0,3},{1,0},{2,1},{3,2},{4,7},{5,4},{6,5},{7,6},{8,11},{9,8},{10,9... | collective-permute-start | bytes 196616 | tf_op jit(solution)/shard_map/ppermute | solution.py:270

commit v4 on v3

--- a/solution.py
+++ b/solution.py
@@ -10,7 +10,7 @@
 ITERS = 5
 descent = 0.1
 
-ROW_FIRST, ROW_LAST, COL_FIRST, COL_LAST, EVEN, LIVE = range(6)
+ROW_FIRST, ROW_LAST, COL_FIRST, COL_LAST, EVEN, ROW_EVEN, LIVE = range(7)
 
 
 def cast_low(value):
@@ -142,7 +142,7 @@
             turned_ref[slot] = blocks_ref[slot].T
 
 
-def first_kernel(sizes, info_ref, rows_ref, cols_ref, coef_ref, above_ref, below_ref, pair_in, next_in, observed_ref, blocks_ref, turned_ref, x_ref, grad_ref, pair_ref, next_ref, low_ref, rlow_ref, residual_ref):
+def first_kernel(sizes, info_ref, rows_ref, cols_ref, coef_ref, far_in, near_in, pair_in, next_in, observed_ref, blocks_ref, turned_ref, x_ref, grad_ref, pair_ref, next_ref, low_ref, rlow_ref, residual_ref):
     tile_x, tile_y, _ = sizes
     span = tile_y + 2
     even = info_ref[EVEN] == 1
@@ -153,9 +153,9 @@
             elif col == tile_y + 1:
                 value = wide_value(jnp.where(even, pair_in[row], next_in[row]))
             elif row == 0:
-                value = wide_value(above_ref[col - 1])
+                value = came_along_narrow(info_ref, near_in, far_in, True, col - 1)
             elif row == tile_x + 1:
-                value = wide_value(below_ref[col - 1])
+                value = came_along_narrow(info_ref, near_in, far_in, False, col - 1)
             else:
                 value = coef_ref[(row - 1) * tile_y + col - 1]
             drop = outside(sizes, info_ref, row, col)
@@ -167,15 +167,13 @@
     send_columns(sizes, False, info_ref, grad_ref, pair_ref, next_ref)
 
 
-def step_kernel(sizes, last, info_ref, rows_ref, cols_ref, x_in, grad_in, pair_in, next_in, above_ref, below_ref, observed_ref, blocks_ref, turned_ref, x_ref, grad_ref, pair_ref, next_ref, *rest):
+def step_kernel(sizes, last, info_ref, rows_ref, cols_ref, x_in, grad_in, pair_in, next_in, far_in, near_in, observed_ref, blocks_ref, turned_ref, x_ref, grad_ref, pair_ref, next_ref, *rest):
     tile_x, tile_y, _ = sizes
     span = tile_y + 2
     if last:
         residual_ref, low_ref, rlow_ref = rest
     else:
         low_ref, rlow_ref, residual_ref = rest
-    first = info_ref[ROW_FIRST] == 1
-    final = info_ref[ROW_LAST] == 1
     for row in range(tile_x + 2):
         for col in range(span):
             at = row * span + col
@@ -184,9 +182,9 @@
             if came is not None:
                 gradient = gradient + came
             if row < 2:
-                gradient = gradient + wide_value(kept(above_ref[row * span + col], first))
+                gradient = gradient + came_along_narrow(info_ref, near_in, far_in, True, at)
             elif row >= tile_x:
-                gradient = gradient + wide_value(kept(below_ref[(row - tile_x) * span + col], final))
+                gradient = gradient + came_along_narrow(info_ref, near_in, far_in, False, at - tile_x * span)
             value = x_in[at] - descent * gradient
             drop = outside(sizes, info_ref, row, col)
             if drop is not None:
@@ -197,31 +195,38 @@
     send_columns(sizes, last, info_ref, grad_ref, pair_ref, next_ref)
 
 
-def fold_kernel(sizes, last, info_ref, grad_in, pair_in, next_in, up_ref, down_ref):
-    tile_x, tile_y, _ = sizes
-    span = tile_y + 2
+def came_along_narrow(info_ref, near_in, far_in, upper, at):
+    even = info_ref[ROW_EVEN] == 1
+    from_near = jnp.logical_not(even) if upper else even
+    came = jnp.where(from_near, near_in[at], far_in[at])
+    return wide_value(kept(came, info_ref[ROW_FIRST if upper else ROW_LAST] == 1))
+
+
+def fold_kernel(sizes, last, info_ref, grad_in, pair_in, next_in, far_ref, near_ref):
+    tile_x, tile_y, _ = sizes
+    span = tile_y + 2
+    even = info_ref[ROW_EVEN] == 1
 
     def folded(row, col):
         value = grad_in[row * span + col]
         came = came_along_wide(sizes, last, info_ref, pair_in, next_in, row, col)
         return cast_low(value if came is None else value + came)
 
-    if last:
-        for col in range(1, tile_y + 1):
-            up_ref[col - 1] = folded(0, col)
-            down_ref[col - 1] = folded(tile_x + 1, col)
-    else:
-        for row in range(2):
-            for col in range(span):
-                up_ref[row * span + col] = folded(row, col)
-                down_ref[row * span + col] = folded(tile_x + row, col)
-
-
-def final_kernel(sizes, info_ref, x_in, grad_in, pair_in, next_in, above_ref, below_ref, out_ref):
-    tile_x, tile_y, _ = sizes
-    span = tile_y + 2
-    first = info_ref[ROW_FIRST] == 1
-    final = info_ref[ROW_LAST] == 1
+    for out_ref, lower in ((near_ref, even), (far_ref, jnp.logical_not(even))):
+        if last:
+            row = jnp.where(lower, tile_x + 1, 0)
+            for col in range(1, tile_y + 1):
+                out_ref[col - 1] = folded(row, col)
+        else:
+            row = jnp.where(lower, tile_x, 0)
+            for step in range(2):
+                for col in range(span):
+                    out_ref[step * span + col] = folded(row + step, col)
+
+
+def final_kernel(sizes, info_ref, x_in, grad_in, pair_in, next_in, far_in, near_in, out_ref):
+    tile_x, tile_y, _ = sizes
+    span = tile_y + 2
     for row in range(1, tile_x + 1):
         for col in range(1, tile_y + 1):
             at = row * span + col
@@ -230,9 +235,9 @@
             if came is not None:
                 gradient = gradient + came
             if row == 1:
-                gradient = gradient + wide_value(kept(above_ref[col - 1], first))
+                gradient = gradient + came_along_narrow(info_ref, near_in, far_in, True, col - 1)
             if row == tile_x:
-                gradient = gradient + wide_value(kept(below_ref[col - 1], final))
+                gradient = gradient + came_along_narrow(info_ref, near_in, far_in, False, col - 1)
             out_ref[(row - 1) * tile_y + col - 1] = x_in[at] - descent * gradient
 
 
@@ -247,8 +252,9 @@
     wide = lax.axis_size("wide")
     a = lax.axis_index("narrow")
     b = lax.axis_index("wide")
-    flags = jnp.stack([a == 0, a == narrow - 1, b == 0, b == wide - 1, b % 2 == 0]).astype(jnp.int32)
+    flags = jnp.stack([a == 0, a == narrow - 1, b == 0, b == wide - 1, b % 2 == 0, a % 2 == 0]).astype(jnp.int32)
     even = b % 2 == 0
+    row_even = a % 2 == 0
 
     def everywhere(move):
         return [
@@ -261,16 +267,19 @@
     def other(i, j):
         return (i, j ^ 1) if i in (0, wide - 1) else (((i - 1) ^ 1) + 1, j)
 
-    up_ring = everywhere(lambda i, j: (i, (j - 1) % narrow))
-    down_ring = everywhere(lambda i, j: (i, (j + 1) % narrow))
+    def far(i, j):
+        return (i ^ 1, j) if j in (0, narrow - 1) else (i, ((j - 1) ^ 1) + 1)
+
+    near_pairs = everywhere(lambda i, j: (i, j ^ 1))
+    far_pairs = everywhere(far)
     pairs = everywhere(lambda i, j: (i ^ 1, j))
     others = everywhere(other)
 
     def send(value, ring):
         return lax.ppermute(value, ("wide", "narrow"), ring)
 
-    def along_narrow(up, down):
-        return send(down, down_ring), send(up, up_ring)
+    def along_narrow(far, near):
+        return send(far, far_pairs), send(near, near_pairs)
 
     def along_wide(pair, other):
         return send(pair, pairs), send(other, others)
@@ -314,7 +323,9 @@
         return outputs + [shape(own + 1, jnp.float32)] if last else outputs
 
     top, bottom = lax.optimization_barrier((coefficients[0], coefficients[tile_x - 1]))
-    above, below = along_narrow(cast_low(top), cast_low(bottom))
+    far_row, near = along_narrow(
+        cast_low(jnp.where(row_even, top, bottom)), cast_low(jnp.where(row_even, bottom, top))
+    )
     in_hbm = pltpu.with_memory_space_constraint
     info, row_ids, col_ids = call(
         functools.partial(plan_kernel, sizes),
@@ -344,7 +355,9 @@
         cost_estimate=pl.CostEstimate(flops=work, bytes_accessed=12 << 20, transcendentals=0),
         name="turn_blocks",
     )(in_hbm(blocks.reshape(slots, width, width), pltpu.HBM))
-    above, below, info = lax.optimization_barrier((above, below, info))
+    near, far_row, info = lax.optimization_barrier((near, far_row, info))
+    above = jnp.where(row_even, far_row, near)
+    below = jnp.where(row_even, near, far_row)
     left, right = lax.optimization_barrier((coefficients[:, 0], coefficients[:, tile_y - 1]))
     left, right = cast_low(left), cast_low(right)
     sides = []
@@ -356,7 +369,7 @@
     x, grad, pair_out, next_out = call(
         functools.partial(first_kernel, sizes),
         "first_step",
-        [info, row_ids, col_ids, coefficients.reshape(own, frames, width), above, below, pair_in, next_in, seen, matrices, turned],
+        [info, row_ids, col_ids, coefficients.reshape(own, frames, width), far_row, near, pair_in, next_in, seen, matrices, turned],
         3,
         step_outputs(False),
         [low_scratch, rlow_scratch, residual_scratch],
@@ -366,19 +379,19 @@
         last = iteration == ITERS - 1
         pair_in, next_in = along_wide(pair_out, next_out)
         rows_sent = tile_y if last else 2 * span
-        up, down = call(
+        far_row, near = call(
             functools.partial(fold_kernel, sizes, last),
             "fold_columns",
             [info, grad, pair_in, next_in],
             1,
             [shape(rows_sent, jnp.bfloat16), shape(rows_sent, jnp.bfloat16)],
         )
-        above, below = along_narrow(up, down)
+        far_row, near = along_narrow(far_row, near)
         if last:
             updated = call(
                 functools.partial(final_kernel, sizes),
                 "final_update",
-                [info, x, grad, pair_in, next_in, above, below],
+                [info, x, grad, pair_in, next_in, far_row, near],
                 1,
                 shape(own, jnp.float32),
             )
@@ -387,7 +400,7 @@
             x, grad, pair_out, next_out, *rest = call(
                 functools.partial(step_kernel, sizes, ending),
                 "one_step",
-                [info, row_ids, col_ids, x, grad, pair_in, next_in, above, below, seen, matrices, turned],
+                [info, row_ids, col_ids, x, grad, pair_in, next_in, far_row, near, seen, matrices, turned],
                 3,
                 step_outputs(ending),
                 [low_scratch, rlow_scratch] + ([] if ending else [residual_scratch]),

time: 88.4 us -> 86.7 us (0.981)
  waiting for transfers between devices: 47.7 us -> 42.6 us
  starting transfers between devices: 22.4 us -> 25.6 us
    ppermute x24, waiting for transfers between devices: 47.7 us -> 42.6 us  [send(): return lax.ppermute(value, ('wide', 'narrow'), ring)]
    ppermute x24, starting transfers between devices: 22.4 us -> 25.6 us  [send(): return lax.ppermute(value, ('wide', 'narrow'), ring)]
  transfers between devices with their start and end apart: 24 -> 24, of which waited for: 19 -> 17; matrix products, arithmetic and copies ran while one was open for 2% -> 2% of each run, Pallas kernels for 4% -> 4%
where the time goes in v4:
time: 86.7 us; the launch traced here: 86.2 us
  waiting for transfers between devices  42.6 us (49%)
  starting transfers between devices  25.6 us (30%)
  Pallas kernels  13.6 us (16%)
  local copies, waits for them, and re-layouts  2.9 us (3%)
  between operations  1.49 us (2%)
    ppermute x24, waiting for transfers between devices, send(): return lax.ppermute(value, ('wide', 'narrow'), ring)  42.6 us
    ppermute x24, starting transfers between devices, send(): return lax.ppermute(value, ('wide', 'narrow'), ring)  25.6 us
    pallas_call x12, Pallas kernels, call(): pl.pallas_call(kernel, out_shape=outputs, in_specs=[smem] * scalars + [vm...  11 us
    pallas_call x1, Pallas kernels, local(): pl.pallas_call(functools.partial(turn_kernel, chunks), out_shape=[pltpu.V...  2.63 us
  transfers between devices with their start and end apart: 24, of which 17 were waited for; matrix products, arithmetic and copies ran while one was open for 2% of the time, Pallas kernels for 4%

profile of v4, /device:TPU:26, one launch (start us, length us, event | category | flops | bytes accessed | tf_op | source)
XLA Modules:
  0.0 86.2 jit_solution(18351088370548513190)
XLA Ops:
  0.7 1.1 %slice_bitcast_fusion = (bf16[8,32,128]{2,1,0:T(8,128)(2,1)S(1)}, bf16[8,32,128]{2,1,0:T(8,128)(2,1)S(1)}) fusion(f32[4,8,32,128]{3,2,1,0:T(8,128)} %param.6), kind=kLoop, calls=%fused_computation.2 | loop fusion | bytes 262144 | tf_op jit(solution)/shard_map/squeeze | solution.py:325
  1.8 1.6 %collective-permute-start.1 = (bf16[8,32,128]{2,1,0:T(8,128)(2,1)S(1)}, bf16[8,32,128]{2,1,0:T(8,128)(2,1)S(1)}, u32[]{:S(2)}, u32[]{:S(2)}) collective-permute-start(bf16[8,32,128]{2,1,0:T(8,128)(2,1)S(1)} %get-tuple-element.94), channel_id=1, source_target_pairs={{0,4},{1,2},{2,1},{3,7},{4,0},{5,6},{6,5},{7,3},{8,12},{9,10},{10,... | collective-permute-start | bytes 196616 | tf_op jit(solution)/shard_map/ppermute | solution.py:279
  3.3 0.9 %slice_bitcast_fusion.2 = (bf16[4,32,128]{2,1,0:T(8,128)(2,1)S(1)}, bf16[4,32,128]{2,1,0:T(8,128)(2,1)S(1)}) fusion(f32[4,8,32,128]{3,2,1,0:T(8,128)} %param.6), kind=kLoop, calls=%fused_computation.4 | loop fusion | bytes 131072 | tf_op jit(solution)/shard_map/squeeze | solution.py:361
  4.9 0.1 stack.27
  5.0 1.1 %plan_slots.1 = (s32[7]{0:T(128)S(4)}, s32[128]{0:T(128)S(4)}, s32[128]{0:T(128)S(4)}) custom-call(s32[6]{0:T(128)S(1)} %convert_element_type.17.flags_ref, s32[1]{0:T(128)} %bitcast.26.live_ref, s32[128]{0:T(128)} %bitcast.36, s32[128]{0:T(128)} %bitcast.37), custom_call_target="tpu_custom_call" | custom-call | flops 268435456 | bytes 1048576 | tf_op jit(solution)/shard_map/plan_slots/pallas_call | solution.py:299
  6.1 1.5 %collective-permute-done.near_in = bf16[8,32,128]{2,1,0:T(8,128)(2,1)S(1)} collective-permute-done((bf16[8,32,128]{2,1,0:T(8,128)(2,1)S(1)}, bf16[8,32,128]{2,1,0:T(8,128)(2,1)S(1)}, u32[]{:S(2)}, u32[]{:S(2)}) %collective-permute-start) | collective-permute-done | bytes 65568 | tf_op jit(solution)/shard_map/ppermute | solution.py:279
  7.7 2.5 %collective-permute-start.3 = (bf16[6,32,128]{2,1,0:T(8,128)(2,1)S(1)}, bf16[6,32,128]{2,1,0:T(8,128)(2,1)S(1)}, u32[]{:S(2)}, u32[]{:S(2)}) collective-permute-start(bf16[6,32,128]{2,1,0:T(8,128)(2,1)S(1)} %get-tuple-element.96), channel_id=1, source_target_pairs={{0,1},{1,0},{2,3},{3,2},{4,8},{5,9},{6,10},{7,11},{8,4},{9,5},{10,... | collective-permute-start | bytes 147464 | tf_op jit(solution)/shard_map/ppermute | solution.py:279
  10.2 2.6 %turn_blocks.1 = (bf16[128,128,128]{2,1,0:T(8,128)(2,1)S(1)}, bf16[128,128,128]{2,1,0:T(8,128)(2,1)S(1)}) custom-call(bf16[128,128,128]{2,1,0:T(8,128)(2,1)} %bitcast.33), custom_call_target="tpu_custom_call" | custom-call | flops 268435456 | bytes 12582912 | tf_op jit(solution)/shard_map/turn_blocks/pallas_call | solution.py:348
  12.8 0.5 collective-permute-done.3.next_in
  13.4 1.6 %first_step.1 = (f32[60,32,128]{2,1,0:T(8,128)S(1)}, f32[61,32,128]{2,1,0:T(8,128)S(1)}, bf16[12,32,128]{2,1,0:T(8,128)(2,1)S(1)}, bf16[12,32,128]{2,1,0:T(8,128)(2,1)S(1)}) custom-call(s32[7]{0:T(128)S(4)} %get-tuple-element.48.info_ref, s32[128]{0:T(128)S(4)} %get-tuple-element.49.rows_ref, s32[128]{0:T(128)S(4)} %get-tuple-element.50.cols_ref, ...), custom_call_target="tpu_custom_call" | custom-call | flops 268435456 | bytes 1048576 | tf_op jit(solution)/shard_map/first_step/pallas_call | solution.py:299
  14.9 0.1 collective-permute-start.4
  15.0 2.5 %collective-permute-start.5 = (bf16[12,32,128]{2,1,0:T(8,128)(2,1)S(1)}, bf16[12,32,128]{2,1,0:T(8,128)(2,1)S(1)}, u32[]{:S(2)}, u32[]{:S(2)}) collective-permute-start(bf16[12,32,128]{2,1,0:T(8,128)(2,1)S(1)} %get-tuple-element.60), channel_id=1, source_target_pairs={{0,1},{1,0},{2,3},{3,2},{4,8},{5,9},{6,10},{7,11},{8,4},{9,5},{10,... | collective-permute-start | bytes 294920 | tf_op jit(solution)/shard_map/ppermute | solution.py:279
  17.6 3.7 %collective-permute-done.5.next_in = bf16[12,32,128]{2,1,0:T(8,128)(2,1)S(1)} collective-permute-done((bf16[12,32,128]{2,1,0:T(8,128)(2,1)S(1)}, bf16[12,32,128]{2,1,0:T(8,128)(2,1)S(1)}, u32[]{:S(2)}, u32[]{:S(2)}) %collective-permute-start.5) | collective-permute-done | bytes 98336 | tf_op jit(solution)/shard_map/ppermute | solution.py:279
  21.3 1.4 %collective-permute-start.6 = (bf16[20,32,128]{2,1,0:T(8,128)(2,1)S(1)}, bf16[20,32,128]{2,1,0:T(8,128)(2,1)S(1)}, u32[]{:S(2)}, u32[]{:S(2)}) collective-permute-start(bf16[20,32,128]{2,1,0:T(8,128)(2,1)S(1)} %get-tuple-element.61), channel_id=1, source_target_pairs={{0,4},{1,2},{2,1},{3,7},{4,0},{5,6},{6,5},{7,3},{8,12},{9,10},{10,... | collective-permute-start | bytes 491528 | tf_op jit(solution)/shard_map/ppermute | solution.py:279
  22.7 4.0 %collective-permute-done.6.far_in = bf16[20,32,128]{2,1,0:T(8,128)(2,1)S(1)} collective-permute-done((bf16[20,32,128]{2,1,0:T(8,128)(2,1)S(1)}, bf16[20,32,128]{2,1,0:T(8,128)(2,1)S(1)}, u32[]{:S(2)}, u32[]{:S(2)}) %collective-permute-start.6) | collective-permute-done | bytes 163872 | tf_op jit(solution)/shard_map/ppermute | solution.py:279
  26.7 1.3 %collective-permute-done.7.near_in = bf16[20,32,128]{2,1,0:T(8,128)(2,1)S(1)} collective-permute-done((bf16[20,32,128]{2,1,0:T(8,128)(2,1)S(1)}, bf16[20,32,128]{2,1,0:T(8,128)(2,1)S(1)}, u32[]{:S(2)}, u32[]{:S(2)}) %collective-permute-start.7) | collective-permute-done | bytes 163872 | tf_op jit(solution)/shard_map/ppermute | solution.py:279
  28.0 1.8 %one_step.4 = (f32[60,32,128]{2,1,0:T(8,128)S(1)}, f32[61,32,128]{2,1,0:T(8,128)S(1)}, bf16[12,32,128]{2,1,0:T(8,128)(2,1)S(1)}, bf16[12,32,128]{2,1,0:T(8,128)(2,1)S(1)}) custom-call(s32[7]{0:T(128)S(4)} %get-tuple-element.48.info_ref, s32[128]{0:T(128)S(4)} %get-tuple-element.49.rows_ref, s32[128]{0:T(128)S(4)} %get-tuple-element.50.cols_ref, ...), custom_call_target="tpu_custom_call" | custom-call | flops 268435456 | bytes 1048576 | tf_op jit(solution)/shard_map/one_step/pallas_call | solution.py:299
  29.8 0.1 collective-permute-start.8
  29.9 2.0 %collective-permute-start.9 = (bf16[12,32,128]{2,1,0:T(8,128)(2,1)S(1)}, bf16[12,32,128]{2,1,0:T(8,128)(2,1)S(1)}, u32[]{:S(2)}, u32[]{:S(2)}) collective-permute-start(bf16[12,32,128]{2,1,0:T(8,128)(2,1)S(1)} %get-tuple-element.66), channel_id=1, source_target_pairs={{0,1},{1,0},{2,3},{3,2},{4,8},{5,9},{6,10},{7,11},{8,4},{9,5},{10,... | collective-permute-start | bytes 294920 | tf_op jit(solution)/shard_map/ppermute | solution.py:279
  31.9 4.2 %collective-permute-done.9.next_in = bf16[12,32,128]{2,1,0:T(8,128)(2,1)S(1)} collective-permute-done((bf16[12,32,128]{2,1,0:T(8,128)(2,1)S(1)}, bf16[12,32,128]{2,1,0:T(8,128)(2,1)S(1)}, u32[]{:S(2)}, u32[]{:S(2)}) %collective-permute-start.9) | collective-permute-done | bytes 98336 | tf_op jit(solution)/shard_map/ppermute | solution.py:279
  36.2 0.8 collective-permute-start.10
  37.0 0.5 collective-permute-start.11
  37.5 4.1 %collective-permute-done.10.far_in = bf16[20,32,128]{2,1,0:T(8,128)(2,1)S(1)} collective-permute-done((bf16[20,32,128]{2,1,0:T(8,128)(2,1)S(1)}, bf16[20,32,128]{2,1,0:T(8,128)(2,1)S(1)}, u32[]{:S(2)}, u32[]{:S(2)}) %collective-permute-start.10) | collective-permute-done | bytes 163872 | tf_op jit(solution)/shard_map/ppermute | solution.py:279
  41.6 0.7 collective-permute-done.11.near_in
  42.3 1.9 %one_step.5 = (f32[60,32,128]{2,1,0:T(8,128)S(1)}, f32[61,32,128]{2,1,0:T(8,128)S(1)}, bf16[12,32,128]{2,1,0:T(8,128)(2,1)S(1)}, bf16[12,32,128]{2,1,0:T(8,128)(2,1)S(1)}) custom-call(s32[7]{0:T(128)S(4)} %get-tuple-element.48.info_ref, s32[128]{0:T(128)S(4)} %get-tuple-element.49.rows_ref, s32[128]{0:T(128)S(4)} %get-tuple-element.50.cols_ref, ...), custom_call_target="tpu_custom_call" | custom-call | flops 268435456 | bytes 1048576 | tf_op jit(solution)/shard_map/one_step/pallas_call | solution.py:299
  44.2 0.1 collective-permute-start.12
  44.3 2.8 %collective-permute-start.13 = (bf16[12,32,128]{2,1,0:T(8,128)(2,1)S(1)}, bf16[12,32,128]{2,1,0:T(8,128)(2,1)S(1)}, u32[]{:S(2)}, u32[]{:S(2)}) collective-permute-start(bf16[12,32,128]{2,1,0:T(8,128)(2,1)S(1)} %get-tuple-element.72), channel_id=1, source_target_pairs={{0,1},{1,0},{2,3},{3,2},{4,8},{5,9},{6,10},{7,11},{8,4},{9,5},{10,... | collective-permute-start | bytes 294920 | tf_op jit(solution)/shard_map/ppermute | solution.py:279
  47.1 3.5 %collective-permute-done.13.next_in = bf16[12,32,128]{2,1,0:T(8,128)(2,1)S(1)} collective-permute-done((bf16[12,32,128]{2,1,0:T(8,128)(2,1)S(1)}, bf16[12,32,128]{2,1,0:T(8,128)(2,1)S(1)}, u32[]{:S(2)}, u32[]{:S(2)}) %collective-permute-start.13) | collective-permute-done | bytes 98336 | tf_op jit(solution)/shard_map/ppermute | solution.py:279
  50.6 1.4 %collective-permute-start.14 = (bf16[20,32,128]{2,1,0:T(8,128)(2,1)S(1)}, bf16[20,32,128]{2,1,0:T(8,128)(2,1)S(1)}, u32[]{:S(2)}, u32[]{:S(2)}) collective-permute-start(bf16[20,32,128]{2,1,0:T(8,128)(2,1)S(1)} %get-tuple-element.73), channel_id=1, source_target_pairs={{0,4},{1,2},{2,1},{3,7},{4,0},{5,6},{6,5},{7,3},{8,12},{9,10},{10,... | collective-permute-start | bytes 491528 | tf_op jit(solution)/shard_map/ppermute | solution.py:279
  52.0 0.5 collective-permute-start.15
  52.5 3.5 %collective-permute-done.14.far_in = bf16[20,32,128]{2,1,0:T(8,128)(2,1)S(1)} collective-permute-done((bf16[20,32,128]{2,1,0:T(8,128)(2,1)S(1)}, bf16[20,32,128]{2,1,0:T(8,128)(2,1)S(1)}, u32[]{:S(2)}, u32[]{:S(2)}) %collective-permute-start.14) | collective-permute-done | bytes 163872 | tf_op jit(solution)/shard_map/ppermute | solution.py:279
  56.0 1.3 %collective-permute-done.15.near_in = bf16[20,32,128]{2,1,0:T(8,128)(2,1)S(1)} collective-permute-done((bf16[20,32,128]{2,1,0:T(8,128)(2,1)S(1)}, bf16[20,32,128]{2,1,0:T(8,128)(2,1)S(1)}, u32[]{:S(2)}, u32[]{:S(2)}) %collective-permute-start.15) | collective-permute-done | bytes 163872 | tf_op jit(solution)/shard_map/ppermute | solution.py:279
  57.3 1.8 %one_step.6 = (f32[60,32,128]{2,1,0:T(8,128)S(1)}, f32[61,32,128]{2,1,0:T(8,128)S(1)}, bf16[12,32,128]{2,1,0:T(8,128)(2,1)S(1)}, bf16[12,32,128]{2,1,0:T(8,128)(2,1)S(1)}) custom-call(s32[7]{0:T(128)S(4)} %get-tuple-element.48.info_ref, s32[128]{0:T(128)S(4)} %get-tuple-element.49.rows_ref, s32[128]{0:T(128)S(4)} %get-tuple-element.50.cols_ref, ...), custom_call_target="tpu_custom_call" | custom-call | flops 268435456 | bytes 1048576 | tf_op jit(solution)/shard_map/one_step/pallas_call | solution.py:299
  59.1 2.7 %collective-permute-start.17 = (bf16[12,32,128]{2,1,0:T(8,128)(2,1)S(1)}, bf16[12,32,128]{2,1,0:T(8,128)(2,1)S(1)}, u32[]{:S(2)}, u32[]{:S(2)}) collective-permute-start(bf16[12,32,128]{2,1,0:T(8,128)(2,1)S(1)} %get-tuple-element.78), channel_id=1, source_target_pairs={{0,1},{1,0},{2,3},{3,2},{4,8},{5,9},{6,10},{7,11},{8,4},{9,5},{10,... | collective-permute-start | bytes 294920 | tf_op jit(solution)/shard_map/ppermute | solution.py:279
  61.8 3.5 %collective-permute-done.17.next_in = bf16[12,32,128]{2,1,0:T(8,128)(2,1)S(1)} collective-permute-done((bf16[12,32,128]{2,1,0:T(8,128)(2,1)S(1)}, bf16[12,32,128]{2,1,0:T(8,128)(2,1)S(1)}, u32[]{:S(2)}, u32[]{:S(2)}) %collective-permute-start.17) | collective-permute-done | bytes 98336 | tf_op jit(solution)/shard_map/ppermute | solution.py:279
  65.4 1.3 %collective-permute-start.18 = (bf16[20,32,128]{2,1,0:T(8,128)(2,1)S(1)}, bf16[20,32,128]{2,1,0:T(8,128)(2,1)S(1)}, u32[]{:S(2)}, u32[]{:S(2)}) collective-permute-start(bf16[20,32,128]{2,1,0:T(8,128)(2,1)S(1)} %get-tuple-element.79), channel_id=1, source_target_pairs={{0,4},{1,2},{2,1},{3,7},{4,0},{5,6},{6,5},{7,3},{8,12},{9,10},{10,... | collective-permute-start | bytes 491528 | tf_op jit(solution)/shard_map/ppermute | solution.py:279
  66.7 0.6 collective-permute-start.19
  67.3 3.5 %collective-permute-done.18.far_in = bf16[20,32,128]{2,1,0:T(8,128)(2,1)S(1)} collective-permute-done((bf16[20,32,128]{2,1,0:T(8,128)(2,1)S(1)}, bf16[20,32,128]{2,1,0:T(8,128)(2,1)S(1)}, u32[]{:S(2)}, u32[]{:S(2)}) %collective-permute-start.18) | collective-permute-done | bytes 163872 | tf_op jit(solution)/shard_map/ppermute | solution.py:279
  70.8 1.3 %collective-permute-done.19.near_in = bf16[20,32,128]{2,1,0:T(8,128)(2,1)S(1)} collective-permute-done((bf16[20,32,128]{2,1,0:T(8,128)(2,1)S(1)}, bf16[20,32,128]{2,1,0:T(8,128)(2,1)S(1)}, u32[]{:S(2)}, u32[]{:S(2)}) %collective-permute-start.19) | collective-permute-done | bytes 163872 | tf_op jit(solution)/shard_map/ppermute | solution.py:279
  72.1 1.7 %one_step.7 = (f32[60,32,128]{2,1,0:T(8,128)S(1)}, f32[61,32,128]{2,1,0:T(8,128)S(1)}, bf16[6,32,128]{2,1,0:T(8,128)(2,1)S(1)}, bf16[6,32,128]{2,1,0:T(8,128)(2,1)S(1)}, f32[33,32,128]{2,1,0:T(8,128)S(1)}) custom-call(s32[7]{0:T(128)S(4)} %get-tuple-element.48.info_ref, s32[128]{0:T(128)S(4)} %get-tuple-element.49.rows_ref, ...), custom_call_target="tpu_custom_call" | custom-call | flops 268435456 | bytes 1048576 | tf_op jit(solution)/shard_map/one_step/pallas_call | solution.py:299
  74.0 2.7 %collective-permute-start.21 = (bf16[6,32,128]{2,1,0:T(8,128)(2,1)S(1)}, bf16[6,32,128]{2,1,0:T(8,128)(2,1)S(1)}, u32[]{:S(2)}, u32[]{:S(2)}) collective-permute-start(bf16[6,32,128]{2,1,0:T(8,128)(2,1)S(1)} %get-tuple-element.84), channel_id=1, source_target_pairs={{0,1},{1,0},{2,3},{3,2},{4,8},{5,9},{6,10},{7,11},{8,4},{9,5},{10,... | collective-permute-start | bytes 147464 | tf_op jit(solution)/shard_map/ppermute | solution.py:279
  76.6 3.0 %collective-permute-done.21.next_in = bf16[6,32,128]{2,1,0:T(8,128)(2,1)S(1)} collective-permute-done((bf16[6,32,128]{2,1,0:T(8,128)(2,1)S(1)}, bf16[6,32,128]{2,1,0:T(8,128)(2,1)S(1)}, u32[]{:S(2)}, u32[]{:S(2)}) %collective-permute-start.21) | collective-permute-done | bytes 49184 | tf_op jit(solution)/shard_map/ppermute | solution.py:279
  79.7 1.3 %collective-permute-start.22 = (bf16[8,32,128]{2,1,0:T(8,128)(2,1)S(1)}, bf16[8,32,128]{2,1,0:T(8,128)(2,1)S(1)}, u32[]{:S(2)}, u32[]{:S(2)}) collective-permute-start(bf16[8,32,128]{2,1,0:T(8,128)(2,1)S(1)} %get-tuple-element.85), channel_id=1, source_target_pairs={{0,4},{1,2},{2,1},{3,7},{4,0},{5,6},{6,5},{7,3},{8,12},{9,10},{10,... | collective-permute-start | bytes 196616 | tf_op jit(solution)/shard_map/ppermute | solution.py:279
  81.0 0.6 collective-permute-start.23
  81.6 0.8 slice.35
  82.4 1.6 %collective-permute-done.22.far_in = bf16[8,32,128]{2,1,0:T(8,128)(2,1)S(1)} collective-permute-done((bf16[8,32,128]{2,1,0:T(8,128)(2,1)S(1)}, bf16[8,32,128]{2,1,0:T(8,128)(2,1)S(1)}, u32[]{:S(2)}, u32[]{:S(2)}) %collective-permute-start.22) | collective-permute-done | bytes 65568 | tf_op jit(solution)/shard_map/ppermute | solution.py:279
  84.0 1.3 %collective-permute-done.23.near_in = bf16[8,32,128]{2,1,0:T(8,128)(2,1)S(1)} collective-permute-done((bf16[8,32,128]{2,1,0:T(8,128)(2,1)S(1)}, bf16[8,32,128]{2,1,0:T(8,128)(2,1)S(1)}, u32[]{:S(2)}, u32[]{:S(2)}) %collective-permute-start.23) | collective-permute-done | bytes 65568 | tf_op jit(solution)/shard_map/ppermute | solution.py:279
  85.3 0.9 %final_update.1 = f32[32,32,128]{2,1,0:T(8,128)} custom-call(s32[7]{0:T(128)S(4)} %get-tuple-element.48.info_ref, f32[60,32,128]{2,1,0:T(8,128)S(1)} %get-tuple-element.81.x_in, f32[61,32,128]{2,1,0:T(8,128)S(1)} %get-tuple-element.82.grad_in, bf16[6,32,128]{2,1,0:T(8,128)(2,1)S(1)} %collective-permute-done.20.pair_in, ...), custom_call_target="tpu_custom_call" | custom-call | bytes 1048576 | tf_op jit(solution)/shard_map/final_update/pallas_call | solution.py:299
  (26 shorter events, 0.5 us)
Async XLA Ops:
  0.6 12.7 %copy-start.1 = (f32[4,8,32,128]{3,2,1,0:T(8,128)S(1)}, f32[4,8,32,128]{3,2,1,0:T(8,128)}, u32[]{:S(2)}) copy-start(f32[4,8,32,128]{3,2,1,0:T(8,128)} %param.6) | copy-start | bytes 1572868
  0.6 12.7 %copy-start = (f32[4,8,32,128]{3,2,1,0:T(8,128)S(1)}, f32[4,8,32,128]{3,2,1,0:T(8,128)}, u32[]{:S(2)}) copy-start(f32[4,8,32,128]{3,2,1,0:T(8,128)} %param.7) | copy-start | bytes 1572868
  1.8 4.3 %collective-permute-start.1 = (bf16[8,32,128]{2,1,0:T(8,128)(2,1)S(1)}, bf16[8,32,128]{2,1,0:T(8,128)(2,1)S(1)}, u32[]{:S(2)}, u32[]{:S(2)}) collective-permute-start(bf16[8,32,128]{2,1,0:T(8,128)(2,1)S(1)} %get-tuple-element.94), channel_id=1, source_target_pairs={{0,4},{1,2},{2,1},{3,7},{4,0},{5,6},{6,5},{7,3},{8,12},{9,10},{10,... | collective-permute-start | bytes 196616 | tf_op jit(solution)/shard_map/ppermute | solution.py:279
  3.3 4.3 %collective-permute-start = (bf16[8,32,128]{2,1,0:T(8,128)(2,1)S(1)}, bf16[8,32,128]{2,1,0:T(8,128)(2,1)S(1)}, u32[]{:S(2)}, u32[]{:S(2)}) collective-permute-start(bf16[8,32,128]{2,1,0:T(8,128)(2,1)S(1)} %get-tuple-element.95), channel_id=1, source_target_pairs={{0,1},{1,0},{2,3},{3,2},{4,5},{5,4},{6,7},{7,6},{8,9},{9,8},{10,11... | collective-permute-start | bytes 196616 | tf_op jit(solution)/shard_map/ppermute | solution.py:279
  7.7 5.7 %collective-permute-start.3 = (bf16[6,32,128]{2,1,0:T(8,128)(2,1)S(1)}, bf16[6,32,128]{2,1,0:T(8,128)(2,1)S(1)}, u32[]{:S(2)}, u32[]{:S(2)}) collective-permute-start(bf16[6,32,128]{2,1,0:T(8,128)(2,1)S(1)} %get-tuple-element.96), channel_id=1, source_target_pairs={{0,1},{1,0},{2,3},{3,2},{4,8},{5,9},{6,10},{7,11},{8,4},{9,5},{10,... | collective-permute-start | bytes 147464 | tf_op jit(solution)/shard_map/ppermute | solution.py:279
  10.2 3.2 %collective-permute-start.2 = (bf16[6,32,128]{2,1,0:T(8,128)(2,1)S(1)}, bf16[6,32,128]{2,1,0:T(8,128)(2,1)S(1)}, u32[]{:S(2)}, u32[]{:S(2)}) collective-permute-start(bf16[6,32,128]{2,1,0:T(8,128)(2,1)S(1)} %get-tuple-element.97), channel_id=1, source_target_pairs={{0,4},{1,5},{2,6},{3,7},{4,0},{5,1},{6,2},{7,3},{8,12},{9,13},{10,... | collective-permute-start | bytes 147464 | tf_op jit(solution)/shard_map/ppermute | solution.py:279
  14.9 2.6 %collective-permute-start.4 = (bf16[12,32,128]{2,1,0:T(8,128)(2,1)S(1)}, bf16[12,32,128]{2,1,0:T(8,128)(2,1)S(1)}, u32[]{:S(2)}, u32[]{:S(2)}) collective-permute-start(bf16[12,32,128]{2,1,0:T(8,128)(2,1)S(1)} %get-tuple-element.59), channel_id=1, source_target_pairs={{0,4},{1,5},{2,6},{3,7},{4,0},{5,1},{6,2},{7,3},{8,12},{9,13},{10,... | collective-permute-start | bytes 294920 | tf_op jit(solution)/shard_map/ppermute | solution.py:279
  15.0 6.2 %collective-permute-start.5 = (bf16[12,32,128]{2,1,0:T(8,128)(2,1)S(1)}, bf16[12,32,128]{2,1,0:T(8,128)(2,1)S(1)}, u32[]{:S(2)}, u32[]{:S(2)}) collective-permute-start(bf16[12,32,128]{2,1,0:T(8,128)(2,1)S(1)} %get-tuple-element.60), channel_id=1, source_target_pairs={{0,1},{1,0},{2,3},{3,2},{4,8},{5,9},{6,10},{7,11},{8,4},{9,5},{10,... | collective-permute-start | bytes 294920 | tf_op jit(solution)/shard_map/ppermute | solution.py:279
  21.3 5.4 %collective-permute-start.6 = (bf16[20,32,128]{2,1,0:T(8,128)(2,1)S(1)}, bf16[20,32,128]{2,1,0:T(8,128)(2,1)S(1)}, u32[]{:S(2)}, u32[]{:S(2)}) collective-permute-start(bf16[20,32,128]{2,1,0:T(8,128)(2,1)S(1)} %get-tuple-element.61), channel_id=1, source_target_pairs={{0,4},{1,2},{2,1},{3,7},{4,0},{5,6},{6,5},{7,3},{8,12},{9,10},{10,... | collective-permute-start | bytes 491528 | tf_op jit(solution)/shard_map/ppermute | solution.py:279
  22.7 5.3 %collective-permute-start.7 = (bf16[20,32,128]{2,1,0:T(8,128)(2,1)S(1)}, bf16[20,32,128]{2,1,0:T(8,128)(2,1)S(1)}, u32[]{:S(2)}, u32[]{:S(2)}) collective-permute-start(bf16[20,32,128]{2,1,0:T(8,128)(2,1)S(1)} %get-tuple-element.62), channel_id=1, source_target_pairs={{0,1},{1,0},{2,3},{3,2},{4,5},{5,4},{6,7},{7,6},{8,9},{9,8},{10,11... | collective-permute-start | bytes 491528 | tf_op jit(solution)/shard_map/ppermute | solution.py:279
  29.8 2.1 %collective-permute-start.8 = (bf16[12,32,128]{2,1,0:T(8,128)(2,1)S(1)}, bf16[12,32,128]{2,1,0:T(8,128)(2,1)S(1)}, u32[]{:S(2)}, u32[]{:S(2)}) collective-permute-start(bf16[12,32,128]{2,1,0:T(8,128)(2,1)S(1)} %get-tuple-element.65), channel_id=1, source_target_pairs={{0,4},{1,5},{2,6},{3,7},{4,0},{5,1},{6,2},{7,3},{8,12},{9,13},{10,... | collective-permute-start | bytes 294920 | tf_op jit(solution)/shard_map/ppermute | solution.py:279
  29.9 6.2 %collective-permute-start.9 = (bf16[12,32,128]{2,1,0:T(8,128)(2,1)S(1)}, bf16[12,32,128]{2,1,0:T(8,128)(2,1)S(1)}, u32[]{:S(2)}, u32[]{:S(2)}) collective-permute-start(bf16[12,32,128]{2,1,0:T(8,128)(2,1)S(1)} %get-tuple-element.66), channel_id=1, source_target_pairs={{0,1},{1,0},{2,3},{3,2},{4,8},{5,9},{6,10},{7,11},{8,4},{9,5},{10,... | collective-permute-start | bytes 294920 | tf_op jit(solution)/shard_map/ppermute | solution.py:279
  36.2 5.4 %collective-permute-start.10 = (bf16[20,32,128]{2,1,0:T(8,128)(2,1)S(1)}, bf16[20,32,128]{2,1,0:T(8,128)(2,1)S(1)}, u32[]{:S(2)}, u32[]{:S(2)}) collective-permute-start(bf16[20,32,128]{2,1,0:T(8,128)(2,1)S(1)} %get-tuple-element.67), channel_id=1, source_target_pairs={{0,4},{1,2},{2,1},{3,7},{4,0},{5,6},{6,5},{7,3},{8,12},{9,10},{10,... | collective-permute-start | bytes 491528 | tf_op jit(solution)/shard_map/ppermute | solution.py:279
  37.0 5.3 %collective-permute-start.11 = (bf16[20,32,128]{2,1,0:T(8,128)(2,1)S(1)}, bf16[20,32,128]{2,1,0:T(8,128)(2,1)S(1)}, u32[]{:S(2)}, u32[]{:S(2)}) collective-permute-start(bf16[20,32,128]{2,1,0:T(8,128)(2,1)S(1)} %get-tuple-element.68), channel_id=1, source_target_pairs={{0,1},{1,0},{2,3},{3,2},{4,5},{5,4},{6,7},{7,6},{8,9},{9,8},{10,11... | collective-permute-start | bytes 491528 | tf_op jit(solution)/shard_map/ppermute | solution.py:279
  44.2 2.9 %collective-permute-start.12 = (bf16[12,32,128]{2,1,0:T(8,128)(2,1)S(1)}, bf16[12,32,128]{2,1,0:T(8,128)(2,1)S(1)}, u32[]{:S(2)}, u32[]{:S(2)}) collective-permute-start(bf16[12,32,128]{2,1,0:T(8,128)(2,1)S(1)} %get-tuple-element.71), channel_id=1, source_target_pairs={{0,4},{1,5},{2,6},{3,7},{4,0},{5,1},{6,2},{7,3},{8,12},{9,13},{10,... | collective-permute-start | bytes 294920 | tf_op jit(solution)/shard_map/ppermute | solution.py:279
  44.3 6.2 %collective-permute-start.13 = (bf16[12,32,128]{2,1,0:T(8,128)(2,1)S(1)}, bf16[12,32,128]{2,1,0:T(8,128)(2,1)S(1)}, u32[]{:S(2)}, u32[]{:S(2)}) collective-permute-start(bf16[12,32,128]{2,1,0:T(8,128)(2,1)S(1)} %get-tuple-element.72), channel_id=1, source_target_pairs={{0,1},{1,0},{2,3},{3,2},{4,8},{5,9},{6,10},{7,11},{8,4},{9,5},{10,... | collective-permute-start | bytes 294920 | tf_op jit(solution)/shard_map/ppermute | solution.py:279
  50.6 5.4 %collective-permute-start.14 = (bf16[20,32,128]{2,1,0:T(8,128)(2,1)S(1)}, bf16[20,32,128]{2,1,0:T(8,128)(2,1)S(1)}, u32[]{:S(2)}, u32[]{:S(2)}) collective-permute-start(bf16[20,32,128]{2,1,0:T(8,128)(2,1)S(1)} %get-tuple-element.73), channel_id=1, source_target_pairs={{0,4},{1,2},{2,1},{3,7},{4,0},{5,6},{6,5},{7,3},{8,12},{9,10},{10,... | collective-permute-start | bytes 491528 | tf_op jit(solution)/shard_map/ppermute | solution.py:279
  52.0 5.3 %collective-permute-start.15 = (bf16[20,32,128]{2,1,0:T(8,128)(2,1)S(1)}, bf16[20,32,128]{2,1,0:T(8,128)(2,1)S(1)}, u32[]{:S(2)}, u32[]{:S(2)}) collective-permute-start(bf16[20,32,128]{2,1,0:T(8,128)(2,1)S(1)} %get-tuple-element.74), channel_id=1, source_target_pairs={{0,1},{1,0},{2,3},{3,2},{4,5},{5,4},{6,7},{7,6},{8,9},{9,8},{10,11... | collective-permute-start | bytes 491528 | tf_op jit(solution)/shard_map/ppermute | solution.py:279
  59.1 2.8 %collective-permute-start.16 = (bf16[12,32,128]{2,1,0:T(8,128)(2,1)S(1)}, bf16[12,32,128]{2,1,0:T(8,128)(2,1)S(1)}, u32[]{:S(2)}, u32[]{:S(2)}) collective-permute-start(bf16[12,32,128]{2,1,0:T(8,128)(2,1)S(1)} %get-tuple-element.77), channel_id=1, source_target_pairs={{0,4},{1,5},{2,6},{3,7},{4,0},{5,1},{6,2},{7,3},{8,12},{9,13},{10,... | collective-permute-start | bytes 294920 | tf_op jit(solution)/shard_map/ppermute | solution.py:279
  59.1 6.2 %collective-permute-start.17 = (bf16[12,32,128]{2,1,0:T(8,128)(2,1)S(1)}, bf16[12,32,128]{2,1,0:T(8,128)(2,1)S(1)}, u32[]{:S(2)}, u32[]{:S(2)}) collective-permute-start(bf16[12,32,128]{2,1,0:T(8,128)(2,1)S(1)} %get-tuple-element.78), channel_id=1, source_target_pairs={{0,1},{1,0},{2,3},{3,2},{4,8},{5,9},{6,10},{7,11},{8,4},{9,5},{10,... | collective-permute-start | bytes 294920 | tf_op jit(solution)/shard_map/ppermute | solution.py:279
  65.4 5.4 %collective-permute-start.18 = (bf16[20,32,128]{2,1,0:T(8,128)(2,1)S(1)}, bf16[20,32,128]{2,1,0:T(8,128)(2,1)S(1)}, u32[]{:S(2)}, u32[]{:S(2)}) collective-permute-start(bf16[20,32,128]{2,1,0:T(8,128)(2,1)S(1)} %get-tuple-element.79), channel_id=1, source_target_pairs={{0,4},{1,2},{2,1},{3,7},{4,0},{5,6},{6,5},{7,3},{8,12},{9,10},{10,... | collective-permute-start | bytes 491528 | tf_op jit(solution)/shard_map/ppermute | solution.py:279
  66.7 5.4 %collective-permute-start.19 = (bf16[20,32,128]{2,1,0:T(8,128)(2,1)S(1)}, bf16[20,32,128]{2,1,0:T(8,128)(2,1)S(1)}, u32[]{:S(2)}, u32[]{:S(2)}) collective-permute-start(bf16[20,32,128]{2,1,0:T(8,128)(2,1)S(1)} %get-tuple-element.80), channel_id=1, source_target_pairs={{0,1},{1,0},{2,3},{3,2},{4,5},{5,4},{6,7},{7,6},{8,9},{9,8},{10,11... | collective-permute-start | bytes 491528 | tf_op jit(solution)/shard_map/ppermute | solution.py:279
  73.9 2.8 %collective-permute-start.20 = (bf16[6,32,128]{2,1,0:T(8,128)(2,1)S(1)}, bf16[6,32,128]{2,1,0:T(8,128)(2,1)S(1)}, u32[]{:S(2)}, u32[]{:S(2)}) collective-permute-start(bf16[6,32,128]{2,1,0:T(8,128)(2,1)S(1)} %get-tuple-element.83), channel_id=1, source_target_pairs={{0,4},{1,5},{2,6},{3,7},{4,0},{5,1},{6,2},{7,3},{8,12},{9,13},{10,... | collective-permute-start | bytes 147464 | tf_op jit(solution)/shard_map/ppermute | solution.py:279
  74.0 5.7 %collective-permute-start.21 = (bf16[6,32,128]{2,1,0:T(8,128)(2,1)S(1)}, bf16[6,32,128]{2,1,0:T(8,128)(2,1)S(1)}, u32[]{:S(2)}, u32[]{:S(2)}) collective-permute-start(bf16[6,32,128]{2,1,0:T(8,128)(2,1)S(1)} %get-tuple-element.84), channel_id=1, source_target_pairs={{0,1},{1,0},{2,3},{3,2},{4,8},{5,9},{6,10},{7,11},{8,4},{9,5},{10,... | collective-permute-start | bytes 147464 | tf_op jit(solution)/shard_map/ppermute | solution.py:279
  79.7 4.3 %collective-permute-start.22 = (bf16[8,32,128]{2,1,0:T(8,128)(2,1)S(1)}, bf16[8,32,128]{2,1,0:T(8,128)(2,1)S(1)}, u32[]{:S(2)}, u32[]{:S(2)}) collective-permute-start(bf16[8,32,128]{2,1,0:T(8,128)(2,1)S(1)} %get-tuple-element.85), channel_id=1, source_target_pairs={{0,4},{1,2},{2,1},{3,7},{4,0},{5,6},{6,5},{7,3},{8,12},{9,10},{10,... | collective-permute-start | bytes 196616 | tf_op jit(solution)/shard_map/ppermute | solution.py:279
  81.0 4.3 %collective-permute-start.23 = (bf16[8,32,128]{2,1,0:T(8,128)(2,1)S(1)}, bf16[8,32,128]{2,1,0:T(8,128)(2,1)S(1)}, u32[]{:S(2)}, u32[]{:S(2)}) collective-permute-start(bf16[8,32,128]{2,1,0:T(8,128)(2,1)S(1)} %get-tuple-element.86), channel_id=1, source_target_pairs={{0,1},{1,0},{2,3},{3,2},{4,5},{5,4},{6,7},{7,6},{8,9},{9,8},{10,11... | collective-permute-start | bytes 196616 | tf_op jit(solution)/shard_map/ppermute | solution.py:279

commit v5 on v4

--- a/solution.py
+++ b/solution.py
@@ -25,38 +25,48 @@
     return jnp.where(drop, jnp.zeros_like(value), value)
 
 
-def half_step(source_ref, blocks_ref, total_ref, source_ids, target_ids, live, slots):
-    part = slots // 2
-
-    def add(first):
-        for slot in range(first, first + part):
-            product = jnp.dot(
-                source_ref[source_ids[slot]], blocks_ref[slot], preferred_element_type=jnp.float32
+def half_step(source_ref, blocks, total_ref, source_ids, target_ids, live):
+    def add(first, blocks_ref):
+        for at in range(0, blocks_ref.shape[0], 2):
+            slot = first + at
+            upper = source_ref[source_ids[slot]]
+            lower = source_ref[source_ids[slot + 1]]
+            frames, width = upper.shape
+            zeros = jnp.zeros_like(upper)
+            taken = jnp.concatenate(
+                [jnp.concatenate([upper, zeros], axis=1), jnp.concatenate([zeros, lower], axis=1)],
+                axis=0,
             )
+            matrices = blocks_ref[pl.ds(at, 2)].reshape(2 * width, width)
+            product = jnp.dot(taken, matrices, preferred_element_type=jnp.float32)
             target = target_ids[slot]
-            total_ref[target] = total_ref[target] + product
-
-    add(0)
-
-    @pl.when(live > part)
+            total_ref[target] = total_ref[target] + product[:frames]
+            target = target_ids[slot + 1]
+            total_ref[target] = total_ref[target] + product[frames:]
+
+    first_ref, second_ref = blocks
+    half = first_ref.shape[0]
+    add(0, first_ref)
+
+    @pl.when(live > half)
     def _():
-        add(part)
-
-
-def products(sizes, info_ref, rows_ref, cols_ref, observed_ref, blocks_ref, turned_ref, grad_ref, residual_ref, low_ref, rlow_ref):
-    tile_x, tile_y, slots = sizes
+        add(half, second_ref)
+
+
+def products(sizes, info_ref, rows_ref, cols_ref, observed_ref, blocks, turned, grad_ref, residual_ref, low_ref, rlow_ref):
+    tile_x, tile_y, _ = sizes
     own = tile_x * tile_y
     extended = (tile_x + 2) * (tile_y + 2)
     low_ref[extended] = jnp.zeros_like(low_ref[extended])
     for block in range(own):
         residual_ref[block] = -observed_ref[block]
     residual_ref[own] = jnp.zeros_like(residual_ref[own])
-    half_step(low_ref, blocks_ref, residual_ref, cols_ref, rows_ref, info_ref[LIVE], slots)
+    half_step(low_ref, blocks, residual_ref, cols_ref, rows_ref, info_ref[LIVE])
     for block in range(own + 1):
         rlow_ref[block] = cast_low(residual_ref[block])
     for block in range(extended + 1):
         grad_ref[block] = jnp.zeros_like(grad_ref[block])
-    half_step(rlow_ref, turned_ref, grad_ref, rows_ref, cols_ref, info_ref[LIVE], slots)
+    half_step(rlow_ref, turned, grad_ref, rows_ref, cols_ref, info_ref[LIVE])
 
 
 def send_columns(sizes, last, info_ref, grad_ref, pair_ref, next_ref):
@@ -107,8 +117,19 @@
     return None
 
 
-def plan_kernel(sizes, flags_ref, live_ref, rows_in, cols_in, info_ref, rows_ref, cols_ref):
+def bring(blocks_in, blocks_ref, arrived, chunk, first):
+    size = blocks_ref.shape[0] // arrived.shape[0]
+    return pltpu.make_async_copy(
+        blocks_in.at[pl.ds(first + chunk * size, size)],
+        blocks_ref.at[pl.ds(chunk * size, size)],
+        arrived.at[chunk],
+    )
+
+
+def plan_kernel(sizes, flags_ref, live_ref, rows_in, cols_in, blocks_in, info_ref, rows_ref, cols_ref, first_blocks, arrived):
     tile_x, tile_y, slots = sizes
+    for chunk in range(arrived.shape[0]):
+        bring(blocks_in, first_blocks, arrived, chunk, 0).start()
     live = live_ref[0]
     for place in range(LIVE):
         info_ref[place] = flags_ref[place]
@@ -124,25 +145,32 @@
         return carry
 
     lax.fori_loop(0, slots // group, copy, 0)
-
-
-def turn_kernel(chunks, blocks_in, blocks_ref, turned_ref, arrived):
-    size = blocks_in.shape[0] // chunks
-
-    def bring(chunk):
-        part = pl.ds(chunk * size, size)
-        return pltpu.make_async_copy(blocks_in.at[part], blocks_ref.at[part], arrived.at[chunk])
-
-    for chunk in range(chunks):
-        bring(chunk).start()
-    for chunk in range(chunks):
-        bring(chunk).wait()
-        for place in range(size):
-            slot = chunk * size + place
-            turned_ref[slot] = blocks_ref[slot].T
-
-
-def first_kernel(sizes, info_ref, rows_ref, cols_ref, coef_ref, far_in, near_in, pair_in, next_in, observed_ref, blocks_ref, turned_ref, x_ref, grad_ref, pair_ref, next_ref, low_ref, rlow_ref, residual_ref):
+    for chunk in range(arrived.shape[0]):
+        bring(blocks_in, first_blocks, arrived, chunk, 0).wait()
+
+
+def turn_kernel(info_ref, first_blocks, blocks_in, first_turned, second_blocks, second_turned, arrived):
+    half = first_blocks.shape[0]
+    more = info_ref[LIVE] > half
+
+    @pl.when(more)
+    def _():
+        for chunk in range(arrived.shape[0]):
+            bring(blocks_in, second_blocks, arrived, chunk, half).start()
+
+    for slot in range(half):
+        first_turned[slot] = first_blocks[slot].T
+
+    @pl.when(more)
+    def _():
+        size = half // arrived.shape[0]
+        for chunk in range(arrived.shape[0]):
+            bring(blocks_in, second_blocks, arrived, chunk, half).wait()
+            for slot in range(chunk * size, (chunk + 1) * size):
+                second_turned[slot] = second_blocks[slot].T
+
+
+def first_kernel(sizes, info_ref, rows_ref, cols_ref, coef_ref, far_in, near_in, pair_in, next_in, observed_ref, first_blocks, second_blocks, first_turned, second_turned, x_ref, grad_ref, pair_ref, next_ref, low_ref, rlow_ref, residual_ref):
     tile_x, tile_y, _ = sizes
     span = tile_y + 2
     even = info_ref[EVEN] == 1
@@ -163,11 +191,11 @@
                 value = kept(value, drop)
             x_ref[row * span + col] = value
             low_ref[row * span + col] = cast_low(value)
-    products(sizes, info_ref, rows_ref, cols_ref, observed_ref, blocks_ref, turned_ref, grad_ref, residual_ref, low_ref, rlow_ref)
+    products(sizes, info_ref, rows_ref, cols_ref, observed_ref, (first_blocks, second_blocks), (first_turned, second_turned), grad_ref, residual_ref, low_ref, rlow_ref)
     send_columns(sizes, False, info_ref, grad_ref, pair_ref, next_ref)
 
 
-def step_kernel(sizes, last, info_ref, rows_ref, cols_ref, x_in, grad_in, pair_in, next_in, far_in, near_in, observed_ref, blocks_ref, turned_ref, x_ref, grad_ref, pair_ref, next_ref, *rest):
+def step_kernel(sizes, last, info_ref, rows_ref, cols_ref, x_in, grad_in, pair_in, next_in, far_in, near_in, observed_ref, first_blocks, second_blocks, first_turned, second_turned, x_ref, grad_ref, pair_ref, next_ref, *rest):
     tile_x, tile_y, _ = sizes
     span = tile_y + 2
     if last:
@@ -191,7 +219,7 @@
                 value = kept(value, drop)
             x_ref[at] = value
             low_ref[at] = cast_low(value)
-    products(sizes, info_ref, rows_ref, cols_ref, observed_ref, blocks_ref, turned_ref, grad_ref, residual_ref, low_ref, rlow_ref)
+    products(sizes, info_ref, rows_ref, cols_ref, observed_ref, (first_blocks, second_blocks), (first_turned, second_turned), grad_ref, residual_ref, low_ref, rlow_ref)
     send_columns(sizes, last, info_ref, grad_ref, pair_ref, next_ref)
 
 
@@ -327,34 +355,44 @@
         cast_low(jnp.where(row_even, top, bottom)), cast_low(jnp.where(row_even, bottom, top))
     )
     in_hbm = pltpu.with_memory_space_constraint
-    info, row_ids, col_ids = call(
+    chunks = 4
+    half = slots // 2
+    stay = pl.BlockSpec(memory_space=pltpu.HBM)
+    matrices = in_hbm(blocks.reshape(slots, width, width), pltpu.HBM)
+    half_shape = pltpu.VMEM((half, width, width), jnp.bfloat16)
+    options = dict(
+        scratch_shapes=[pltpu.SemaphoreType.DMA((chunks,))],
+        compiler_params=pltpu.CompilerParams(vmem_limit_bytes=24 << 20),
+        cost_estimate=pl.CostEstimate(flops=work, bytes_accessed=4 << 20, transcendentals=0),
+    )
+    info, row_ids, col_ids, first_blocks = pl.pallas_call(
         functools.partial(plan_kernel, sizes),
-        "plan_slots",
-        [
-            flags,
-            live_count.reshape(1),
-            in_hbm(block_rows.reshape(slots), pltpu.HBM),
-            in_hbm(block_cols.reshape(slots), pltpu.HBM),
-        ],
-        4,
-        [
+        out_shape=[
             pltpu.SMEM((LIVE + 1,), jnp.int32),
             pltpu.SMEM((slots,), jnp.int32),
             pltpu.SMEM((slots,), jnp.int32),
+            half_shape,
         ],
-        flops=work,
-    )
-    chunks = 8
-    matrices, turned = pl.pallas_call(
-        functools.partial(turn_kernel, chunks),
-        out_shape=[pltpu.VMEM((slots, width, width), jnp.bfloat16)] * 2,
-        in_specs=[pl.BlockSpec(memory_space=pltpu.HBM)],
-        out_specs=[vmem] * 2,
-        scratch_shapes=[pltpu.SemaphoreType.DMA((chunks,))],
-        compiler_params=pltpu.CompilerParams(vmem_limit_bytes=24 << 20),
-        cost_estimate=pl.CostEstimate(flops=work, bytes_accessed=12 << 20, transcendentals=0),
+        in_specs=[smem] * 4 + [stay],
+        out_specs=[smem] * 3 + [vmem],
+        name="plan_slots",
+        **options,
+    )(
+        flags,
+        live_count.reshape(1),
+        in_hbm(block_rows.reshape(slots), pltpu.HBM),
+        in_hbm(block_cols.reshape(slots), pltpu.HBM),
+        matrices,
+    )
+    first_turned, second_blocks, second_turned = pl.pallas_call(
+        turn_kernel,
+        out_shape=[half_shape] * 3,
+        in_specs=[smem, vmem, stay],
+        out_specs=[vmem] * 3,
         name="turn_blocks",
-    )(in_hbm(blocks.reshape(slots, width, width), pltpu.HBM))
+        **options,
+    )(info, first_blocks, matrices)
+    operator = [first_blocks, second_blocks, first_turned, second_turned]
     near, far_row, info = lax.optimization_barrier((near, far_row, info))
     above = jnp.where(row_even, far_row, near)
     below = jnp.where(row_even, near, far_row)
@@ -363,13 +401,14 @@
     sides = []
     for col, edge in ((0, left), (tile_y - 1, right)):
         sides.append(jnp.concatenate([above[col : col + 1], edge, below[col : col + 1]], axis=0))
-    pair_in, next_in = along_wide(
-        jnp.where(even, sides[1], sides[0]), jnp.where(even, sides[0], sides[1])
-    )
+    pair_out, next_out = lax.optimization_barrier(
+        (jnp.where(even, sides[1], sides[0]), jnp.where(even, sides[0], sides[1]))
+    )
+    pair_in, next_in = along_wide(pair_out, next_out)
     x, grad, pair_out, next_out = call(
         functools.partial(first_kernel, sizes),
         "first_step",
-        [info, row_ids, col_ids, coefficients.reshape(own, frames, width), far_row, near, pair_in, next_in, seen, matrices, turned],
+        [info, row_ids, col_ids, coefficients.reshape(own, frames, width), far_row, near, pair_in, next_in, seen, *operator],
         3,
         step_outputs(False),
         [low_scratch, rlow_scratch, residual_scratch],
@@ -400,7 +439,7 @@
             x, grad, pair_out, next_out, *rest = call(
                 functools.partial(step_kernel, sizes, ending),
                 "one_step",
-                [info, row_ids, col_ids, x, grad, pair_in, next_in, far_row, near, seen, matrices, turned],
+                [info, row_ids, col_ids, x, grad, pair_in, next_in, far_row, near, seen, *operator],
                 3,
                 step_outputs(ending),
                 [low_scratch, rlow_scratch] + ([] if ending else [residual_scratch]),

time: 86.7 us -> 86.9 us (level)
  starting transfers between devices: 25.6 us -> 34.4 us
  waiting for transfers between devices: 42.6 us -> 36 us
  Pallas kernels: 13.6 us -> 11.6 us
    ppermute x24, starting transfers between devices: 25.6 us -> 34.4 us  [send(): return lax.ppermute(value, ('wide', 'narrow'), ring)]
    ppermute x24, waiting for transfers between devices: 42.6 us -> 36 us  [send(): return lax.ppermute(value, ('wide', 'narrow'), ring)]
    pallas_call x12 -> x11, Pallas kernels: 11 us -> 8.75 us  [call(): pl.pallas_call(kernel, out_shape=outputs, in_specs=[smem] * scalars + [vm...]
    pallas_call x1 -> x2, Pallas kernels: 2.63 us -> 2.86 us  [the longest x1 2.23 us: local(): pl.pallas_call(functools.partial(plan_kernel, sizes), out_shape=[pltpu.SM...]
  transfers between devices with their start and end apart: 24 -> 24, of which waited for: 17 -> 17; matrix products, arithmetic and copies ran while one was open for 2% -> 2% of each run, Pallas kernels for 4% -> 3%
where the time goes in v5:
time: 86.9 us; the launch traced here: 86.5 us
  waiting for transfers between devices  36 us (41%)
  starting transfers between devices  34.4 us (40%)
  Pallas kernels  11.6 us (13%)
  local copies, waits for them, and re-layouts  2.82 us (3%)
  between operations  1.51 us (2%)
    ppermute x24, waiting for transfers between devices, send(): return lax.ppermute(value, ('wide', 'narrow'), ring)  36 us
    ppermute x24, starting transfers between devices, send(): return lax.ppermute(value, ('wide', 'narrow'), ring)  34.4 us
    pallas_call x11, Pallas kernels, call(): pl.pallas_call(kernel, out_shape=outputs, in_specs=[smem] * scalars + [vm...  8.75 us
    pallas_call x1, Pallas kernels, local(): pl.pallas_call(functools.partial(plan_kernel, sizes), out_shape=[pltpu.SM...  2.23 us
  transfers between devices with their start and end apart: 24, of which 17 were waited for; matrix products, arithmetic and copies ran while one was open for 2% of the time, Pallas kernels for 3%

profile of v5, /device:TPU:26, one launch (start us, length us, event | category | flops | bytes accessed | tf_op | source)
XLA Modules:
  0.0 86.5 jit_solution(11135270198879820103)
XLA Ops:
  0.6 1.0 %slice_bitcast_fusion = (bf16[8,32,128]{2,1,0:T(8,128)(2,1)S(1)}, bf16[8,32,128]{2,1,0:T(8,128)(2,1)S(1)}) fusion(f32[4,8,32,128]{3,2,1,0:T(8,128)} %param.6), kind=kLoop, calls=%fused_computation.2 | loop fusion | bytes 262144 | tf_op jit(solution)/shard_map/squeeze | solution.py:353
  1.7 1.6 %collective-permute-start.1 = (bf16[8,32,128]{2,1,0:T(8,128)(2,1)S(1)}, bf16[8,32,128]{2,1,0:T(8,128)(2,1)S(1)}, u32[]{:S(2)}, u32[]{:S(2)}) collective-permute-start(bf16[8,32,128]{2,1,0:T(8,128)(2,1)S(1)} %get-tuple-element.102), channel_id=1, source_target_pairs={{0,4},{1,2},{2,1},{3,7},{4,0},{5,6},{6,5},{7,3},{8,12},{9,10},{10,... | collective-permute-start | bytes 196616 | tf_op jit(solution)/shard_map/ppermute | solution.py:307
  3.2 0.9 %slice_bitcast_fusion.2 = (bf16[4,32,128]{2,1,0:T(8,128)(2,1)S(1)}, bf16[4,32,128]{2,1,0:T(8,128)(2,1)S(1)}) fusion(f32[4,8,32,128]{3,2,1,0:T(8,128)} %param.6), kind=kLoop, calls=%fused_computation.4 | loop fusion | bytes 131072 | tf_op jit(solution)/shard_map/squeeze | solution.py:399
  4.8 0.1 stack.27
  4.9 2.2 %plan_slots.1 = (s32[7]{0:T(128)S(4)}, s32[128]{0:T(128)S(4)}, s32[128]{0:T(128)S(4)}, bf16[64,128,128]{2,1,0:T(8,128)(2,1)S(1)}) custom-call(s32[6]{0:T(128)S(1)} %convert_element_type.17.flags_ref, s32[1]{0:T(128)} %bitcast.26.live_ref, s32[128]{0:T(128)} %bitcast.37, s32[128]{0:T(128)} %bitcast.38, bf16[128,128,128]{2,1,0:T(8,128)(2,1)} %bitcast.33), custom_call_target="tpu_custom_call" | custom-call | flops 268435456 | bytes 4194304 | tf_op jit(solution)/shard_map/plan_slots/pallas_call | solution.py:368
  7.2 0.3 collective-permute-done.near_in
  7.6 0.1 collective-permute-start.2
  7.6 4.3 %collective-permute-start.3 = (bf16[6,32,128]{2,1,0:T(8,128)(2,1)S(1)}, bf16[6,32,128]{2,1,0:T(8,128)(2,1)S(1)}, u32[]{:S(2)}, u32[]{:S(2)}) collective-permute-start(bf16[6,32,128]{2,1,0:T(8,128)(2,1)S(1)} %get-tuple-element.60), channel_id=1, source_target_pairs={{0,1},{1,0},{2,3},{3,2},{4,8},{5,9},{6,10},{7,11},{8,4},{9,5},{10,... | collective-permute-start | bytes 147464 | tf_op jit(solution)/shard_map/ppermute | solution.py:307
  12.0 0.6 turn_blocks.1
  12.6 1.1 %collective-permute-done.3.next_in = bf16[6,32,128]{2,1,0:T(8,128)(2,1)S(1)} collective-permute-done((bf16[6,32,128]{2,1,0:T(8,128)(2,1)S(1)}, bf16[6,32,128]{2,1,0:T(8,128)(2,1)S(1)}, u32[]{:S(2)}, u32[]{:S(2)}) %collective-permute-start.3) | collective-permute-done | bytes 49184 | tf_op jit(solution)/shard_map/ppermute | solution.py:307
  13.7 1.4 %first_step.1 = (f32[60,32,128]{2,1,0:T(8,128)S(1)}, f32[61,32,128]{2,1,0:T(8,128)S(1)}, bf16[12,32,128]{2,1,0:T(8,128)(2,1)S(1)}, bf16[12,32,128]{2,1,0:T(8,128)(2,1)S(1)}) custom-call(s32[7]{0:T(128)S(4)} %get-tuple-element.52.info_ref, s32[128]{0:T(128)S(4)} %get-tuple-element.53.rows_ref, s32[128]{0:T(128)S(4)} %get-tuple-element.54.cols_ref, ...), custom_call_target="tpu_custom_call" | custom-call | flops 268435456 | bytes 1048576 | tf_op jit(solution)/shard_map/first_step/pallas_call | solution.py:327
  15.1 0.1 collective-permute-start.4
  15.2 4.0 %collective-permute-start.5 = (bf16[12,32,128]{2,1,0:T(8,128)(2,1)S(1)}, bf16[12,32,128]{2,1,0:T(8,128)(2,1)S(1)}, u32[]{:S(2)}, u32[]{:S(2)}) collective-permute-start(bf16[12,32,128]{2,1,0:T(8,128)(2,1)S(1)} %get-tuple-element.68), channel_id=1, source_target_pairs={{0,1},{1,0},{2,3},{3,2},{4,8},{5,9},{6,10},{7,11},{8,4},{9,5},{10,... | collective-permute-start | bytes 294920 | tf_op jit(solution)/shard_map/ppermute | solution.py:307
  19.2 2.3 %collective-permute-done.5.next_in = bf16[12,32,128]{2,1,0:T(8,128)(2,1)S(1)} collective-permute-done((bf16[12,32,128]{2,1,0:T(8,128)(2,1)S(1)}, bf16[12,32,128]{2,1,0:T(8,128)(2,1)S(1)}, u32[]{:S(2)}, u32[]{:S(2)}) %collective-permute-start.5) | collective-permute-done | bytes 98336 | tf_op jit(solution)/shard_map/ppermute | solution.py:307
  21.6 2.0 %collective-permute-start.6 = (bf16[20,32,128]{2,1,0:T(8,128)(2,1)S(1)}, bf16[20,32,128]{2,1,0:T(8,128)(2,1)S(1)}, u32[]{:S(2)}, u32[]{:S(2)}) collective-permute-start(bf16[20,32,128]{2,1,0:T(8,128)(2,1)S(1)} %get-tuple-element.69), channel_id=1, source_target_pairs={{0,4},{1,2},{2,1},{3,7},{4,0},{5,6},{6,5},{7,3},{8,12},{9,10},{10,... | collective-permute-start | bytes 491528 | tf_op jit(solution)/shard_map/ppermute | solution.py:307
  23.5 3.4 %collective-permute-done.6.far_in = bf16[20,32,128]{2,1,0:T(8,128)(2,1)S(1)} collective-permute-done((bf16[20,32,128]{2,1,0:T(8,128)(2,1)S(1)}, bf16[20,32,128]{2,1,0:T(8,128)(2,1)S(1)}, u32[]{:S(2)}, u32[]{:S(2)}) %collective-permute-start.6) | collective-permute-done | bytes 163872 | tf_op jit(solution)/shard_map/ppermute | solution.py:307
  27.0 1.9 %collective-permute-done.7.near_in = bf16[20,32,128]{2,1,0:T(8,128)(2,1)S(1)} collective-permute-done((bf16[20,32,128]{2,1,0:T(8,128)(2,1)S(1)}, bf16[20,32,128]{2,1,0:T(8,128)(2,1)S(1)}, u32[]{:S(2)}, u32[]{:S(2)}) %collective-permute-start.7) | collective-permute-done | bytes 163872 | tf_op jit(solution)/shard_map/ppermute | solution.py:307
  28.9 1.5 %one_step.4 = (f32[60,32,128]{2,1,0:T(8,128)S(1)}, f32[61,32,128]{2,1,0:T(8,128)S(1)}, bf16[12,32,128]{2,1,0:T(8,128)(2,1)S(1)}, bf16[12,32,128]{2,1,0:T(8,128)(2,1)S(1)}) custom-call(s32[7]{0:T(128)S(4)} %get-tuple-element.52.info_ref, s32[128]{0:T(128)S(4)} %get-tuple-element.53.rows_ref, s32[128]{0:T(128)S(4)} %get-tuple-element.54.cols_ref, ...), custom_call_target="tpu_custom_call" | custom-call | flops 268435456 | bytes 1048576 | tf_op jit(solution)/shard_map/one_step/pallas_call | solution.py:327
  30.5 3.4 %collective-permute-start.9 = (bf16[12,32,128]{2,1,0:T(8,128)(2,1)S(1)}, bf16[12,32,128]{2,1,0:T(8,128)(2,1)S(1)}, u32[]{:S(2)}, u32[]{:S(2)}) collective-permute-start(bf16[12,32,128]{2,1,0:T(8,128)(2,1)S(1)} %get-tuple-element.74), channel_id=1, source_target_pairs={{0,1},{1,0},{2,3},{3,2},{4,8},{5,9},{6,10},{7,11},{8,4},{9,5},{10,... | collective-permute-start | bytes 294920 | tf_op jit(solution)/shard_map/ppermute | solution.py:307
  33.8 2.9 %collective-permute-done.9.next_in = bf16[12,32,128]{2,1,0:T(8,128)(2,1)S(1)} collective-permute-done((bf16[12,32,128]{2,1,0:T(8,128)(2,1)S(1)}, bf16[12,32,128]{2,1,0:T(8,128)(2,1)S(1)}, u32[]{:S(2)}, u32[]{:S(2)}) %collective-permute-start.9) | collective-permute-done | bytes 98336 | tf_op jit(solution)/shard_map/ppermute | solution.py:307
  36.8 0.9 %collective-permute-start.10 = (bf16[20,32,128]{2,1,0:T(8,128)(2,1)S(1)}, bf16[20,32,128]{2,1,0:T(8,128)(2,1)S(1)}, u32[]{:S(2)}, u32[]{:S(2)}) collective-permute-start(bf16[20,32,128]{2,1,0:T(8,128)(2,1)S(1)} %get-tuple-element.75), channel_id=1, source_target_pairs={{0,4},{1,2},{2,1},{3,7},{4,0},{5,6},{6,5},{7,3},{8,12},{9,10},{10,... | collective-permute-start | bytes 491528 | tf_op jit(solution)/shard_map/ppermute | solution.py:307
  37.7 0.5 collective-permute-start.11
  38.1 4.0 %collective-permute-done.10.far_in = bf16[20,32,128]{2,1,0:T(8,128)(2,1)S(1)} collective-permute-done((bf16[20,32,128]{2,1,0:T(8,128)(2,1)S(1)}, bf16[20,32,128]{2,1,0:T(8,128)(2,1)S(1)}, u32[]{:S(2)}, u32[]{:S(2)}) %collective-permute-start.10) | collective-permute-done | bytes 163872 | tf_op jit(solution)/shard_map/ppermute | solution.py:307
  42.2 0.8 collective-permute-done.11.near_in
  43.0 1.7 %one_step.5 = (f32[60,32,128]{2,1,0:T(8,128)S(1)}, f32[61,32,128]{2,1,0:T(8,128)S(1)}, bf16[12,32,128]{2,1,0:T(8,128)(2,1)S(1)}, bf16[12,32,128]{2,1,0:T(8,128)(2,1)S(1)}) custom-call(s32[7]{0:T(128)S(4)} %get-tuple-element.52.info_ref, s32[128]{0:T(128)S(4)} %get-tuple-element.53.rows_ref, s32[128]{0:T(128)S(4)} %get-tuple-element.54.cols_ref, ...), custom_call_target="tpu_custom_call" | custom-call | flops 268435456 | bytes 1048576 | tf_op jit(solution)/shard_map/one_step/pallas_call | solution.py:327
  44.7 0.1 collective-permute-start.12
  44.8 4.0 %collective-permute-start.13 = (bf16[12,32,128]{2,1,0:T(8,128)(2,1)S(1)}, bf16[12,32,128]{2,1,0:T(8,128)(2,1)S(1)}, u32[]{:S(2)}, u32[]{:S(2)}) collective-permute-start(bf16[12,32,128]{2,1,0:T(8,128)(2,1)S(1)} %get-tuple-element.80), channel_id=1, source_target_pairs={{0,1},{1,0},{2,3},{3,2},{4,8},{5,9},{6,10},{7,11},{8,4},{9,5},{10,... | collective-permute-start | bytes 294920 | tf_op jit(solution)/shard_map/ppermute | solution.py:307
  48.8 2.3 %collective-permute-done.13.next_in = bf16[12,32,128]{2,1,0:T(8,128)(2,1)S(1)} collective-permute-done((bf16[12,32,128]{2,1,0:T(8,128)(2,1)S(1)}, bf16[12,32,128]{2,1,0:T(8,128)(2,1)S(1)}, u32[]{:S(2)}, u32[]{:S(2)}) %collective-permute-start.13) | collective-permute-done | bytes 98336 | tf_op jit(solution)/shard_map/ppermute | solution.py:307
  51.1 1.4 %collective-permute-start.14 = (bf16[20,32,128]{2,1,0:T(8,128)(2,1)S(1)}, bf16[20,32,128]{2,1,0:T(8,128)(2,1)S(1)}, u32[]{:S(2)}, u32[]{:S(2)}) collective-permute-start(bf16[20,32,128]{2,1,0:T(8,128)(2,1)S(1)} %get-tuple-element.81), channel_id=1, source_target_pairs={{0,4},{1,2},{2,1},{3,7},{4,0},{5,6},{6,5},{7,3},{8,12},{9,10},{10,... | collective-permute-start | bytes 491528 | tf_op jit(solution)/shard_map/ppermute | solution.py:307
  52.5 0.5 collective-permute-start.15
  53.0 3.5 %collective-permute-done.14.far_in = bf16[20,32,128]{2,1,0:T(8,128)(2,1)S(1)} collective-permute-done((bf16[20,32,128]{2,1,0:T(8,128)(2,1)S(1)}, bf16[20,32,128]{2,1,0:T(8,128)(2,1)S(1)}, u32[]{:S(2)}, u32[]{:S(2)}) %collective-permute-start.14) | collective-permute-done | bytes 163872 | tf_op jit(solution)/shard_map/ppermute | solution.py:307
  56.5 1.3 %collective-permute-done.15.near_in = bf16[20,32,128]{2,1,0:T(8,128)(2,1)S(1)} collective-permute-done((bf16[20,32,128]{2,1,0:T(8,128)(2,1)S(1)}, bf16[20,32,128]{2,1,0:T(8,128)(2,1)S(1)}, u32[]{:S(2)}, u32[]{:S(2)}) %collective-permute-start.15) | collective-permute-done | bytes 163872 | tf_op jit(solution)/shard_map/ppermute | solution.py:307
  57.8 1.5 %one_step.6 = (f32[60,32,128]{2,1,0:T(8,128)S(1)}, f32[61,32,128]{2,1,0:T(8,128)S(1)}, bf16[12,32,128]{2,1,0:T(8,128)(2,1)S(1)}, bf16[12,32,128]{2,1,0:T(8,128)(2,1)S(1)}) custom-call(s32[7]{0:T(128)S(4)} %get-tuple-element.52.info_ref, s32[128]{0:T(128)S(4)} %get-tuple-element.53.rows_ref, s32[128]{0:T(128)S(4)} %get-tuple-element.54.cols_ref, ...), custom_call_target="tpu_custom_call" | custom-call | flops 268435456 | bytes 1048576 | tf_op jit(solution)/shard_map/one_step/pallas_call | solution.py:327
  59.5 3.8 %collective-permute-start.17 = (bf16[12,32,128]{2,1,0:T(8,128)(2,1)S(1)}, bf16[12,32,128]{2,1,0:T(8,128)(2,1)S(1)}, u32[]{:S(2)}, u32[]{:S(2)}) collective-permute-start(bf16[12,32,128]{2,1,0:T(8,128)(2,1)S(1)} %get-tuple-element.86), channel_id=1, source_target_pairs={{0,1},{1,0},{2,3},{3,2},{4,8},{5,9},{6,10},{7,11},{8,4},{9,5},{10,... | collective-permute-start | bytes 294920 | tf_op jit(solution)/shard_map/ppermute | solution.py:307
  63.2 2.4 %collective-permute-done.17.next_in = bf16[12,32,128]{2,1,0:T(8,128)(2,1)S(1)} collective-permute-done((bf16[12,32,128]{2,1,0:T(8,128)(2,1)S(1)}, bf16[12,32,128]{2,1,0:T(8,128)(2,1)S(1)}, u32[]{:S(2)}, u32[]{:S(2)}) %collective-permute-start.17) | collective-permute-done | bytes 98336 | tf_op jit(solution)/shard_map/ppermute | solution.py:307
  65.7 1.4 %collective-permute-start.18 = (bf16[20,32,128]{2,1,0:T(8,128)(2,1)S(1)}, bf16[20,32,128]{2,1,0:T(8,128)(2,1)S(1)}, u32[]{:S(2)}, u32[]{:S(2)}) collective-permute-start(bf16[20,32,128]{2,1,0:T(8,128)(2,1)S(1)} %get-tuple-element.87), channel_id=1, source_target_pairs={{0,4},{1,2},{2,1},{3,7},{4,0},{5,6},{6,5},{7,3},{8,12},{9,10},{10,... | collective-permute-start | bytes 491528 | tf_op jit(solution)/shard_map/ppermute | solution.py:307
  67.2 0.5 collective-permute-start.19
  67.7 3.4 %collective-permute-done.18.far_in = bf16[20,32,128]{2,1,0:T(8,128)(2,1)S(1)} collective-permute-done((bf16[20,32,128]{2,1,0:T(8,128)(2,1)S(1)}, bf16[20,32,128]{2,1,0:T(8,128)(2,1)S(1)}, u32[]{:S(2)}, u32[]{:S(2)}) %collective-permute-start.18) | collective-permute-done | bytes 163872 | tf_op jit(solution)/shard_map/ppermute | solution.py:307
  71.1 1.4 %collective-permute-done.19.near_in = bf16[20,32,128]{2,1,0:T(8,128)(2,1)S(1)} collective-permute-done((bf16[20,32,128]{2,1,0:T(8,128)(2,1)S(1)}, bf16[20,32,128]{2,1,0:T(8,128)(2,1)S(1)}, u32[]{:S(2)}, u32[]{:S(2)}) %collective-permute-start.19) | collective-permute-done | bytes 163872 | tf_op jit(solution)/shard_map/ppermute | solution.py:307
  72.5 1.5 %one_step.7 = (f32[60,32,128]{2,1,0:T(8,128)S(1)}, f32[61,32,128]{2,1,0:T(8,128)S(1)}, bf16[6,32,128]{2,1,0:T(8,128)(2,1)S(1)}, bf16[6,32,128]{2,1,0:T(8,128)(2,1)S(1)}, f32[33,32,128]{2,1,0:T(8,128)S(1)}) custom-call(s32[7]{0:T(128)S(4)} %get-tuple-element.52.info_ref, s32[128]{0:T(128)S(4)} %get-tuple-element.53.rows_ref, ...), custom_call_target="tpu_custom_call" | custom-call | flops 268435456 | bytes 1048576 | tf_op jit(solution)/shard_map/one_step/pallas_call | solution.py:327
  74.1 3.7 %collective-permute-start.21 = (bf16[6,32,128]{2,1,0:T(8,128)(2,1)S(1)}, bf16[6,32,128]{2,1,0:T(8,128)(2,1)S(1)}, u32[]{:S(2)}, u32[]{:S(2)}) collective-permute-start(bf16[6,32,128]{2,1,0:T(8,128)(2,1)S(1)} %get-tuple-element.92), channel_id=1, source_target_pairs={{0,1},{1,0},{2,3},{3,2},{4,8},{5,9},{6,10},{7,11},{8,4},{9,5},{10,... | collective-permute-start | bytes 147464 | tf_op jit(solution)/shard_map/ppermute | solution.py:307
  77.8 2.0 %collective-permute-done.21.next_in = bf16[6,32,128]{2,1,0:T(8,128)(2,1)S(1)} collective-permute-done((bf16[6,32,128]{2,1,0:T(8,128)(2,1)S(1)}, bf16[6,32,128]{2,1,0:T(8,128)(2,1)S(1)}, u32[]{:S(2)}, u32[]{:S(2)}) %collective-permute-start.21) | collective-permute-done | bytes 49184 | tf_op jit(solution)/shard_map/ppermute | solution.py:307
  79.9 1.4 %collective-permute-start.22 = (bf16[8,32,128]{2,1,0:T(8,128)(2,1)S(1)}, bf16[8,32,128]{2,1,0:T(8,128)(2,1)S(1)}, u32[]{:S(2)}, u32[]{:S(2)}) collective-permute-start(bf16[8,32,128]{2,1,0:T(8,128)(2,1)S(1)} %get-tuple-element.93), channel_id=1, source_target_pairs={{0,4},{1,2},{2,1},{3,7},{4,0},{5,6},{6,5},{7,3},{8,12},{9,10},{10,... | collective-permute-start | bytes 196616 | tf_op jit(solution)/shard_map/ppermute | solution.py:307
  81.3 0.6 collective-permute-start.23
  81.9 0.8 slice.35
  82.7 1.5 %collective-permute-done.22.far_in = bf16[8,32,128]{2,1,0:T(8,128)(2,1)S(1)} collective-permute-done((bf16[8,32,128]{2,1,0:T(8,128)(2,1)S(1)}, bf16[8,32,128]{2,1,0:T(8,128)(2,1)S(1)}, u32[]{:S(2)}, u32[]{:S(2)}) %collective-permute-start.22) | collective-permute-done | bytes 65568 | tf_op jit(solution)/shard_map/ppermute | solution.py:307
  84.2 1.4 %collective-permute-done.23.near_in = bf16[8,32,128]{2,1,0:T(8,128)(2,1)S(1)} collective-permute-done((bf16[8,32,128]{2,1,0:T(8,128)(2,1)S(1)}, bf16[8,32,128]{2,1,0:T(8,128)(2,1)S(1)}, u32[]{:S(2)}, u32[]{:S(2)}) %collective-permute-start.23) | collective-permute-done | bytes 65568 | tf_op jit(solution)/shard_map/ppermute | solution.py:307
  85.6 0.9 %final_update.1 = f32[32,32,128]{2,1,0:T(8,128)} custom-call(s32[7]{0:T(128)S(4)} %get-tuple-element.52.info_ref, f32[60,32,128]{2,1,0:T(8,128)S(1)} %get-tuple-element.89.x_in, f32[61,32,128]{2,1,0:T(8,128)S(1)} %get-tuple-element.90.grad_in, bf16[6,32,128]{2,1,0:T(8,128)(2,1)S(1)} %collective-permute-done.20.pair_in, ...), custom_call_target="tpu_custom_call" | custom-call | bytes 1048576 | tf_op jit(solution)/shard_map/final_update/pallas_call | solution.py:327
  (26 shorter events, 0.6 us)
Async XLA Ops:
  1.7 5.5 %collective-permute-start.1 = (bf16[8,32,128]{2,1,0:T(8,128)(2,1)S(1)}, bf16[8,32,128]{2,1,0:T(8,128)(2,1)S(1)}, u32[]{:S(2)}, u32[]{:S(2)}) collective-permute-start(bf16[8,32,128]{2,1,0:T(8,128)(2,1)S(1)} %get-tuple-element.102), channel_id=1, source_target_pairs={{0,4},{1,2},{2,1},{3,7},{4,0},{5,6},{6,5},{7,3},{8,12},{9,10},{10,... | collective-permute-start | bytes 196616 | tf_op jit(solution)/shard_map/ppermute | solution.py:307
  3.2 4.3 %collective-permute-start = (bf16[8,32,128]{2,1,0:T(8,128)(2,1)S(1)}, bf16[8,32,128]{2,1,0:T(8,128)(2,1)S(1)}, u32[]{:S(2)}, u32[]{:S(2)}) collective-permute-start(bf16[8,32,128]{2,1,0:T(8,128)(2,1)S(1)} %get-tuple-element.103), channel_id=1, source_target_pairs={{0,1},{1,0},{2,3},{3,2},{4,5},{5,4},{6,7},{7,6},{8,9},{9,8},{10,11... | collective-permute-start | bytes 196616 | tf_op jit(solution)/shard_map/ppermute | solution.py:307
  7.6 5.1 %collective-permute-start.2 = (bf16[6,32,128]{2,1,0:T(8,128)(2,1)S(1)}, bf16[6,32,128]{2,1,0:T(8,128)(2,1)S(1)}, u32[]{:S(2)}, u32[]{:S(2)}) collective-permute-start(bf16[6,32,128]{2,1,0:T(8,128)(2,1)S(1)} %get-tuple-element.59), channel_id=1, source_target_pairs={{0,4},{1,5},{2,6},{3,7},{4,0},{5,1},{6,2},{7,3},{8,12},{9,13},{10,... | collective-permute-start | bytes 147464 | tf_op jit(solution)/shard_map/ppermute | solution.py:307
  7.6 6.1 %collective-permute-start.3 = (bf16[6,32,128]{2,1,0:T(8,128)(2,1)S(1)}, bf16[6,32,128]{2,1,0:T(8,128)(2,1)S(1)}, u32[]{:S(2)}, u32[]{:S(2)}) collective-permute-start(bf16[6,32,128]{2,1,0:T(8,128)(2,1)S(1)} %get-tuple-element.60), channel_id=1, source_target_pairs={{0,1},{1,0},{2,3},{3,2},{4,8},{5,9},{6,10},{7,11},{8,4},{9,5},{10,... | collective-permute-start | bytes 147464 | tf_op jit(solution)/shard_map/ppermute | solution.py:307
  12.0 1.8 %copy-start = (f32[4,8,32,128]{3,2,1,0:T(8,128)S(1)}, f32[4,8,32,128]{3,2,1,0:T(8,128)}, u32[]{:S(2)}) copy-start(f32[4,8,32,128]{3,2,1,0:T(8,128)} %param.7) | copy-start | bytes 1572868
  12.0 1.8 %copy-start.1 = (f32[4,8,32,128]{3,2,1,0:T(8,128)S(1)}, f32[4,8,32,128]{3,2,1,0:T(8,128)}, u32[]{:S(2)}) copy-start(f32[4,8,32,128]{3,2,1,0:T(8,128)} %param.6) | copy-start | bytes 1572868
  15.1 4.1 %collective-permute-start.4 = (bf16[12,32,128]{2,1,0:T(8,128)(2,1)S(1)}, bf16[12,32,128]{2,1,0:T(8,128)(2,1)S(1)}, u32[]{:S(2)}, u32[]{:S(2)}) collective-permute-start(bf16[12,32,128]{2,1,0:T(8,128)(2,1)S(1)} %get-tuple-element.67), channel_id=1, source_target_pairs={{0,4},{1,5},{2,6},{3,7},{4,0},{5,1},{6,2},{7,3},{8,12},{9,13},{10,... | collective-permute-start | bytes 294920 | tf_op jit(solution)/shard_map/ppermute | solution.py:307
  15.2 6.3 %collective-permute-start.5 = (bf16[12,32,128]{2,1,0:T(8,128)(2,1)S(1)}, bf16[12,32,128]{2,1,0:T(8,128)(2,1)S(1)}, u32[]{:S(2)}, u32[]{:S(2)}) collective-permute-start(bf16[12,32,128]{2,1,0:T(8,128)(2,1)S(1)} %get-tuple-element.68), channel_id=1, source_target_pairs={{0,1},{1,0},{2,3},{3,2},{4,8},{5,9},{6,10},{7,11},{8,4},{9,5},{10,... | collective-permute-start | bytes 294920 | tf_op jit(solution)/shard_map/ppermute | solution.py:307
  21.6 5.4 %collective-permute-start.6 = (bf16[20,32,128]{2,1,0:T(8,128)(2,1)S(1)}, bf16[20,32,128]{2,1,0:T(8,128)(2,1)S(1)}, u32[]{:S(2)}, u32[]{:S(2)}) collective-permute-start(bf16[20,32,128]{2,1,0:T(8,128)(2,1)S(1)} %get-tuple-element.69), channel_id=1, source_target_pairs={{0,4},{1,2},{2,1},{3,7},{4,0},{5,6},{6,5},{7,3},{8,12},{9,10},{10,... | collective-permute-start | bytes 491528 | tf_op jit(solution)/shard_map/ppermute | solution.py:307
  23.5 5.3 %collective-permute-start.7 = (bf16[20,32,128]{2,1,0:T(8,128)(2,1)S(1)}, bf16[20,32,128]{2,1,0:T(8,128)(2,1)S(1)}, u32[]{:S(2)}, u32[]{:S(2)}) collective-permute-start(bf16[20,32,128]{2,1,0:T(8,128)(2,1)S(1)} %get-tuple-element.70), channel_id=1, source_target_pairs={{0,1},{1,0},{2,3},{3,2},{4,5},{5,4},{6,7},{7,6},{8,9},{9,8},{10,11... | collective-permute-start | bytes 491528 | tf_op jit(solution)/shard_map/ppermute | solution.py:307
  30.4 3.5 %collective-permute-start.8 = (bf16[12,32,128]{2,1,0:T(8,128)(2,1)S(1)}, bf16[12,32,128]{2,1,0:T(8,128)(2,1)S(1)}, u32[]{:S(2)}, u32[]{:S(2)}) collective-permute-start(bf16[12,32,128]{2,1,0:T(8,128)(2,1)S(1)} %get-tuple-element.73), channel_id=1, source_target_pairs={{0,4},{1,5},{2,6},{3,7},{4,0},{5,1},{6,2},{7,3},{8,12},{9,13},{10,... | collective-permute-start | bytes 294920 | tf_op jit(solution)/shard_map/ppermute | solution.py:307
  30.5 6.2 %collective-permute-start.9 = (bf16[12,32,128]{2,1,0:T(8,128)(2,1)S(1)}, bf16[12,32,128]{2,1,0:T(8,128)(2,1)S(1)}, u32[]{:S(2)}, u32[]{:S(2)}) collective-permute-start(bf16[12,32,128]{2,1,0:T(8,128)(2,1)S(1)} %get-tuple-element.74), channel_id=1, source_target_pairs={{0,1},{1,0},{2,3},{3,2},{4,8},{5,9},{6,10},{7,11},{8,4},{9,5},{10,... | collective-permute-start | bytes 294920 | tf_op jit(solution)/shard_map/ppermute | solution.py:307
  36.8 5.4 %collective-permute-start.10 = (bf16[20,32,128]{2,1,0:T(8,128)(2,1)S(1)}, bf16[20,32,128]{2,1,0:T(8,128)(2,1)S(1)}, u32[]{:S(2)}, u32[]{:S(2)}) collective-permute-start(bf16[20,32,128]{2,1,0:T(8,128)(2,1)S(1)} %get-tuple-element.75), channel_id=1, source_target_pairs={{0,4},{1,2},{2,1},{3,7},{4,0},{5,6},{6,5},{7,3},{8,12},{9,10},{10,... | collective-permute-start | bytes 491528 | tf_op jit(solution)/shard_map/ppermute | solution.py:307
  37.7 5.3 %collective-permute-start.11 = (bf16[20,32,128]{2,1,0:T(8,128)(2,1)S(1)}, bf16[20,32,128]{2,1,0:T(8,128)(2,1)S(1)}, u32[]{:S(2)}, u32[]{:S(2)}) collective-permute-start(bf16[20,32,128]{2,1,0:T(8,128)(2,1)S(1)} %get-tuple-element.76), channel_id=1, source_target_pairs={{0,1},{1,0},{2,3},{3,2},{4,5},{5,4},{6,7},{7,6},{8,9},{9,8},{10,11... | collective-permute-start | bytes 491528 | tf_op jit(solution)/shard_map/ppermute | solution.py:307
  44.7 4.1 %collective-permute-start.12 = (bf16[12,32,128]{2,1,0:T(8,128)(2,1)S(1)}, bf16[12,32,128]{2,1,0:T(8,128)(2,1)S(1)}, u32[]{:S(2)}, u32[]{:S(2)}) collective-permute-start(bf16[12,32,128]{2,1,0:T(8,128)(2,1)S(1)} %get-tuple-element.79), channel_id=1, source_target_pairs={{0,4},{1,5},{2,6},{3,7},{4,0},{5,1},{6,2},{7,3},{8,12},{9,13},{10,... | collective-permute-start | bytes 294920 | tf_op jit(solution)/shard_map/ppermute | solution.py:307
  44.8 6.3 %collective-permute-start.13 = (bf16[12,32,128]{2,1,0:T(8,128)(2,1)S(1)}, bf16[12,32,128]{2,1,0:T(8,128)(2,1)S(1)}, u32[]{:S(2)}, u32[]{:S(2)}) collective-permute-start(bf16[12,32,128]{2,1,0:T(8,128)(2,1)S(1)} %get-tuple-element.80), channel_id=1, source_target_pairs={{0,1},{1,0},{2,3},{3,2},{4,8},{5,9},{6,10},{7,11},{8,4},{9,5},{10,... | collective-permute-start | bytes 294920 | tf_op jit(solution)/shard_map/ppermute | solution.py:307
  51.1 5.4 %collective-permute-start.14 = (bf16[20,32,128]{2,1,0:T(8,128)(2,1)S(1)}, bf16[20,32,128]{2,1,0:T(8,128)(2,1)S(1)}, u32[]{:S(2)}, u32[]{:S(2)}) collective-permute-start(bf16[20,32,128]{2,1,0:T(8,128)(2,1)S(1)} %get-tuple-element.81), channel_id=1, source_target_pairs={{0,4},{1,2},{2,1},{3,7},{4,0},{5,6},{6,5},{7,3},{8,12},{9,10},{10,... | collective-permute-start | bytes 491528 | tf_op jit(solution)/shard_map/ppermute | solution.py:307
  52.5 5.3 %collective-permute-start.15 = (bf16[20,32,128]{2,1,0:T(8,128)(2,1)S(1)}, bf16[20,32,128]{2,1,0:T(8,128)(2,1)S(1)}, u32[]{:S(2)}, u32[]{:S(2)}) collective-permute-start(bf16[20,32,128]{2,1,0:T(8,128)(2,1)S(1)} %get-tuple-element.82), channel_id=1, source_target_pairs={{0,1},{1,0},{2,3},{3,2},{4,5},{5,4},{6,7},{7,6},{8,9},{9,8},{10,11... | collective-permute-start | bytes 491528 | tf_op jit(solution)/shard_map/ppermute | solution.py:307
  59.4 3.9 %collective-permute-start.16 = (bf16[12,32,128]{2,1,0:T(8,128)(2,1)S(1)}, bf16[12,32,128]{2,1,0:T(8,128)(2,1)S(1)}, u32[]{:S(2)}, u32[]{:S(2)}) collective-permute-start(bf16[12,32,128]{2,1,0:T(8,128)(2,1)S(1)} %get-tuple-element.85), channel_id=1, source_target_pairs={{0,4},{1,5},{2,6},{3,7},{4,0},{5,1},{6,2},{7,3},{8,12},{9,13},{10,... | collective-permute-start | bytes 294920 | tf_op jit(solution)/shard_map/ppermute | solution.py:307
  59.5 6.2 %collective-permute-start.17 = (bf16[12,32,128]{2,1,0:T(8,128)(2,1)S(1)}, bf16[12,32,128]{2,1,0:T(8,128)(2,1)S(1)}, u32[]{:S(2)}, u32[]{:S(2)}) collective-permute-start(bf16[12,32,128]{2,1,0:T(8,128)(2,1)S(1)} %get-tuple-element.86), channel_id=1, source_target_pairs={{0,1},{1,0},{2,3},{3,2},{4,8},{5,9},{6,10},{7,11},{8,4},{9,5},{10,... | collective-permute-start | bytes 294920 | tf_op jit(solution)/shard_map/ppermute | solution.py:307
  65.7 5.4 %collective-permute-start.18 = (bf16[20,32,128]{2,1,0:T(8,128)(2,1)S(1)}, bf16[20,32,128]{2,1,0:T(8,128)(2,1)S(1)}, u32[]{:S(2)}, u32[]{:S(2)}) collective-permute-start(bf16[20,32,128]{2,1,0:T(8,128)(2,1)S(1)} %get-tuple-element.87), channel_id=1, source_target_pairs={{0,4},{1,2},{2,1},{3,7},{4,0},{5,6},{6,5},{7,3},{8,12},{9,10},{10,... | collective-permute-start | bytes 491528 | tf_op jit(solution)/shard_map/ppermute | solution.py:307
  67.2 5.3 %collective-permute-start.19 = (bf16[20,32,128]{2,1,0:T(8,128)(2,1)S(1)}, bf16[20,32,128]{2,1,0:T(8,128)(2,1)S(1)}, u32[]{:S(2)}, u32[]{:S(2)}) collective-permute-start(bf16[20,32,128]{2,1,0:T(8,128)(2,1)S(1)} %get-tuple-element.88), channel_id=1, source_target_pairs={{0,1},{1,0},{2,3},{3,2},{4,5},{5,4},{6,7},{7,6},{8,9},{9,8},{10,11... | collective-permute-start | bytes 491528 | tf_op jit(solution)/shard_map/ppermute | solution.py:307
  74.0 3.8 %collective-permute-start.20 = (bf16[6,32,128]{2,1,0:T(8,128)(2,1)S(1)}, bf16[6,32,128]{2,1,0:T(8,128)(2,1)S(1)}, u32[]{:S(2)}, u32[]{:S(2)}) collective-permute-start(bf16[6,32,128]{2,1,0:T(8,128)(2,1)S(1)} %get-tuple-element.91), channel_id=1, source_target_pairs={{0,4},{1,5},{2,6},{3,7},{4,0},{5,1},{6,2},{7,3},{8,12},{9,13},{10,... | collective-permute-start | bytes 147464 | tf_op jit(solution)/shard_map/ppermute | solution.py:307
  74.1 5.7 %collective-permute-start.21 = (bf16[6,32,128]{2,1,0:T(8,128)(2,1)S(1)}, bf16[6,32,128]{2,1,0:T(8,128)(2,1)S(1)}, u32[]{:S(2)}, u32[]{:S(2)}) collective-permute-start(bf16[6,32,128]{2,1,0:T(8,128)(2,1)S(1)} %get-tuple-element.92), channel_id=1, source_target_pairs={{0,1},{1,0},{2,3},{3,2},{4,8},{5,9},{6,10},{7,11},{8,4},{9,5},{10,... | collective-permute-start | bytes 147464 | tf_op jit(solution)/shard_map/ppermute | solution.py:307
  79.9 4.3 %collective-permute-start.22 = (bf16[8,32,128]{2,1,0:T(8,128)(2,1)S(1)}, bf16[8,32,128]{2,1,0:T(8,128)(2,1)S(1)}, u32[]{:S(2)}, u32[]{:S(2)}) collective-permute-start(bf16[8,32,128]{2,1,0:T(8,128)(2,1)S(1)} %get-tuple-element.93), channel_id=1, source_target_pairs={{0,4},{1,2},{2,1},{3,7},{4,0},{5,6},{6,5},{7,3},{8,12},{9,10},{10,... | collective-permute-start | bytes 196616 | tf_op jit(solution)/shard_map/ppermute | solution.py:307
  81.3 4.3 %collective-permute-start.23 = (bf16[8,32,128]{2,1,0:T(8,128)(2,1)S(1)}, bf16[8,32,128]{2,1,0:T(8,128)(2,1)S(1)}, u32[]{:S(2)}, u32[]{:S(2)}) collective-permute-start(bf16[8,32,128]{2,1,0:T(8,128)(2,1)S(1)} %get-tuple-element.94), channel_id=1, source_target_pairs={{0,1},{1,0},{2,3},{3,2},{4,5},{5,4},{6,7},{7,6},{8,9},{9,8},{10,11... | collective-permute-start | bytes 196616 | tf_op jit(solution)/shard_map/ppermute | solution.py:307
